TPU v7x, 32 devices: a whole 2x2x4 slice. The times are simulated.
32 devices in a mesh: dp: 2 (over x), ctx: 4 (over y, core), exp: 4 (over z).
Axes of the slice: x: 2, y: 2, z: 4, core: 2. Of those that a mesh axis runs over, the one named last changes fastest.
Arguments:
- hidden_in: float32 [8, 1024, 1536], P(('dp', 'exp'), 'ctx'), may hold values from -6 to 6
- lengths: int32 [8, 3], P(('dp', 'exp')), may hold values from 1 to 512, 1024 in all within a row
- order: int32 [8, 1024], P(('dp', 'exp')), may hold values from 0 to 1023, each once within a row
- routes: int32 [8, 1024, 4], P(('dp', 'exp'), 'ctx'), may hold values from 0 to 7, all different within a row; in each aligned block of 256 rows (0 to 255, 256 to 511, ..., all dimensions but the last counted through in order) at most 192 rows name the same one
- cotangent: float32 [8, 1024, 1536], P(('dp', 'exp'), 'ctx'), may hold values from -6 to 6
- attn_gain: bfloat16 [1536], P(('dp', 'ctx', 'exp')), may hold values from 0.5 to 1.5
- qkv_weight: bfloat16 [1536, 2048], P(('dp', 'ctx', 'exp')), may hold values from -0.15625 to 0.15625
- out_weight: bfloat16 [1536, 1536], P(None, ('dp', 'ctx', 'exp')), may hold values from -0.875 to 0.875
- ffn_gain: bfloat16 [1536], P(('dp', 'ctx', 'exp')), may hold values from 0.5 to 1.5
- router_weight: bfloat16 [1536, 8], P(('dp', 'ctx', 'exp')), may hold values from -0.078125 to 0.078125
- gate_up_weight: bfloat16 [8, 1536, 1536], P('exp', ('dp', 'ctx')), may hold values from -0.15625 to 0.15625
- down_weight: bfloat16 [8, 768, 1536], P('exp', ('dp', 'ctx')), may hold values from -0.21875 to 0.21875
Outputs:
- output: float32 [8, 1024, 1536], P(('dp', 'exp'), 'ctx')
- grad_input: float32 [8, 1024, 1536], P(('dp', 'exp'), 'ctx')
- grad_attn_gain: float32 [1536], P(('dp', 'ctx', 'exp'))
- grad_qkv: float32 [1536, 2048], P(('dp', 'ctx', 'exp'))
- grad_out_proj: float32 [1536, 1536], P(None, ('dp', 'ctx', 'exp'))
- grad_ffn_gain: float32 [1536], P(('dp', 'ctx', 'exp'))
- grad_router: float32 [1536, 8], P(('dp', 'ctx', 'exp'))
- grad_gate_up: float32 [8, 1536, 1536], P('exp', ('dp', 'ctx'))
- grad_down: float32 [8, 768, 1536], P('exp', ('dp', 'ctx'))
Inputs may be any that keep to these rules, and one draw needn't show every extreme that they name: Each row holds the lengths of 3 documents that fill the group's 1024 positions; the longest is exactly 512. `order`: each row is a permutation of the group's packed positions. `routes`: each token names 4 different experts; among the 256 tokens of one device (aligned blocks of rows in the order of the first two dimensions) no expert is named more than 192 times, a bound that some block reaches.
All inputs are finite; a program needn't handle non-finite values.
Results may differ from a plain program's by a relative error of at most 0.029.
Values may be sent and summed in bfloat16 or wider, within the bound.
No kernel may reach another device: no remote copies, remote signals or barrier semaphores. Data moves between devices by JAX's collectives and lax.ppermute only.
A program may use at most 192 MiB of HBM per device.

v0:
```python
import math

import jax
import jax.numpy as jnp
from jax import lax
from jax.sharding import PartitionSpec as P

QUERY_HEADS = 12
KEY_VALUE_HEADS = 2
HEAD_SIZE = 128
TOP = 4


EPS = 1e-06
BASE = 1000000.0


def norm_rows(v, gain):
    return v * lax.rsqrt(jnp.mean(v * v, axis=-1, keepdims=True) + EPS) * gain


def apply_rotation(t, slot_position, sign):
    half = t.shape[-1] // 2
    freq = jnp.exp(jnp.arange(half, dtype=jnp.float32) * (-2.0 * math.log(BASE) / t.shape[-1]))
    angle = slot_position.astype(jnp.float32)[:, None] * freq[None, :]
    cosine = jnp.cos(angle)[:, None, :]
    sine = sign * jnp.sin(angle)[:, None, :]
    first = t[..., :half]
    second = t[..., half:]
    return jnp.concatenate(
        [first * cosine - second * sine, second * cosine + first * sine], axis=-1
    )


def place_docs(packed, lengths):
    ends = jnp.cumsum(lengths)
    before = packed[:, None] >= ends[None, :]
    docs = jnp.sum(before.astype(jnp.int32), axis=1)
    starts = jnp.max(jnp.where(before, ends[None, :], 0), axis=1)
    return (docs, packed - starts)


def act_fn(both):
    half = both.shape[-1] // 2
    return jax.nn.gelu(both[..., :half]) * both[..., half:]


def router_fn(logits, picked):
    probs = jax.nn.softmax(logits, axis=-1)
    chosen = jnp.sum(picked * probs[:, None, :], axis=-1)
    return chosen / jnp.sum(chosen, axis=-1, keepdims=True)


def on_device(
    hidden_in,
    lengths,
    order,
    routes,
    cotangent,
    attn_gain,
    qkv_weight,
    out_weight,
    ffn_gain,
    router_weight,
    gate_up_weight,
    down_weight,
):
    hidden = hidden_in[0]
    token_rows, width = hidden.shape
    packed_all = order[0]
    docs_all, place_all = place_docs(packed_all, lengths[0])
    own_start = lax.axis_index("ctx") * token_rows
    packed = lax.dynamic_slice_in_dim(packed_all, own_start, token_rows, 0)
    docs = lax.dynamic_slice_in_dim(docs_all, own_start, token_rows, 0)
    slot_position = lax.dynamic_slice_in_dim(place_all, own_start, token_rows, 0)
    gain_one_all, qkv_all, out_all, gain_two_all, router_all = (
        lax.all_gather(attn_gain, ("dp", "ctx", "exp"), axis=0, tiled=True),
        lax.all_gather(qkv_weight, ("dp", "ctx", "exp"), axis=0, tiled=True),
        lax.all_gather(out_weight, ("dp", "ctx", "exp"), axis=1, tiled=True),
        lax.all_gather(ffn_gain, ("dp", "ctx", "exp"), axis=0, tiled=True),
        lax.all_gather(router_weight, ("dp", "ctx", "exp"), axis=0, tiled=True),
    )
    gate_up_all, down_all = (
        lax.all_gather(gate_up_weight, ("dp", "ctx"), axis=1, tiled=True),
        lax.all_gather(down_weight, ("dp", "ctx"), axis=1, tiled=True),
    )
    gain_one = gain_one_all.astype(jnp.float32)
    gain_two = gain_two_all.astype(jnp.float32)
    query_width = out_all.shape[0]
    key_value_width = KEY_VALUE_HEADS * HEAD_SIZE
    query_groups = QUERY_HEADS // KEY_VALUE_HEADS
    scale = HEAD_SIZE ** (-0.5)
    normed_f = norm_rows(hidden, gain_one)
    normed = normed_f.astype(jnp.bfloat16)
    projected_output = jnp.dot(normed, qkv_all, preferred_element_type=jnp.float32)
    query_rows = (
        apply_rotation(
            projected_output[:, :query_width].reshape(token_rows, QUERY_HEADS, HEAD_SIZE),
            slot_position,
            1.0,
        )
        .astype(jnp.bfloat16)
        .reshape(token_rows, KEY_VALUE_HEADS, query_groups, HEAD_SIZE)
    )
    key_rows = (
        apply_rotation(
            projected_output[:, query_width : query_width + key_value_width].reshape(
                token_rows, KEY_VALUE_HEADS, HEAD_SIZE
            ),
            slot_position,
            1.0,
        )
        .astype(jnp.bfloat16)
        .reshape(token_rows, key_value_width)
    )
    value_rows = projected_output[:, query_width + key_value_width :].astype(jnp.bfloat16)

    def masked_scores(key_portion):
        token_count = key_portion.shape[0]
        allowed = (docs[:, None] == docs_all[None, :]) & (packed_all[None, :] <= packed[:, None])
        scores = (
            jnp.einsum(
                "qhgd,khd->hgqk",
                query_rows,
                key_portion.reshape(token_count, KEY_VALUE_HEADS, HEAD_SIZE),
                preferred_element_type=jnp.float32,
            )
            * scale
        )
        return jnp.where(allowed, scores, -1e30)

    upper_bound = jnp.full((KEY_VALUE_HEADS, query_groups, token_rows), -1e30, jnp.float32)
    key_portion = lax.all_gather(key_rows, "ctx", axis=0, tiled=True)
    value_portion = lax.all_gather(value_rows, "ctx", axis=0, tiled=True)
    scores = masked_scores(key_portion)
    newtop = jnp.maximum(upper_bound, jnp.max(scores, axis=-1))
    weights = jnp.exp(scores - newtop[..., None])
    total = jnp.sum(weights, axis=-1)
    accum = jnp.einsum(
        "hgqk,khd->hgqd",
        weights.astype(jnp.bfloat16),
        value_portion.reshape(-1, KEY_VALUE_HEADS, HEAD_SIZE),
        preferred_element_type=jnp.float32,
    )
    carry = (newtop, total, accum)
    upper_bound, total, accum = carry
    lse = upper_bound + jnp.log(total)
    attended = accum / total[..., None]
    mixed = (
        jnp.transpose(attended, (2, 0, 1, 3)).reshape(token_rows, query_width).astype(jnp.bfloat16)
    )
    middle = hidden + jnp.dot(mixed, out_all, preferred_element_type=jnp.float32)
    inner = norm_rows(middle, gain_two).astype(jnp.bfloat16)
    logits = jnp.dot(inner, router_all, preferred_element_type=jnp.float32)
    n_experts = router_all.shape[1]
    cap = min(token_rows, 3 * token_rows * TOP // (2 * n_experts))
    chosen_ids = routes[0].reshape(token_rows * TOP)
    onehot = (chosen_ids[:, None] == jnp.arange(n_experts, dtype=jnp.int32)[None, :]).astype(
        jnp.int32
    )
    rank = jnp.sum(onehot * (jnp.cumsum(onehot, axis=0) - 1), axis=1)
    slot_index = chosen_ids * cap + rank
    pair_ids = jnp.arange(token_rows * TOP, dtype=jnp.int32)
    pair_of_slot = jnp.zeros((n_experts * cap,), jnp.int32).at[slot_index].set(pair_ids)
    filled = jnp.zeros((n_experts * cap,), jnp.bool_).at[slot_index].set(True)
    picked = onehot.reshape(token_rows, TOP, n_experts).astype(jnp.float32)

    def build_send(source, index):
        taken = jnp.take(source, index, axis=0)
        return jnp.where(filled[:, None], taken, jnp.zeros_like(taken)).reshape(
            n_experts, cap, width
        )

    def gate_fn(values_in):
        return router_fn(values_in, picked)

    gates, router_pull = jax.vjp(gate_fn, logits)
    received = lax.all_to_all(
        build_send(inner, pair_of_slot // TOP), "exp", split_axis=0, concat_axis=1, tiled=True
    )
    both = jnp.einsum("erd,edf->erf", received, gate_up_all, preferred_element_type=jnp.float32)
    act = act_fn(both).astype(jnp.bfloat16)
    result = jnp.einsum("erf,efd->erd", act, down_all, preferred_element_type=jnp.float32).astype(
        jnp.bfloat16
    )
    returned = lax.all_to_all(result, "exp", split_axis=1, concat_axis=0, tiled=True).reshape(
        n_experts * cap, width
    )
    pair_rows = (
        jnp.take(returned, slot_index, axis=0).reshape(token_rows, TOP, width).astype(jnp.float32)
    )
    output = middle + jnp.einsum("tk,tkd->td", gates, pair_rows)
    grad_out = cotangent[0]
    grad_gates = jnp.einsum("tkd,td->tk", pair_rows, grad_out)
    pair_grads = (
        (gates[:, :, None] * grad_out[:, None, :])
        .astype(jnp.bfloat16)
        .reshape(token_rows * TOP, width)
    )
    grad_result = lax.all_to_all(
        build_send(pair_grads, pair_of_slot), "exp", split_axis=0, concat_axis=1, tiled=True
    )
    rows_back, both_back, act_back = (received, both, act)
    grad_act = jnp.einsum(
        "erd,efd->erf", grad_result, down_all, preferred_element_type=jnp.float32
    ).astype(jnp.bfloat16)
    grad_down = jnp.einsum(
        "erf,erd->efd", act_back, grad_result, preferred_element_type=jnp.float32
    )
    _, act_pull = jax.vjp(act_fn, both_back)
    grad_both = act_pull(grad_act.astype(jnp.float32))[0].astype(jnp.bfloat16)
    grad_gate_up = jnp.einsum(
        "erd,erf->edf", rows_back, grad_both, preferred_element_type=jnp.float32
    )
    grad_entry = jnp.einsum(
        "erf,edf->erd", grad_both, gate_up_all, preferred_element_type=jnp.float32
    ).astype(jnp.bfloat16)
    grad_back = lax.all_to_all(grad_entry, "exp", split_axis=1, concat_axis=0, tiled=True).reshape(
        n_experts * cap, width
    )
    grad_inner = jnp.sum(
        jnp.take(grad_back, slot_index, axis=0).reshape(token_rows, TOP, width).astype(jnp.float32),
        axis=1,
    )
    grad_logits = router_pull(grad_gates)[0].astype(jnp.bfloat16)
    grad_router = jnp.dot(inner.T, grad_logits, preferred_element_type=jnp.float32)
    grad_inner = grad_inner + jnp.dot(grad_logits, router_all.T, preferred_element_type=jnp.float32)
    _, second_pull = jax.vjp(norm_rows, middle, gain_two)
    grad_middle_norm, grad_ffn_gain = second_pull(grad_inner)
    grad_middle = grad_out + grad_middle_norm
    grad_branch = grad_middle.astype(jnp.bfloat16)
    grad_out_proj = jnp.dot(mixed.T, grad_branch, preferred_element_type=jnp.float32)
    blended_gradient = jnp.dot(grad_branch, out_all.T, preferred_element_type=jnp.float32).astype(
        jnp.bfloat16
    )
    head_gradient = jnp.transpose(
        blended_gradient.reshape(token_rows, KEY_VALUE_HEADS, query_groups, HEAD_SIZE), (1, 2, 0, 3)
    )
    offset = jnp.sum(head_gradient.astype(jnp.float32) * attended, axis=-1)
    key_portion = lax.all_gather(key_rows, "ctx", axis=0, tiled=True)
    value_portion = lax.all_gather(value_rows, "ctx", axis=0, tiled=True)
    token_count = key_portion.shape[0]
    scores = masked_scores(key_portion)
    probs = jnp.exp(scores - lse[..., None])
    grad_probs = jnp.einsum(
        "hgqd,khd->hgqk",
        head_gradient,
        value_portion.reshape(token_count, KEY_VALUE_HEADS, HEAD_SIZE),
        preferred_element_type=jnp.float32,
    )
    grad_scores = (probs * (grad_probs - offset[..., None])).astype(jnp.bfloat16)
    grad_query_acc = (
        jnp.einsum(
            "hgqk,khd->hgqd",
            grad_scores,
            key_portion.reshape(token_count, KEY_VALUE_HEADS, HEAD_SIZE),
            preferred_element_type=jnp.float32,
        )
        * scale
    )
    grad_key = (
        jnp.einsum("hgqk,qhgd->khd", grad_scores, query_rows, preferred_element_type=jnp.float32)
        * scale
    )
    grad_value = jnp.einsum(
        "hgqk,hgqd->khd",
        probs.astype(jnp.bfloat16),
        head_gradient,
        preferred_element_type=jnp.float32,
    )
    update = jnp.concatenate(
        [
            grad_key.reshape(token_count, key_value_width),
            grad_value.reshape(token_count, key_value_width),
        ],
        axis=1,
    )
    grad_kv = update
    grad_query_acc, grad_kv = (grad_query_acc, grad_kv)
    local_key_value_gradient = lax.psum_scatter(
        grad_kv.astype(jnp.bfloat16), "ctx", scatter_dimension=0, tiled=True
    ).astype(jnp.float32)
    grad_query = apply_rotation(
        jnp.transpose(grad_query_acc, (2, 0, 1, 3)).reshape(token_rows, QUERY_HEADS, HEAD_SIZE),
        slot_position,
        -1.0,
    )
    local_key_gradient = apply_rotation(
        local_key_value_gradient[:, :key_value_width].reshape(
            token_rows, KEY_VALUE_HEADS, HEAD_SIZE
        ),
        slot_position,
        -1.0,
    )
    grad_projected = jnp.concatenate(
        [
            grad_query.reshape(token_rows, query_width),
            local_key_gradient.reshape(token_rows, key_value_width),
            local_key_value_gradient[:, key_value_width:],
        ],
        axis=1,
    ).astype(jnp.bfloat16)
    grad_qkv = jnp.dot(normed.T, grad_projected, preferred_element_type=jnp.float32)
    grad_normed = jnp.dot(grad_projected, qkv_all.T, preferred_element_type=jnp.float32)
    _, first_pull = jax.vjp(norm_rows, hidden, gain_one)
    grad_hidden_norm, grad_attn_gain = first_pull(grad_normed)
    grad_input = grad_middle + grad_hidden_norm
    summed = (
        lax.psum_scatter(grad_attn_gain, ("dp", "ctx", "exp"), scatter_dimension=0, tiled=True),
        lax.psum_scatter(grad_qkv, ("dp", "ctx", "exp"), scatter_dimension=0, tiled=True),
        lax.psum_scatter(grad_out_proj, ("dp", "ctx", "exp"), scatter_dimension=1, tiled=True),
        lax.psum_scatter(grad_ffn_gain, ("dp", "ctx", "exp"), scatter_dimension=0, tiled=True),
        lax.psum_scatter(grad_router, ("dp", "ctx", "exp"), scatter_dimension=0, tiled=True),
    )
    expert_summed = (
        lax.psum_scatter(
            grad_gate_up.astype(jnp.bfloat16), ("dp", "ctx"), scatter_dimension=1, tiled=True
        ).astype(jnp.float32),
        lax.psum_scatter(
            grad_down.astype(jnp.bfloat16), ("dp", "ctx"), scatter_dimension=1, tiled=True
        ).astype(jnp.float32),
    )
    return (
        output[None],
        grad_input[None],
        summed[0],
        summed[1],
        summed[2],
        summed[3],
        summed[4],
        expert_summed[0],
        expert_summed[1],
    )


def solution(mesh):
    return jax.shard_map(
        on_device,
        mesh=mesh,
        in_specs=(
            P(("dp", "exp"), "ctx", None),
            P(("dp", "exp"), None),
            P(("dp", "exp"), None),
            P(("dp", "exp"), "ctx", None),
            P(("dp", "exp"), "ctx", None),
            P(("dp", "ctx", "exp")),
            P(("dp", "ctx", "exp"), None),
            P(None, ("dp", "ctx", "exp")),
            P(("dp", "ctx", "exp")),
            P(("dp", "ctx", "exp"), None),
            P("exp", ("dp", "ctx"), None),
            P("exp", ("dp", "ctx"), None),
        ),
        out_specs=(
            P(("dp", "exp"), "ctx", None),
            P(("dp", "exp"), "ctx", None),
            P(("dp", "ctx", "exp")),
            P(("dp", "ctx", "exp"), None),
            P(None, ("dp", "ctx", "exp")),
            P(("dp", "ctx", "exp")),
            P(("dp", "ctx", "exp"), None),
            P("exp", ("dp", "ctx"), None),
            P("exp", ("dp", "ctx"), None),
        ),
        check_vma=False,
    )
```

profile of v0, /device:TPU:0, one launch (start us, length us, event | category | flops | bytes accessed | tf_op | source)
XLA Modules:
  0.0 1397.4 jit_solution(4306586660680903490)
XLA Ops:
  24.6 42.6 %all-reduce.7 = (bf16[1536]{0:T(1024)(128)(2,1)S(1)}, bf16[1536]{0:T(1024)(128)(2,1)S(1)}) all-reduce(bf16[1536]{0:T(1024)(128)(2,1)S(1)} %dynamic-update-slice, bf16[1536]{0:T(1024)(128)(2,1)S(1)} %dynamic-update-slice.1), channel_id=1, replica_groups=mesh['dp'=2,'ctx'=4,'exp'=4] {'dp','ctx','exp'}, use_global_device_ids=true, to_apply=%add.2 | all-reduce | flops 3072 | bytes 12288
  68.8 66.8 %all-gather = bf16[32,48,8]{1,2,0:T(8,128)(2,1)S(1)} all-gather(bf16[1,48,8]{1,2,0:T(8,128)(2,1)S(1)} %bitcast.228), channel_id=1, replica_groups=mesh['dp'=2,'ctx'=4,'exp'=4] {'dp','ctx','exp'}, dimensions={0}, use_global_device_ids=true | all-gather | bytes 25344 | tf_op jit(solution)/shard_map/all_gather | solution.py:81
  140.2 7.9 mul.514
  175.1 7.0 all_gather.32
  184.1 10.7 all_gather.31
  212.3 6.2 gather_fusion
  223.3 12.7 gather_fusion.1
  236.0 7.2 select_select_fusion
  243.2 108.6 %all_to_all.66 = bf16[8,192,1536]{2,1,0:T(8,128)(2,1)} all-to-all(bf16[8,192,1536]{2,1,0:T(8,128)(2,1)S(1)} %get-tuple-element.43), channel_id=1, replica_groups=mesh['dp'=2,'ctx'=4,'exp'=4] {'exp'}, dimensions={0} | all-to-all | bytes 9437184 | tf_op jit(solution)/shard_map/all_to_all | solution.py:178
  362.1 98.8 %all-to-all-done.2 = bf16[8,192,1536]{2,1,0:T(8,128)(2,1)} async-done(((bf16[8,192,1536]{2,1,0:T(8,128)(2,1)}), bf16[8,192,1536]{2,1,0:T(8,128)(2,1)}, u32[]{:S(2)}, u32[]{:S(2)}) %all-to-all-start.2) | async-done | bytes 4718624 | tf_op jit(solution)/shard_map/all_to_all | solution.py:200
  465.7 14.4 %fusion.75 = f32[2,768,1536]{2,1,0:T(8,128)} fusion(bf16[2,768,1536]{2,1,0:T(8,128)(2,1)} %bitcast.198, bf16[2,1536,1536]{2,1,0:T(8,128)(2,1)} %all-gather.10.cloned.1.call-done), kind=kOutput, calls=%fused_computation.178 | convolution fusion | flops 7247757312 | bytes 23592960 | tf_op jit(solution)/shard_map/erd,edf->erf/dot_general | solution.py:181
  480.1 14.7 %convert_multiply_fusion.1 = (f32[2,768,768]{2,1,0:T(8,128)}, f32[2,768,768]{2,1,0:T(8,128)}, bf16[2,768,768]{2,1,0:T(8,128)(2,1)S(1)}) fusion(f32[2,768,1536]{2,1,0:T(8,128)} %fusion.75, bf16[2,768,1536]{2,1,0:T(8,128)(2,1)} %bitcast.200, bf16[2,768,1536]{2,1,0:T(8,128)(2,1)} %all-gather.12.cloned.1.call-done), kind=kOutput, calls=%fused_computation.24 | convolution fusion | flops 3654549504 | bytes 30670848 | tf_op jit(solution)/shard_map/erd,efd->erf/dot_general | solution.py:204
  501.7 9.4 copy.126
  516.3 14.3 %convolution_convert_fusion.2 = bf16[2,768,1536]{2,1,0:T(8,128)(2,1)} fusion(bf16[2,1536,1536]{2,1,0:T(8,128)(2,1)} %all-gather.10.cloned.1.call-done, f32[2,768,768]{2,1,0:T(8,128)} %get-tuple-element.25, f32[2,768,768]{2,1,0:T(8,128)} %get-tuple-element.24), kind=kOutput, calls=%fused_computation.35 | convolution fusion | flops 7254835200 | bytes 23592960 | tf_op jit(solution)/shard_map/erf,edf->erd/dot_general | solution.py:215
  530.6 9.3 copy.130
  539.8 80.4 %all-to-all-done.1 = bf16[2,768,1536]{2,0,1:T(2,128)(2,1)} async-done(((bf16[2,768,1536]{2,0,1:T(2,128)(2,1)}), bf16[2,768,1536]{2,0,1:T(2,128)(2,1)}, u32[]{:S(2)}, u32[]{:S(2)}) %all-to-all-start.1) | async-done | bytes 4718624 | tf_op jit(solution)/shard_map/all_to_all | solution.py:186
  631.2 97.9 %all-to-all-done.3 = bf16[2,768,1536]{2,0,1:T(2,128)(2,1)} async-done(((bf16[2,768,1536]{2,0,1:T(2,128)(2,1)}), bf16[2,768,1536]{2,0,1:T(2,128)(2,1)}, u32[]{:S(2)}, u32[]{:S(2)}) %all-to-all-start.3) | async-done | bytes 4718624 | tf_op jit(solution)/shard_map/all_to_all | solution.py:218
  734.3 10.3 gather_fusion.2
  744.6 10.3 gather_fusion.3
  775.6 7.8 reshape.398
  783.3 6.5 reduce_sum.168
  802.5 8.0 fusion.29
  810.5 7.2 multiply_convert_fusion
  824.0 9.1 convolution_convert_fusion.1
  835.6 14.6 %convolution_convert_fusion = bf16[2,1536,1536]{2,1,0:T(8,128)(2,1)} fusion(bf16[2,768,1536]{2,1,0:T(8,128)(2,1)} %bitcast.199, f32[2,768,768]{2,1,0:T(8,128)} %get-tuple-element.25, f32[2,768,768]{2,1,0:T(8,128)} %get-tuple-element.24), kind=kOutput, calls=%fused_computation.13 | convolution fusion | flops 7257194496 | bytes 23592960 | tf_op jit(solution)/shard_map/erd,erf->edf/dot_general | solution.py:212
  870.7 7.7 fusion.35
  878.5 26.7 %reduce-scatter.17.cloned.1.call-done = bf16[2,96,1536]{2,1,0:T(8,128)(2,1)} async-done(((bf16[2,768,1536]{2,1,0:T(8,128)(2,1)}), bf16[2,96,1536]{2,1,0:T(8,128)(2,1)}) %reduce-scatter.17.cloned.1.call-update) | async-done | bytes 589840 | tf_op jit(solution)/shard_map/reduce_scatter | solution.py:319
  907.4 99.0 %reduce-scatter.19.cloned.1.call-done = f32[48,8]{1,0:T(8,128)} async-done(((f32[1536,8]{1,0:T(8,128)}), f32[48,8]{1,0:T(8,128)}) %reduce-scatter.19.cloned.1.call-update) | async-done | bytes 1552
  1013.9 40.4 %all-reduce.6 = (f32[1536]{0:T(1024)S(1)}, f32[1536]{0:T(1024)S(1)}) all-reduce(f32[1536]{0:T(1024)S(1)} %get-tuple-element.12, f32[1536]{0:T(1024)S(1)} %get-tuple-element.10), channel_id=3, replica_groups=mesh['dp'=2,'ctx'=4,'exp'=4] {'dp','ctx','exp'}, use_global_device_ids=true, to_apply=%region_25.27.clone | all-reduce | flops 3072 | bytes 24576
  1058.4 27.8 %reduce-scatter.15.cloned.1.call-done = bf16[2,192,1536]{2,1,0:T(8,128)(2,1)} async-done(((bf16[2,1536,1536]{2,1,0:T(8,128)(2,1)}), bf16[2,192,1536]{2,1,0:T(8,128)(2,1)}) %reduce-scatter.15.cloned.1.call-update) | async-done | bytes 1179664 | tf_op jit(solution)/shard_map/reduce_scatter | solution.py:316
  1089.1 139.2 %reduce-scatter.13.cloned.1.call-done = f32[1536,48]{0,1:T(8,128)} async-done(((f32[1536,1536]{0,1:T(8,128)}), f32[1536,48]{0,1:T(8,128)}) %reduce-scatter.13.cloned.1.call-update) | async-done | bytes 294928 | tf_op jit(solution)/shard_map/reduce_scatter | solution.py:311
  1228.3 161.8 %reduce-scatter.11.cloned.1.call-done = f32[48,2048]{1,0:T(8,128)} async-done(((f32[1536,2048]{1,0:T(8,128)}), f32[48,2048]{1,0:T(8,128)}) %reduce-scatter.11.cloned.1.call-update) | async-done | bytes 393232 | tf_op jit(solution)/shard_map/reduce_scatter | solution.py:310
  (251 shorter events, 197.1 us)
Async XLA Ops:
  7.2 61.6 %copy-start.45 = (bf16[48,8]{0,1:T(8,128)(2,1)S(1)}, bf16[48,8]{0,1:T(8,128)(2,1)}, u32[]{:S(2)}) copy-start(bf16[48,8]{0,1:T(8,128)(2,1)} %param.23) | copy-start | bytes 2308
  7.2 129.2 %copy-start.11 = (f32[1,256,1536]{2,1,0:T(8,128)S(1)}, f32[1,256,1536]{2,1,0:T(8,128)}, u32[]{:S(2)}) copy-start(f32[1,256,1536]{2,1,0:T(8,128)} %param.18) | copy-start | bytes 4718596
  7.2 148.9 %all-gather.6.cloned.1.call-start = ((), (), s32[]{:S(2)}) async-start(), calls=%async_computation.10 | async-start | bytes 6488064 | tf_op jit(solution)/shard_map/all_gather | solution.py:78
  7.9 199.2 %all-gather.8.cloned.1.call-start = ((), (), s32[]{:S(2)}) async-start(), calls=%async_computation.11 | async-start | bytes 4866048 | tf_op jit(solution)/shard_map/all_gather | solution.py:79
  8.7 457.0 %all-gather.10.cloned.1.call-start = ((), (), s32[]{:S(2)}) async-start(), calls=%async_computation.12 | async-start | bytes 10616832 | tf_op jit(solution)/shard_map/all_gather | solution.py:84
  22.0 118.2 %copy-start.23 = (f32[256,64]{0,1:T(8,128)}, f32[256,64]{0,1:T(8,128)S(1)}, u32[]{:S(2)}) copy-start(f32[256,64]{0,1:T(8,128)S(1)} %get-tuple-element.46) | copy-start | bytes 196612
  22.0 118.2 %copy-start.26 = (f32[256,64]{0,1:T(8,128)}, f32[256,64]{0,1:T(8,128)S(1)}, u32[]{:S(2)}) copy-start(f32[256,64]{0,1:T(8,128)S(1)} %get-tuple-element.45) | copy-start | bytes 196612
  22.1 142.7 %copy-start.21 = (f32[256,64]{1,0:T(8,128)}, f32[256,64]{1,0:T(8,128)S(1)}, u32[]{:S(2)}) copy-start(f32[256,64]{1,0:T(8,128)S(1)} %copy.112) | copy-start | bytes 196612
  67.1 89.0 %copy-start.32 = (f32[1536]{0:T(1024)}, f32[1536]{0:T(1024)S(1)}, u32[]{:S(2)}) copy-start(f32[1536]{0:T(1024)S(1)} %convert_element_type.112) | copy-start | bytes 18436
  68.7 87.0 %copy-start.40 = (f32[256]{0:T(256)}, f32[256]{0:T(256)S(1)}, u32[]{:S(2)}) copy-start(f32[256]{0:T(256)S(1)} %fusion.21) | copy-start | bytes 3076
  140.2 15.6 %copy-start.35 = (s32[1,1024]{1,0:T(1,128)S(1)}, s32[1,1024]{1,0:T(1,128)}, u32[]{:S(2)}) copy-start(s32[1,1024]{1,0:T(1,128)} %param.16) | copy-start | bytes 12292
  140.2 16.0 %copy-start.4 = (f32[1,256,1536]{2,1,0:T(8,128)S(1)}, f32[1,256,1536]{2,1,0:T(8,128)}, u32[]{:S(2)}) copy-start(f32[1,256,1536]{2,1,0:T(8,128)} %param.14) | copy-start | bytes 4718596
  156.1 44.2 %copy-start.16 = (pred[256,1024]{0,1:T(8,128)(4,1)}, pred[256,1024]{0,1:T(8,128)(4,1)S(1)}, u32[]{:S(2)}) copy-start(pred[256,1024]{0,1:T(8,128)(4,1)S(1)} %compare_and_fusion) | copy-start | bytes 786436
  173.4 24.3 %copy-start.7 = (bf16[256,12,64]{2,0,1:T(8,128)(2,1)}, bf16[256,12,64]{2,0,1:T(8,128)(2,1)S(1)}, u32[]{:S(2)}) copy-start(bf16[256,12,64]{2,0,1:T(8,128)(2,1)S(1)} %copy.117) | copy-start | bytes 1179652
  175.1 22.6 %copy-start.9 = (bf16[256,12,64]{2,0,1:T(8,128)(2,1)}, bf16[256,12,64]{2,0,1:T(8,128)(2,1)S(1)}, u32[]{:S(2)}) copy-start(bf16[256,12,64]{2,0,1:T(8,128)(2,1)S(1)} %copy.116) | copy-start | bytes 1179652
  211.3 578.5 %copy-start.6 = (f32[256,1536]{1,0:T(8,128)}, f32[256,1536]{1,0:T(8,128)S(1)}, u32[]{:S(2)}) copy-start(f32[256,1536]{1,0:T(8,128)S(1)} %get-tuple-element.54) | copy-start | bytes 4718596
  223.3 12.7 copy-start.43
  223.3 12.7 copy-start.44
  351.8 109.1 %all-to-all-start.2 = ((bf16[8,192,1536]{2,1,0:T(8,128)(2,1)}), bf16[8,192,1536]{2,1,0:T(8,128)(2,1)}, u32[]{:S(2)}, u32[]{:S(2)}) async-start(bf16[8,192,1536]{2,1,0:T(8,128)(2,1)} %get-tuple-element.42), calls=%async_computation.2 | async-start | bytes 9437184 | tf_op jit(solution)/shard_map/all_to_all | solution.py:200
  356.7 123.4 %all-gather.12.cloned.1.call-start = ((), (), s32[]{:S(2)}) async-start(), calls=%async_computation.13 | async-start | bytes 5308416 | tf_op jit(solution)/shard_map/all_gather | solution.py:85
  480.1 16.1 %copy-start.46 = (bf16[2,768,1536]{2,1,0:T(8,128)(2,1)S(1)}, bf16[2,768,1536]{2,1,0:T(8,128)(2,1)}, u32[]{:S(2)}) copy-start(bf16[2,768,1536]{2,1,0:T(8,128)(2,1)} %all-gather.12.cloned.1.call-done) | copy-start | bytes 14155780
  511.1 109.1 %all-to-all-start.1 = ((bf16[2,768,1536]{2,0,1:T(2,128)(2,1)}), bf16[2,768,1536]{2,0,1:T(2,128)(2,1)}, u32[]{:S(2)}, u32[]{:S(2)}) async-start(bf16[2,768,1536]{2,0,1:T(2,128)(2,1)} %copy.126), calls=%async_computation.1 | async-start | bytes 9437184 | tf_op jit(solution)/shard_map/all_to_all | solution.py:186
  620.2 108.9 %all-to-all-start.3 = ((bf16[2,768,1536]{2,0,1:T(2,128)(2,1)}), bf16[2,768,1536]{2,0,1:T(2,128)(2,1)}, u32[]{:S(2)}, u32[]{:S(2)}) async-start(bf16[2,768,1536]{2,0,1:T(2,128)(2,1)} %copy.130), calls=%async_computation.3 | async-start | bytes 9437184 | tf_op jit(solution)/shard_map/all_to_all | solution.py:218
  625.2 238.6 %reduce-scatter.9.cloned.1.call-start = ((), (), s32[]{:S(2)}) async-start(), calls=%async_computation.14 | async-start | bytes 1310720 | tf_op jit(solution)/shard_map/reduce_scatter | solution.py:280
  823.9 81.2 %reduce-scatter.17.cloned.1.call-start = ((), (), s32[]{:S(2)}) async-start(), calls=%async_computation.18 | async-start | bytes 5308416 | tf_op jit(solution)/shard_map/reduce_scatter | solution.py:319
  833.1 173.3 %reduce-scatter.19.cloned.1.call-start = ((), (), s32[]{:S(2)}) async-start(), calls=%async_computation.19 | async-start | bytes 811008
  835.5 250.6 %reduce-scatter.15.cloned.1.call-start = ((), (), s32[]{:S(2)}) async-start(), calls=%async_computation.17 | async-start | bytes 10616832 | tf_op jit(solution)/shard_map/reduce_scatter | solution.py:316
  850.2 378.1 %reduce-scatter.13.cloned.1.call-start = ((), (), s32[]{:S(2)}) async-start(), calls=%async_computation.16 | async-start | bytes 9732096 | tf_op jit(solution)/shard_map/reduce_scatter | solution.py:311
  856.4 533.7 %reduce-scatter.11.cloned.1.call-start = ((), (), s32[]{:S(2)}) async-start(), calls=%async_computation.15 | async-start | bytes 12976128 | tf_op jit(solution)/shard_map/reduce_scatter | solution.py:310
  878.4 129.3 %copy-start.27 = (bf16[256,256]{0,1:T(8,128)(2,1)S(1)}, bf16[256,256]{0,1:T(8,128)(2,1)}, u32[]{:S(2)}) copy-start(bf16[256,256]{0,1:T(8,128)(2,1)} %get-tuple-element.38) | copy-start | bytes 393220
  878.4 129.3 %copy-start.39 = (f32[256]{0:T(256)S(1)}, f32[256]{0:T(256)}, u32[]{:S(2)}) copy-start(f32[256]{0:T(256)} %copy-done.38) | copy-start | bytes 3076
  1007.8 47.6 %copy-start.41 = (f32[256]{0:T(256)S(1)}, f32[256]{0:T(256)}, u32[]{:S(2)}) copy-start(f32[256]{0:T(256)} %copy-done.40) | copy-start | bytes 3076
  (29 other events, 152.0 us)
Sparse Core Ops, SparseCore 0:
  10.9 73.0 all-gather.5
  86.9 62.0 all-gather.7
  150.9 61.4 all-gather.9
  359.2 39.7 all-gather.11
  824.1 23.3 reduce-scatter.8
  851.2 53.9 reduce-scatter.16
  910.8 95.5 reduce-scatter.18
  1009.9 76.2 reduce-scatter.14
  1092.6 135.6 reduce-scatter.12
  1235.8 154.2 reduce-scatter.10
where the time goes:
time: 1410 us; the launch traced here: 1400 us
  waiting for transfers between devices  734 us (52%)
  blocking collectives  276 us (20%)
  local copies, waits for them, and re-layouts  151 us (11%)
  matrix products  146 us (10%)
  other arithmetic  58.6 us (4%)
  starting transfers between devices  16.1 us (1%)
  between operations  15.4 us (1%)
    reduce_scatter x1, waiting for transfers between devices, on_device(): lax.psum_scatter(grad_qkv, ('dp', 'ctx', 'exp'), scatter_dimension=0, til...  162 us
    reduce_scatter x1, waiting for transfers between devices, on_device(): lax.psum_scatter(grad_out_proj, ('dp', 'ctx', 'exp'), scatter_dimension=1...  139 us
    all_to_all x1, blocking collectives, on_device(): lax.all_to_all(build_send(inner, pair_of_slot // TOP), 'exp', split_axis=...  109 us
    unnamed x11, waiting for transfers between devices  102 us
    all_to_all x1, waiting for transfers between devices, on_device(): lax.all_to_all(build_send(pair_grads, pair_of_slot), 'exp', split_axis=0,...  98.8 us
    all_to_all x1, waiting for transfers between devices, on_device(): lax.all_to_all(grad_entry, 'exp', split_axis=1, concat_axis=0, tiled=True)  97.9 us
    unnamed x2, blocking collectives  82.9 us
    all_to_all x1, waiting for transfers between devices, on_device(): lax.all_to_all(result, 'exp', split_axis=1, concat_axis=0, tiled=True)  80.4 us
  transfers between devices with their start and end apart: 13, of which 8 were waited for; matrix products, arithmetic and copies ran while one was open for 16% of the time, Pallas kernels for 0%

commit v1 on v0

v1 whole, which is shorter than its diff:
```python
import math

import jax
import jax.numpy as jnp
from jax import lax
from jax.experimental import pallas as pl
from jax.experimental.pallas import tpu as pltpu
from jax.sharding import PartitionSpec as P

QUERY_HEADS = 12
KEY_VALUE_HEADS = 2
HEAD_SIZE = 128
TOP = 4
CORES = 2
LANES = 128


EPS = 1e-06
BASE = 1000000.0
BF16 = jnp.bfloat16
F32 = jnp.float32


def norm_rows(v, gain):
    return v * lax.rsqrt(jnp.mean(v * v, axis=-1, keepdims=True) + EPS) * gain


def rotation_angles(slot_position):
    half = HEAD_SIZE // 2
    freq = jnp.exp(jnp.arange(half, dtype=F32) * (-2.0 * math.log(BASE) / HEAD_SIZE))
    angle = slot_position.astype(F32)[:, None] * freq[None, :]
    return jnp.cos(angle)[:, None, :], jnp.sin(angle)[:, None, :]


def apply_rotation(t, cosine, sine):
    half = HEAD_SIZE // 2
    first = t[..., :half]
    second = t[..., half:]
    return jnp.concatenate(
        [first * cosine - second * sine, second * cosine + first * sine], axis=-1
    )


def place_docs(packed, lengths):
    ends = jnp.cumsum(lengths)
    before = packed[:, None] >= ends[None, :]
    docs = jnp.sum(before.astype(jnp.int32), axis=1)
    starts = jnp.max(jnp.where(before, ends[None, :], 0), axis=1)
    return (docs, packed - starts)


def act_fn(both):
    half = both.shape[-1] // 2
    return jax.nn.gelu(both[..., :half]) * both[..., half:]


def dot(a, b):
    return jnp.dot(a, b, preferred_element_type=F32)


def dot_turned(a, b):
    return lax.dot_general(a, b, (((1,), (1,)), ((), ())), preferred_element_type=F32)


def dot_rows(a, b):
    return lax.dot_general(a, b, (((0,), (0,)), ((), ())), preferred_element_type=F32)


def after(value, *others):
    return lax.optimization_barrier((value, others))[0]


def axis_len(axis):
    if axis == "y":
        return lax.axis_size("ctx") // CORES
    return lax.axis_size(axis)


def axis_place(axis):
    if axis == "y":
        return lax.axis_index("ctx") // CORES
    return lax.axis_index(axis)


def shifted(value, axis, step):
    name, stride = ("ctx", CORES) if axis == "y" else (axis, 1)
    n = lax.axis_size(name)
    return lax.ppermute(value, name, [(i, (i + step * stride) % n) for i in range(n)])


def core_swap(value):
    n = lax.axis_size("ctx")
    return lax.ppermute(value, "ctx", [(i, i ^ 1) for i in range(n)])


def both_cores(value):
    return jnp.concatenate([value, core_swap(value)], axis=0)


def core_sum(value):
    half = value.shape[0] // 2
    other = core_swap(value[half:].astype(BF16))
    return value[:half].astype(F32) + other.astype(F32)


def in_core_order(mine, other):
    core = lax.axis_index("ctx") % CORES
    return jnp.where(core == 0, jnp.stack([mine, other]), jnp.stack([other, mine]))


def plane_gather(first, second, *before_far):
    lists = []
    for value, order in ((first, ("dp", "y")), (second, ("y", "dp"))):
        n1, n2 = axis_len(order[0]), axis_len(order[1])
        near = jnp.stack([value] + [shifted(value, order[0], s) for s in range(1, n1)])
        if before_far:
            near = after(near, *before_far)
        lists.append([near] + [shifted(near, order[1], t) for t in range(1, n2)])
    return lists


def place_blocks(first, second, parts):
    nx, ny = axis_len("dp"), axis_len("y")

    def kernel(place_ref, *refs):
        first_refs, second_refs = refs[:ny], refs[ny : ny + nx]
        outs = refs[ny + nx :]
        at = pl.program_id(0)
        x_step = lax.rem(place_ref[0] - at // ny + nx, nx)
        y_step = lax.rem(place_ref[1] - at % ny + ny, ny)
        first_columns = first_refs[0].shape[2]
        for taken, step, index, left in (
            (first_refs, y_step, x_step, 0),
            (second_refs, x_step, y_step, first_columns),
        ):
            columns_here = taken[0].shape[2]
            for k, block in enumerate(taken):

                @pl.when(step == k)
                def _(block=block):
                    for (row, n_rows, column, columns), out in zip(parts, outs):
                        low, high = max(column, left), min(column + columns, left + columns_here)
                        if low < high:
                            out[:, low - column : high - column] = block[
                                index, row : row + n_rows, low - left : high - left
                            ]

    whole = [
        pl.BlockSpec(v.shape, lambda i, place_ref: (0, 0, 0)) for v in (*first, *second)
    ]
    return pl.pallas_call(
        kernel,
        grid_spec=pltpu.PrefetchScalarGridSpec(
            num_scalar_prefetch=1,
            grid=(nx * ny,),
            in_specs=whole,
            out_specs=[
                pl.BlockSpec((n_rows, columns), lambda i, place_ref: (i, 0))
                for _, n_rows, _, columns in parts
            ],
        ),
        out_shape=[
            jax.ShapeDtypeStruct((nx * ny * n_rows, columns), first[0].dtype)
            for _, n_rows, _, columns in parts
        ],
        compiler_params=pltpu.CompilerParams(vmem_limit_bytes=48 * 1024 * 1024),
        name="place_blocks",
    )(jnp.stack([axis_place("dp"), axis_place("y")]).astype(jnp.int32), *first, *second)


def xor_shift(value, step):
    n = lax.axis_size("exp")
    return lax.ppermute(value, "exp", [(i, i ^ step) for i in range(n)])


def line_gather(value, n):
    blocks = [value]
    for step in range(1, n):
        if step % 2 == 1:
            blocks.append(xor_shift(blocks[step - 1], 1))
        else:
            blocks.append(xor_shift(value, step))
    return blocks


def line_scatter(blocks):
    total = blocks[0].astype(F32) + xor_shift(blocks[1].astype(BF16), 1).astype(F32)
    for step in range(2, len(blocks), 2):
        handed = xor_shift(blocks[step + 1].astype(BF16), 1).astype(F32)
        pair = (blocks[step].astype(F32) + handed).astype(BF16)
        total = total + xor_shift(pair, step).astype(F32)
    return total


def take_block(parts, dim, place):
    return jnp.concatenate(
        [lax.dynamic_index_in_dim(part, place, dim, keepdims=False) for part in parts], axis=-2
    )


def axis_scatter(parts, axis, dim):
    n, place = axis_len(axis), axis_place(axis)
    total = take_block(parts, dim, place).astype(F32)
    for step in range(1, n):
        sent = take_block(parts, dim, lax.rem(place + step, n))
        total = total + shifted(sent, axis, step).astype(F32)
    return total


def plane_scatter(first, second):
    first = axis_scatter(first, "dp", 0).astype(BF16)
    second = axis_scatter(second, "y", 1).astype(BF16)
    return axis_scatter([first], "y", 0), axis_scatter([second], "dp", 0)


def on_device(
    hidden_in,
    lengths,
    order,
    routes,
    cotangent,
    attn_gain,
    qkv_weight,
    out_weight,
    ffn_gain,
    router_weight,
    gate_up_weight,
    down_weight,
):
    hidden = hidden_in[0]
    grad_out = cotangent[0]
    rows, width = hidden.shape
    n_experts = router_weight.shape[1]
    nx, ny, nz = axis_len("dp"), axis_len("y"), axis_len("exp")
    core = lax.axis_index("ctx") % CORES
    other_core = 1 - core
    shard = qkv_weight.shape[0]
    chip_rows = CORES * rows
    query_width = QUERY_HEADS * HEAD_SIZE
    heads = QUERY_HEADS // KEY_VALUE_HEADS
    own_query = heads * HEAD_SIZE
    own_width = own_query + 2 * HEAD_SIZE
    hidden_units = gate_up_weight.shape[2] // 2
    scale = HEAD_SIZE ** (-0.5)

    def head_columns(which):
        query = lax.dynamic_slice_in_dim(qkv_weight, which * own_query, own_query, 1)
        key = lax.dynamic_slice_in_dim(qkv_weight, query_width + which * HEAD_SIZE, HEAD_SIZE, 1)
        value = lax.dynamic_slice_in_dim(
            qkv_weight, query_width + (KEY_VALUE_HEADS + which) * HEAD_SIZE, HEAD_SIZE, 1
        )
        return [query, key, value]

    extra = jnp.concatenate([attn_gain[:, None], ffn_gain[:, None], router_weight], axis=1)
    extra = jnp.pad(extra, ((0, 0), (0, LANES - extra.shape[1])))
    split = 4 * HEAD_SIZE

    def gather_z(mine, theirs):
        pair = in_core_order(mine, core_swap(theirs)).reshape(CORES * shard, -1)
        blocks = line_gather(pair, nz)
        place = lax.axis_index("exp")
        whole = jnp.zeros((CORES, nz, shard, pair.shape[1]), BF16)
        for step, block in enumerate(blocks):
            at = jnp.bitwise_xor(place, step)
            whole = lax.dynamic_update_slice_in_dim(
                whole, block.reshape(CORES, 1, shard, -1), at, 1
            )
        return whole.reshape(CORES * nz * shard, -1)

    qkv_z = gather_z(
        jnp.concatenate(head_columns(core) + [extra], axis=1),
        jnp.concatenate(head_columns(other_core) + [extra], axis=1),
    )
    block_rows = CORES * nz * shard
    w_all, extra_all = place_blocks(
        *plane_gather(qkv_z[:, :split], qkv_z[:, split:]),
        ((0, block_rows, 0, own_width), (0, block_rows, own_width, LANES)),
    )
    gain_one = extra_all[:, 0].astype(F32)
    gain_two = extra_all[:, 1].astype(F32)
    router_all = extra_all[:, 2 : 2 + n_experts]

    out_rows = out_weight.T
    out_z = gather_z(
        after(lax.dynamic_slice_in_dim(out_rows, core * own_query, own_query, 1), qkv_z),
        lax.dynamic_slice_in_dim(out_rows, other_core * own_query, own_query, 1),
    )
    half_query = own_query // 2
    (out_turned,) = place_blocks(
        *plane_gather(*after((out_z[:, :half_query], out_z[:, half_query:]), w_all)),
        ((0, block_rows, 0, own_query),),
    )

    def expert_rows(which):
        return (
            lax.dynamic_index_in_dim(gate_up_weight, which, 0, keepdims=False),
            lax.dynamic_index_in_dim(down_weight, which, 0, keepdims=False),
        )

    gu_mine, down_mine = expert_rows(core)
    gu_shard, down_shard = gu_mine.shape[0], down_mine.shape[0]
    received = core_swap(jnp.concatenate(expert_rows(other_core), axis=0))
    gu_pair = in_core_order(gu_mine, received[:gu_shard]).reshape(CORES * gu_shard, -1)
    down_pair = in_core_order(down_mine, received[gu_shard:]).reshape(CORES * down_shard, -1)
    expert_block = jnp.concatenate([gu_pair, down_pair], axis=0)
    half_width = width // 2
    gate_up_all, down_all = place_blocks(
        *plane_gather(
            expert_block[:, :hidden_units], expert_block[:, hidden_units:], out_turned
        ),
        (
            (0, CORES * gu_shard, 0, 2 * hidden_units),
            (CORES * gu_shard, CORES * down_shard, 0, width),
        ),
    )

    expert_ids = jnp.arange(n_experts, dtype=jnp.int32)
    used = jnp.any(routes[0][:, :, None] == expert_ids[None, None, :], axis=1)
    marks = jnp.pad(used.astype(BF16), ((0, 0), (0, LANES - n_experts)))
    cot_rows = after(jnp.concatenate([grad_out.astype(BF16), marks], axis=1), out_z)
    group = 4 if nz % 4 == 0 else nz
    cot_near = line_gather(cot_rows, group) if group == nz else None

    mean_root = lax.rsqrt(jnp.mean(hidden * hidden, axis=-1, keepdims=True) + EPS)
    normed = (both_cores((hidden * mean_root).astype(BF16)).astype(F32) * gain_one).astype(BF16)
    packed_all, all_lengths = after((order[0], lengths[0]), qkv_z)
    docs_all, place_all = place_docs(packed_all, all_lengths)

    def own_first(values):
        y_place, y_rows = axis_place("y"), chip_rows
        parts = []
        for t in range(ny):
            at = lax.rem(y_place - t + ny, ny) * y_rows
            for which in (core, other_core):
                parts.append(lax.dynamic_slice_in_dim(values, at + which * rows, rows, 0))
        return jnp.concatenate(parts, axis=0)

    packed_keys, docs_keys, place_keys = (own_first(v) for v in (packed_all, docs_all, place_all))
    packed, docs, slot_position = (v[:chip_rows] for v in (packed_keys, docs_keys, place_keys))
    cosine, sine = rotation_angles(slot_position)
    projected = dot(normed, w_all)
    query_out = projected[:, :own_query]
    query_rows = apply_rotation(
        query_out.reshape(chip_rows, heads, HEAD_SIZE), cosine, sine
    ).astype(BF16)
    key_rows = apply_rotation(
        projected[:, own_query : own_query + HEAD_SIZE].reshape(
            chip_rows, 1, HEAD_SIZE
        ),
        cosine,
        sine,
    ).astype(BF16).reshape(chip_rows, HEAD_SIZE)
    value_rows = projected[:, own_query + HEAD_SIZE :].astype(BF16)
    key_value = jnp.concatenate([key_rows, value_rows], axis=1)
    key_value = jnp.concatenate(
        [key_value] + [shifted(key_value, "y", t) for t in range(1, ny)], axis=0
    )
    keys, values = key_value[:, :HEAD_SIZE], key_value[:, HEAD_SIZE:]
    allowed = (docs[:, None] == docs_keys[None, :]) & (packed_keys[None, :] <= packed[:, None])

    def masked_scores():
        scores = jnp.einsum("qhd,kd->hqk", query_rows, keys, preferred_element_type=F32) * scale
        return jnp.where(allowed, scores, -1e30)

    scores = masked_scores()
    top_score = jnp.max(scores, axis=-1)
    weights = jnp.exp(scores - top_score[..., None])
    total = jnp.sum(weights, axis=-1)
    accum = jnp.einsum("hqk,kd->hqd", weights.astype(BF16), values, preferred_element_type=F32)
    lse = top_score + jnp.log(total)
    attended = accum / total[..., None]
    mixed = jnp.transpose(attended, (1, 0, 2)).reshape(chip_rows, own_query).astype(BF16)
    middle = hidden + core_sum(dot_turned(mixed, out_turned))
    inner = norm_rows(middle, gain_two).astype(BF16)

    def dense_gates(chunk, named):
        logits = dot(chunk, router_all)
        return jax.nn.softmax(jnp.where(named, logits, -jnp.inf), axis=-1)

    gates = dense_gates(inner, used)
    own_expert = lax.axis_index("exp") * CORES + core
    is_own = (expert_ids == own_expert).astype(F32)

    def expert_group(inner_near, cot_near):
        cots = [both_cores(c) for c in cot_near]
        chunks = [both_cores(c) for c in inner_near]
        backs, gated, grads = [], [], []
        for chunk, cot_chunk in zip(chunks, cots):
            if backs:
                chunk = after(chunk, partial)
            cot, named = cot_chunk[:, :width], cot_chunk[:, width : width + n_experts] > 0
            gate = jnp.sum(dense_gates(chunk, named) * is_own, axis=-1, keepdims=True)
            act, act_pull = jax.vjp(act_fn, dot(chunk, gate_up_all))
            grad_act = dot_turned(cot, down_all)
            share = jnp.sum(act * grad_act, axis=-1, keepdims=True)
            grad_both = act_pull(grad_act * gate)[0].astype(BF16)
            gated.append((act * gate).astype(BF16))
            grads.append(grad_both)
            partial = dot_turned(grad_both, gate_up_all)
            shares = jnp.pad(share * is_own, ((0, 0), (0, LANES // 2 - n_experts)))
            high = lax.reduce_precision(shares, 8, 7)
            partial = jnp.concatenate([partial, high, shares - high], axis=1).astype(BF16)
            backs.append(core_sum(partial))
        gated_all, grads_all, chunks_all = after(
            (jnp.concatenate(gated, 0), jnp.concatenate(grads, 0), jnp.concatenate(chunks, 0)),
            backs,
        )
        cot_all = jnp.concatenate([c[:, :width] for c in cots], axis=0)
        weight_grads = (
            dot_rows(chunks_all, grads_all[:, :hidden_units]),
            dot_rows(chunks_all, grads_all[:, hidden_units:]),
            dot_rows(gated_all, cot_all),
        )
        partial_out = dot(gated_all, down_all).astype(BF16).reshape(-1, CORES, rows, width)
        outs = partial_out[:, 0].astype(F32) + core_swap(partial_out[:, 1]).astype(F32)
        return line_scatter(backs), outs, weight_grads

    if group == nz:
        grad_back, outs, weight_grads = expert_group(line_gather(inner, nz), cot_near)
    else:

        def visit(_, state):
            inner_here, cot_here, back, out, sums = state
            more_back, outs, more = expert_group(
                line_gather(inner_here, group), line_gather(cot_here, group)
            )
            out = out + line_scatter([outs[i] for i in range(group)])
            sums = tuple(a + b for a, b in zip(sums, more))
            moved = (shifted(v, "exp", nz - group) for v in (inner_here, cot_here, back + more_back, out))
            return (*moved, sums)

        sums = (
            jnp.zeros((width, hidden_units), F32),
            jnp.zeros((width, hidden_units), F32),
            jnp.zeros((hidden_units, width), F32),
        )
        start = (jnp.zeros((rows, width + LANES), F32), jnp.zeros((rows, width), F32), sums)
        _, _, grad_back, moe, weight_grads = lax.fori_loop(
            0, nz // group, visit, (inner, cot_rows, *start)
        )
        outs = None
    grad_gate_weight, grad_up_weight, grad_down_weight = (w.astype(BF16) for w in weight_grads)

    gu_block, down_block = CORES * gu_shard, CORES * down_shard
    first_sum, second_sum = plane_scatter(
        [
            grad_gate_weight.reshape(nx, ny, gu_block, hidden_units),
            grad_down_weight[:, :half_width].reshape(nx, ny, down_block, half_width),
        ],
        [
            grad_up_weight.reshape(nx, ny, gu_block, hidden_units),
            grad_down_weight[:, half_width:].reshape(nx, ny, down_block, half_width),
        ],
    )
    gu_sum = jnp.concatenate([first_sum[:gu_block], second_sum[:gu_block]], axis=1)
    down_sum = jnp.concatenate([first_sum[gu_block:], second_sum[gu_block:]], axis=1)
    gu_sum = gu_sum.reshape(CORES, gu_shard, 2 * hidden_units)
    down_sum = down_sum.reshape(CORES, down_shard, width)

    def of_core(value, which):
        return lax.dynamic_index_in_dim(value, which, 0, keepdims=False)

    received = core_swap(
        jnp.concatenate([of_core(gu_sum, other_core), of_core(down_sum, other_core)], 0).astype(BF16)
    ).astype(F32)
    grad_gate_up = in_core_order(of_core(gu_sum, core), received[:gu_shard])
    grad_down = in_core_order(of_core(down_sum, core), received[gu_shard:])

    shares = (
        grad_back[:, width : width + n_experts]
        + grad_back[:, width + LANES // 2 : width + LANES // 2 + n_experts]
    )
    mean_share = jnp.sum(gates * shares, axis=1, keepdims=True)
    grad_logits = (gates * (shares - mean_share)).astype(BF16)
    grad_router = dot_rows(inner, grad_logits)
    grad_inner = grad_back[:, :width] + dot_turned(grad_logits, router_all)
    _, second_pull = jax.vjp(norm_rows, middle, gain_two)
    grad_middle_norm, grad_ffn_gain = second_pull(grad_inner)
    grad_middle = grad_out + grad_middle_norm
    grad_branch = both_cores(grad_middle.astype(BF16))
    if outs is not None:
        outs = after(outs, grad_branch)
        moe = line_scatter([outs[i] for i in range(nz)])
    grad_out_turned = dot_rows(grad_branch, mixed).astype(BF16)
    blended_gradient = dot(after(grad_branch, grad_out_turned), out_turned).astype(BF16)
    head_gradient = jnp.transpose(
        blended_gradient.reshape(chip_rows, heads, HEAD_SIZE), (1, 0, 2)
    )
    offset = jnp.sum(head_gradient.astype(F32) * attended, axis=-1)
    probs = jnp.exp(masked_scores() - lse[..., None])
    grad_probs = jnp.einsum("hqd,kd->hqk", head_gradient, values, preferred_element_type=F32)
    grad_scores = (probs * (grad_probs - offset[..., None])).astype(BF16)
    grad_query = jnp.einsum("hqk,kd->qhd", grad_scores, keys, preferred_element_type=F32) * scale
    grad_key = (
        jnp.einsum("hqk,qhd->kd", grad_scores, query_rows, preferred_element_type=F32) * scale
    )
    grad_value = jnp.einsum(
        "hqk,hqd->kd", probs.astype(BF16), head_gradient, preferred_element_type=F32
    )
    grad_kv = jnp.concatenate([grad_key, grad_value], axis=1)
    grad_kv_own = grad_kv[:chip_rows]
    for t in range(1, ny):
        part = grad_kv[t * chip_rows : (t + 1) * chip_rows].astype(BF16)
        grad_kv_own = grad_kv_own + shifted(part, "y", ny - t).astype(F32)
    grad_query = apply_rotation(grad_query, cosine, -sine).reshape(chip_rows, own_query)
    grad_key = apply_rotation(
        grad_kv_own[:, :HEAD_SIZE].reshape(chip_rows, 1, HEAD_SIZE), cosine, -sine
    ).reshape(chip_rows, HEAD_SIZE)
    grad_projected = jnp.concatenate(
        [grad_query, grad_key, grad_kv_own[:, HEAD_SIZE:]], axis=1
    ).astype(BF16)
    output = middle + after(moe, grad_projected)
    grad_first, grad_rest = grad_projected[:, :split], grad_projected[:, split:]
    grad_normed = core_sum(dot_turned(grad_projected, w_all))
    _, first_pull = jax.vjp(norm_rows, hidden, gain_one)
    grad_hidden_norm, grad_attn_gain = first_pull(grad_normed)
    grad_input = grad_middle + grad_hidden_norm

    def scatter_sum(first, second):
        first, second = plane_scatter(
            [first.reshape(nx, ny, block_rows, -1)], [second.reshape(nx, ny, block_rows, -1)]
        )
        summed = jnp.concatenate([first, second], axis=1).reshape(CORES, nz, shard, -1)
        place = lax.axis_index("exp")
        return line_scatter(
            [
                lax.dynamic_index_in_dim(summed, jnp.bitwise_xor(place, step), 1, keepdims=False)
                for step in range(nz)
            ]
        )

    out_sum = scatter_sum(grad_out_turned[:, :half_query], grad_out_turned[:, half_query:])
    out_other = core_swap(of_core(out_sum, other_core).astype(BF16)).astype(F32)
    out_sum = in_core_order(of_core(out_sum, core), out_other)
    grad_out_proj = out_sum.swapaxes(0, 1).reshape(shard, query_width).T

    extra_grad = jnp.concatenate([grad_attn_gain[:, None], grad_ffn_gain[:, None], grad_router], 1)
    extra_grad = jnp.pad(extra_grad, ((0, 0), (0, LANES - extra_grad.shape[1]))).astype(BF16)
    qkv_sum = scatter_sum(
        dot_rows(normed, grad_first).astype(BF16),
        jnp.concatenate([dot_rows(normed, grad_rest).astype(BF16), extra_grad], axis=1),
    )
    qkv_other = core_swap(of_core(qkv_sum, other_core).astype(BF16)).astype(F32)
    qkv_mine = of_core(qkv_sum, core)
    extra_sum = qkv_mine[:, own_width:] + qkv_other[:, own_width:]
    pair = in_core_order(qkv_mine[:, :own_width], qkv_other[:, :own_width])
    key_at, value_at = own_query, own_query + HEAD_SIZE
    grad_qkv = jnp.concatenate(
        [
            pair[:, :, :key_at].swapaxes(0, 1).reshape(shard, -1),
            pair[:, :, key_at:value_at].swapaxes(0, 1).reshape(shard, -1),
            pair[:, :, value_at:].swapaxes(0, 1).reshape(shard, -1),
        ],
        axis=1,
    )
    return (
        output[None],
        grad_input[None],
        extra_sum[:, 0],
        grad_qkv,
        grad_out_proj,
        extra_sum[:, 1],
        extra_sum[:, 2 : 2 + n_experts],
        grad_gate_up,
        grad_down,
    )


def solution(mesh):
    return jax.shard_map(
        on_device,
        mesh=mesh,
        in_specs=(
            P(("dp", "exp"), "ctx", None),
            P(("dp", "exp"), None),
            P(("dp", "exp"), None),
            P(("dp", "exp"), "ctx", None),
            P(("dp", "exp"), "ctx", None),
            P(("dp", "ctx", "exp")),
            P(("dp", "ctx", "exp"), None),
            P(None, ("dp", "ctx", "exp")),
            P(("dp", "ctx", "exp")),
            P(("dp", "ctx", "exp"), None),
            P("exp", ("dp", "ctx"), None),
            P("exp", ("dp", "ctx"), None),
        ),
        out_specs=(
            P(("dp", "exp"), "ctx", None),
            P(("dp", "exp"), "ctx", None),
            P(("dp", "ctx", "exp")),
            P(("dp", "ctx", "exp"), None),
            P(None, ("dp", "ctx", "exp")),
            P(("dp", "ctx", "exp")),
            P(("dp", "ctx", "exp"), None),
            P("exp", ("dp", "ctx"), None),
            P("exp", ("dp", "ctx"), None),
        ),
        check_vma=False,
    )
```

time: 1410 us -> 588 us (0.42)
  waiting for transfers between devices: 734 us -> 189 us
  blocking collectives: 276 us -> 0 us
  starting transfers between devices: 16.1 us -> 58.2 us
  local copies, waits for them, and re-layouts: 151 us -> 112 us
  other arithmetic: 58.6 us -> 84.1 us
  matrix products: 146 us -> 123 us
    reduce_scatter x5 -> x0, waiting for transfers between devices: 355 us -> none  [the longest x1 162 us: on_device(): lax.psum_scatter(grad_qkv, ('dp', 'ctx', 'exp'), scatter_dimension=0, til...]
    all_to_all x3 -> x0, waiting for transfers between devices: 277 us -> none  [the longest x1 98.8 us: on_device(): lax.all_to_all(build_send(pair_grads, pair_of_slot), 'exp', split_axis=0,...]
    ppermute x0 -> x73, waiting for transfers between devices: none -> 189 us  [the longest x24 158 us: xor_shift(): return lax.ppermute(value, 'exp', [(i, i ^ step) for i in range(n)])]
    all_to_all x1 -> x0, blocking collectives: 109 us -> none  [on_device(): lax.all_to_all(build_send(inner, pair_of_slot // TOP), 'exp', split_axis=...]
    unnamed x11 -> x0, waiting for transfers between devices: 102 us -> none
    all_gather x3 -> x0, blocking collectives: 84.5 us -> none  [the longest x1 66.8 us: on_device(): lax.all_gather(router_weight, ('dp', 'ctx', 'exp'), axis=0, tiled=True)]
    unnamed x2 -> x0, blocking collectives: 82.9 us -> none
    ppermute x0 -> x73, starting transfers between devices: none -> 58.2 us  [the longest x26 28.4 us: shifted(): lax.ppermute(value, name, [(i, (i + step * stride) % n) for i in range(n)])]
  transfers between devices with their start and end apart: 13 -> 73, of which waited for: 8 -> 27; matrix products, arithmetic and copies ran while one was open for 16% -> 51% of each run, Pallas kernels for 0% -> 2%
where the time goes in v1:
time: 588 us; the launch traced here: 579 us
  waiting for transfers between devices  189 us (32%)
  matrix products  123 us (21%)
  local copies, waits for them, and re-layouts  112 us (19%)
  other arithmetic  84.1 us (14%)
  starting transfers between devices  58.2 us (10%)
  Pallas kernels  8.97 us (2%)
    ppermute x24, waiting for transfers between devices, xor_shift(): return lax.ppermute(value, 'exp', [(i, i ^ step) for i in range(n)])  158 us
    unnamed x264, local copies, waits for them, and re-layouts  48.8 us
    dot_general x12, matrix products, dot(): return jnp.dot(a, b, preferred_element_type=F32)  36.5 us
    ppermute x26, waiting for transfers between devices, shifted(): lax.ppermute(value, name, [(i, (i + step * stride) % n) for i in range(n)])  29.2 us
    ppermute x26, starting transfers between devices, shifted(): lax.ppermute(value, name, [(i, (i + step * stride) % n) for i in range(n)])  28.4 us
    dot_general x11, matrix products, dot_turned(): lax.dot_general(a, b, (((1,), (1,)), ((), ())), preferred_element_type=F32)  27.8 us
    dot_general x7, matrix products, dot_rows(): lax.dot_general(a, b, (((0,), (0,)), ((), ())), preferred_element_type=F32)  26.1 us
    ppermute x24, starting transfers between devices, xor_shift(): return lax.ppermute(value, 'exp', [(i, i ^ step) for i in range(n)])  25.7 us
  transfers between devices with their start and end apart: 73, of which 27 were waited for; matrix products, arithmetic and copies ran while one was open for 51% of the time, Pallas kernels for 2%

profile of v1, /device:TPU:0, one launch (start us, length us, event | category | flops | bytes accessed | tf_op | source)
XLA Modules:
  0.0 579.2 jit_solution(6420332025608040471)
XLA Ops:
  22.8 7.0 %collective-permute-done.1 = bf16[96,1152]{1,0:T(8,128)(2,1)S(1)} collective-permute-done((bf16[96,1152]{1,0:T(8,128)(2,1)S(1)}, bf16[96,1152]{1,0:T(8,128)(2,1)S(1)}, u32[]{:S(2)}, u32[]{:S(2)}) %collective-permute-start.1) | collective-permute-done | bytes 221216 | tf_op jit(solution)/shard_map/ppermute | solution.py:173
  32.8 5.5 collective-permute-done.3
  53.0 4.8 collective-permute-done.13
  68.9 26.9 %collective-permute-done.28 = bf16[256,1664]{0,1:T(8,128)(2,1)} collective-permute-done((bf16[256,1664]{0,1:T(8,128)(2,1)S(1)}, bf16[256,1664]{0,1:T(8,128)(2,1)}, u32[]{:S(2)}, u32[]{:S(2)}) %collective-permute-start.28) | collective-permute-done | bytes 852000 | tf_op jit(solution)/shard_map/ppermute | solution.py:173
  109.4 4.1 fusion.170
  145.9 9.0 %fusion.55 = (bf16[512,6,128]{0,2,1:T(8,128)(2,1)S(1)}, f32[6,512,128]{1,2,0:T(8,128)}) fusion(f32[512,6]{0,1:T(8,128)S(1)} %bitcast.408, bf16[1024,256]{1,0:T(8,128)(2,1)S(1)} %pad_maximum_fusion.34, f32[1024,512,6]{1,0,2:T(8,128)} %copy-done.5, f32[6,512]{1,0:T(8,128)S(1)} %get-tuple-element.197, pred[512,1024]{0,1:T(8,128)(4,1)S(1)} %compare_and_fusion), kind=kOutput, calls=%fused_computation.125 | convolution fusion | flops 818675712 | bytes 15761408 | tf_op jit(solution)/shard_map/hqk,kd->hqd/dot_general | solution.py:369
  168.5 6.2 %collective-permute-done.36 = bf16[256,1664]{0,1:T(8,128)(2,1)S(1)} collective-permute-done((bf16[256,1664]{0,1:T(8,128)(2,1)}, bf16[256,1664]{0,1:T(8,128)(2,1)S(1)}, u32[]{:S(2)}, u32[]{:S(2)}) %collective-permute-start.36) | collective-permute-done | bytes 852000 | tf_op jit(solution)/shard_map/ppermute | solution.py:173
  184.2 32.9 %collective-permute-done.30 = bf16[256,1536]{0,1:T(8,128)(2,1)S(1)} collective-permute-done((bf16[256,1536]{0,1:T(8,128)(2,1)S(1)}, bf16[256,1536]{0,1:T(8,128)(2,1)S(1)}, u32[]{:S(2)}, u32[]{:S(2)}) %collective-permute-start.30) | collective-permute-done | bytes 786464 | tf_op jit(solution)/shard_map/ppermute | solution.py:173
  222.5 5.2 place_blocks.5
  227.8 13.7 %fusion.66 = f32[512,1536]{1,0:T(8,128)S(1)} fusion(bf16[1536,1536]{1,0:T(8,128)(2,1)} %get-tuple-element.39, bf16[256,1536]{0,1:T(8,128)(2,1)} %copy-done.71, bf16[256,1536]{0,1:T(8,128)(2,1)S(1)} %get-tuple-element.100), kind=kOutput, calls=%fused_computation.188 | convolution fusion | flops 2419064832 | bytes 9437184 | tf_op jit(solution)/shard_map/dot_general | solution.py:58
  281.8 7.3 %convolution_convert_fusion.2 = bf16[1536,768]{1,0:T(8,128)(2,1)S(1)} fusion(bf16[2048,1536]{0,1:T(8,128)(2,1)} %constant_dynamic-update-slice_fusion.8, bf16[2048,1536]{1,0:T(8,128)(2,1)S(1)} %pad_maximum_fusion), kind=kOutput, calls=%fused_computation.27 | convolution fusion | flops 4833017856 | bytes 11796480 | tf_op jit(solution)/shard_map/dot_general | solution.py:66
  289.0 7.2 %convolution_convert_fusion.1 = bf16[1536,768]{1,0:T(8,128)(2,1)S(1)} fusion(bf16[2048,1536]{0,1:T(8,128)(2,1)} %constant_dynamic-update-slice_fusion.8, bf16[2048,1536]{1,0:T(8,128)(2,1)S(1)} %pad_maximum_fusion), kind=kOutput, calls=%fused_computation.26 | convolution fusion | flops 4833017856 | bytes 11796480 | tf_op jit(solution)/shard_map/dot_general | solution.py:66
  299.1 5.5 fusion.18
  315.5 5.2 convolution_convert_fusion
  328.8 3.6 copy.234
  334.7 8.2 %collective-permute-done.44 = bf16[256,1664]{0,1:T(8,128)(2,1)} collective-permute-done((bf16[256,1664]{0,1:T(8,128)(2,1)}, bf16[256,1664]{0,1:T(8,128)(2,1)}, u32[]{:S(2)}, u32[]{:S(2)}) %collective-permute-start.44) | collective-permute-done | bytes 852000 | tf_op jit(solution)/shard_map/ppermute | solution.py:173
  358.2 16.1 %collective-permute-done.43 = bf16[256,1664]{0,1:T(8,128)(2,1)S(1)} collective-permute-done((bf16[256,1664]{0,1:T(8,128)(2,1)S(1)}, bf16[256,1664]{0,1:T(8,128)(2,1)S(1)}, u32[]{:S(2)}, u32[]{:S(2)}) %collective-permute-start.43) | collective-permute-done | bytes 852000 | tf_op jit(solution)/shard_map/ppermute | solution.py:173
  374.3 15.0 %collective-permute-done.45 = bf16[256,1664]{0,1:T(8,128)(2,1)S(1)} collective-permute-done((bf16[256,1664]{0,1:T(8,128)(2,1)S(1)}, bf16[256,1664]{0,1:T(8,128)(2,1)S(1)}, u32[]{:S(2)}, u32[]{:S(2)}) %collective-permute-start.45) | collective-permute-done | bytes 852000 | tf_op jit(solution)/shard_map/ppermute | solution.py:173
  401.6 3.3 convert_add_fusion
  415.4 8.4 %fusion.59 = f32[1024,128]{1,0:T(8,128)} fusion(bf16[6,512,128]{1,2,0:T(8,128)(2,1)S(1)} %bitcast.384, f32[1024,512,6]{1,0,2:T(8,128)} %copy-done.5, f32[6,512]{1,0:T(8,128)S(1)} %copy-done.92, pred[512,1024]{0,1:T(8,128)(4,1)S(1)} %copy-done.24), kind=kOutput, calls=%fused_computation.166 | convolution fusion | flops 817889280 | bytes 14430208 | tf_op jit(solution)/shard_map/hqk,hqd->kd/dot_general | solution.py:497
  423.8 7.1 %multiply_convert_fusion = bf16[6,512,1024]{1,2,0:T(8,128)(2,1)S(1)} fusion(f32[1024,512,6]{1,0,2:T(8,128)} %copy-done.5, f32[6,512]{1,0:T(8,128)S(1)} %multiply_reduce_fusion.2, f32[6,512]{1,0:T(8,128)S(1)} %copy-done.92, pred[512,1024]{0,1:T(8,128)(4,1)S(1)} %copy-done.24, bf16[6,512,128]{1,2,0:T(8,128)(2,1)S(1)} %bitcast.385, ...), kind=kOutput, calls=%fused_computation.1 | convolution fusion | flops 824180736 | bytes 20480000 | tf_op jit(solution)/shard_map/hqd,kd->hqk/dot_general | solution.py:491
  462.3 3.8 fusion.169
  485.8 6.8 %collective-permute-done.65 = bf16[2,48,768]{2,1,0:T(8,128)(2,1)S(1)} collective-permute-done((bf16[2,48,768]{2,1,0:T(8,128)(2,1)S(1)}, bf16[2,48,768]{2,1,0:T(8,128)(2,1)S(1)}, u32[]{:S(2)}, u32[]{:S(2)}) %collective-permute-start.65) | collective-permute-done | bytes 147488 | tf_op jit(solution)/shard_map/ppermute | solution.py:173
  496.1 4.2 reshape.591
  500.3 5.9 %constant_dynamic-slice_fusion.4 = (bf16[2,1,384,640]{2,1,0,3:T(2,128)(2,1)}, bf16[2,1,384,640]{2,1,0,3:T(2,128)(2,1)}) fusion(bf16[2,2,384,640]{2,1,0,3:T(2,128)(2,1)S(1)} %reshape.591, s32[]{:T(128)S(6)} %select_n.343, s32[]{:T(128)S(6)} %select_n.344), kind=kLoop, calls=%fused_computation.382 | loop fusion | bytes 3932168 | tf_op jit(solution)/shard_map/jit(dynamic_index_in_dim)/dynamic_slice | solution.py:197
  506.2 4.9 copy.237
  512.5 3.9 fusion.50
  516.4 3.8 copy.236
  525.2 6.7 %collective-permute-done.54 = bf16[2,384,640]{2,1,0:T(8,128)(2,1)} collective-permute-done((bf16[2,384,640]{2,1,0:T(8,128)(2,1)}, bf16[2,384,640]{2,1,0:T(8,128)(2,1)}, u32[]{:S(2)}, u32[]{:S(2)}) %collective-permute-start.54) | collective-permute-done | bytes 983072 | tf_op jit(solution)/shard_map/ppermute | solution.py:88
  536.0 6.4 %collective-permute-done.55 = bf16[384,640]{1,0:T(8,128)(2,1)S(1)} collective-permute-done((bf16[384,640]{1,0:T(8,128)(2,1)S(1)}, bf16[384,640]{1,0:T(8,128)(2,1)S(1)}, u32[]{:S(2)}, u32[]{:S(2)}) %collective-permute-start.55) | collective-permute-done | bytes 491552 | tf_op jit(solution)/shard_map/ppermute | solution.py:88
  544.7 11.0 %collective-permute-done.49 = bf16[256,1536]{0,1:T(8,128)(2,1)S(1)} collective-permute-done((bf16[256,1536]{0,1:T(8,128)(2,1)}, bf16[256,1536]{0,1:T(8,128)(2,1)S(1)}, u32[]{:S(2)}, u32[]{:S(2)}) %collective-permute-start.49) | collective-permute-done | bytes 786464 | tf_op jit(solution)/shard_map/ppermute | solution.py:173
  565.2 8.6 %collective-permute-done.58 = bf16[2,48,1152]{2,1,0:T(8,128)(2,1)} collective-permute-done((bf16[2,48,1152]{2,1,0:T(8,128)(2,1)}, bf16[2,48,1152]{2,1,0:T(8,128)(2,1)}, u32[]{:S(2)}, u32[]{:S(2)}) %collective-permute-start.58) | collective-permute-done | bytes 221216 | tf_op jit(solution)/shard_map/ppermute | solution.py:173
  (646 shorter events, 307.4 us)
Async XLA Ops:
  6.1 34.0 %collective-permute-start.10 = (bf16[48,768]{1,0:T(8,128)(2,1)}, bf16[48,768]{1,0:T(8,128)(2,1)}, u32[]{:S(2)}, u32[]{:S(2)}) collective-permute-start(bf16[48,768]{1,0:T(8,128)(2,1)} %get-tuple-element.172), channel_id=1, source_target_pairs={{0,4},{4,0},{8,12},{12,8},{1,5},{5,1},{9,13},{13,9},{2,6},{6,2},{1... | collective-permute-start | bytes 221192 | tf_op jit(solution)/shard_map/ppermute | solution.py:93
  8.8 50.4 %collective-permute-start.20 = (bf16[288,1536]{1,0:T(8,128)(2,1)}, bf16[288,1536]{1,0:T(8,128)(2,1)}, u32[]{:S(2)}, u32[]{:S(2)}) collective-permute-start(bf16[288,1536]{1,0:T(8,128)(2,1)} %pad_maximum_fusion.25), channel_id=1, source_target_pairs={{0,4},{4,0},{8,12},{12,8},{1,5},{5,1},{9,13},{13,9},{2,6},{6,2},{1... | collective-permute-start | bytes 2654216 | tf_op jit(solution)/shard_map/ppermute | solution.py:93
  57.9 37.9 %collective-permute-start.28 = (bf16[256,1664]{0,1:T(8,128)(2,1)S(1)}, bf16[256,1664]{0,1:T(8,128)(2,1)}, u32[]{:S(2)}, u32[]{:S(2)}) collective-permute-start(bf16[256,1664]{0,1:T(8,128)(2,1)S(1)} %pad_maximum_fusion.27), channel_id=1, source_target_pairs={{0,1},{1,0},{2,3},{3,2},{4,5},{5,4},{6,7},{7,6},{8,9},{9,8},{10,11... | collective-permute-start | bytes 2555912 | tf_op jit(solution)/shard_map/ppermute | solution.py:173
  59.2 40.4 %collective-permute-start.32 = (bf16[256,1664]{0,1:T(8,128)(2,1)S(1)}, bf16[256,1664]{0,1:T(8,128)(2,1)}, u32[]{:S(2)}, u32[]{:S(2)}) collective-permute-start(bf16[256,1664]{0,1:T(8,128)(2,1)S(1)} %pad_maximum_fusion.27), channel_id=1, source_target_pairs={{0,2},{1,3},{2,0},{3,1},{4,6},{5,7},{6,4},{7,5},{8,10},{9,11},{10,... | collective-permute-start | bytes 2555912 | tf_op jit(solution)/shard_map/ppermute | solution.py:173
  63.6 38.6 %collective-permute-start.21 = (bf16[576,768]{1,0:T(8,128)(2,1)S(1)}, bf16[576,768]{1,0:T(8,128)(2,1)S(1)}, u32[]{:S(2)}, u32[]{:S(2)}) collective-permute-start(bf16[576,768]{1,0:T(8,128)(2,1)S(1)} %get-tuple-element.140), channel_id=1, source_target_pairs={{0,16},{16,0},{1,17},{17,1},{2,18},{18,2},{3,19},{19,3},{4,20},{20... | collective-permute-start | bytes 2654216 | tf_op jit(solution)/shard_map/ppermute | solution.py:88
  65.2 40.9 %collective-permute-start.8 = (bf16[2,384,640]{2,1,0:T(8,128)(2,1)S(1)}, bf16[2,384,640]{2,1,0:T(8,128)(2,1)S(1)}, u32[]{:S(2)}, u32[]{:S(2)}) collective-permute-start(bf16[2,384,640]{2,1,0:T(8,128)(2,1)S(1)} %pad_maximum_fusion.23.refs_2_), channel_id=1, source_target_pairs={{0,16},{16,0},{1,17},{17,1},{2,18},{18,2},{3,19},{19,3},{4,20},{20... | collective-permute-start | bytes 2949128 | tf_op jit(solution)/shard_map/ppermute | solution.py:88
  65.9 36.5 %collective-permute-start.6 = (bf16[2,384,512]{2,1,0:T(8,128)(2,1)S(1)}, bf16[2,384,512]{2,1,0:T(8,128)(2,1)S(1)}, u32[]{:S(2)}, u32[]{:S(2)}) collective-permute-start(bf16[2,384,512]{2,1,0:T(8,128)(2,1)S(1)} %pad_maximum_fusion.28.refs_0_), channel_id=1, source_target_pairs={{0,8},{4,12},{8,0},{12,4},{1,9},{5,13},{9,1},{13,5},{2,10},{6,14},... | collective-permute-start | bytes 2359304 | tf_op jit(solution)/shard_map/ppermute | solution.py:88
  99.6 60.7 %collective-permute-start.23 = (bf16[576,768]{1,0:T(8,128)(2,1)}, bf16[576,768]{1,0:T(8,128)(2,1)}, u32[]{:S(2)}, u32[]{:S(2)}) collective-permute-start(bf16[576,768]{1,0:T(8,128)(2,1)} %get-tuple-element.139), channel_id=1, source_target_pairs={{0,8},{4,12},{8,0},{12,4},{1,9},{5,13},{9,1},{13,5},{2,10},{6,14},... | collective-permute-start | bytes 2654216 | tf_op jit(solution)/shard_map/ppermute | solution.py:88
  102.2 60.5 %collective-permute-start.29 = (bf16[256,1664]{0,1:T(8,128)(2,1)}, bf16[256,1664]{0,1:T(8,128)(2,1)}, u32[]{:S(2)}, u32[]{:S(2)}) collective-permute-start(bf16[256,1664]{0,1:T(8,128)(2,1)} %collective-permute-done.28), channel_id=1, source_target_pairs={{0,4},{4,0},{8,12},{12,8},{1,5},{5,1},{9,13},{13,9},{2,6},{6,2},{1... | collective-permute-start | bytes 2555912 | tf_op jit(solution)/shard_map/ppermute | solution.py:93
  102.4 62.8 %collective-permute-start.33 = (bf16[256,1664]{0,1:T(8,128)(2,1)}, bf16[256,1664]{0,1:T(8,128)(2,1)}, u32[]{:S(2)}, u32[]{:S(2)}) collective-permute-start(bf16[256,1664]{0,1:T(8,128)(2,1)} %collective-permute-done.32), channel_id=1, source_target_pairs={{0,4},{4,0},{8,12},{12,8},{1,5},{5,1},{9,13},{13,9},{2,6},{6,2},{1... | collective-permute-start | bytes 2555912 | tf_op jit(solution)/shard_map/ppermute | solution.py:93
  174.7 47.8 %collective-permute-start.22 = (bf16[2,576,768]{2,1,0:T(8,128)(2,1)S(1)}, bf16[2,576,768]{2,1,0:T(8,128)(2,1)S(1)}, u32[]{:S(2)}, u32[]{:S(2)}) collective-permute-start(bf16[2,576,768]{2,1,0:T(8,128)(2,1)S(1)} %pad_maximum_fusion.4.refs_0_), channel_id=1, source_target_pairs={{0,8},{4,12},{8,0},{12,4},{1,9},{5,13},{9,1},{13,5},{2,10},{6,14},... | collective-permute-start | bytes 5308424 | tf_op jit(solution)/shard_map/ppermute | solution.py:88
  176.2 46.3 %collective-permute-start.24 = (bf16[2,576,768]{2,1,0:T(8,128)(2,1)S(1)}, bf16[2,576,768]{2,1,0:T(8,128)(2,1)}, u32[]{:S(2)}, u32[]{:S(2)}) collective-permute-start(bf16[2,576,768]{2,1,0:T(8,128)(2,1)S(1)} %pad_maximum_fusion.5.refs_2_), channel_id=1, source_target_pairs={{0,16},{16,0},{1,17},{17,1},{2,18},{18,2},{3,19},{19,3},{4,20},{20... | collective-permute-start | bytes 5308424 | tf_op jit(solution)/shard_map/ppermute | solution.py:88
  179.1 38.1 %collective-permute-start.19 = (bf16[256,1536]{0,1:T(8,128)(2,1)S(1)}, bf16[256,1536]{0,1:T(8,128)(2,1)S(1)}, u32[]{:S(2)}, u32[]{:S(2)}) collective-permute-start(bf16[256,1536]{0,1:T(8,128)(2,1)S(1)} %get-tuple-element.100), channel_id=1, source_target_pairs={{0,4},{4,0},{8,12},{12,8},{1,5},{5,1},{9,13},{13,9},{2,6},{6,2},{1... | collective-permute-start | bytes 2359304 | tf_op jit(solution)/shard_map/ppermute | solution.py:93
  179.1 38.2 %collective-permute-start.26 = (bf16[256,1536]{0,1:T(8,128)(2,1)S(1)}, bf16[256,1536]{0,1:T(8,128)(2,1)S(1)}, u32[]{:S(2)}, u32[]{:S(2)}) collective-permute-start(bf16[256,1536]{0,1:T(8,128)(2,1)S(1)} %get-tuple-element.100), channel_id=1, source_target_pairs={{0,1},{1,0},{2,3},{3,2},{4,5},{5,4},{6,7},{7,6},{8,9},{9,8},{10,11... | collective-permute-start | bytes 2359304 | tf_op jit(solution)/shard_map/ppermute | solution.py:173
  179.7 37.5 %collective-permute-start.30 = (bf16[256,1536]{0,1:T(8,128)(2,1)S(1)}, bf16[256,1536]{0,1:T(8,128)(2,1)S(1)}, u32[]{:S(2)}, u32[]{:S(2)}) collective-permute-start(bf16[256,1536]{0,1:T(8,128)(2,1)S(1)} %get-tuple-element.100), channel_id=1, source_target_pairs={{0,2},{1,3},{2,0},{3,1},{4,6},{5,7},{6,4},{7,5},{8,10},{9,11},{10,... | collective-permute-start | bytes 2359304 | tf_op jit(solution)/shard_map/ppermute | solution.py:173
  217.2 40.8 %collective-permute-start.31 = (bf16[256,1536]{0,1:T(8,128)(2,1)S(1)}, bf16[256,1536]{0,1:T(8,128)(2,1)S(1)}, u32[]{:S(2)}, u32[]{:S(2)}) collective-permute-start(bf16[256,1536]{0,1:T(8,128)(2,1)S(1)} %collective-permute-done.30), channel_id=1, source_target_pairs={{0,4},{4,0},{8,12},{12,8},{1,5},{5,1},{9,13},{13,9},{2,6},{6,2},{1... | collective-permute-start | bytes 2359304 | tf_op jit(solution)/shard_map/ppermute | solution.py:93
  217.2 52.4 %collective-permute-start.34 = (bf16[256,1536]{0,1:T(8,128)(2,1)S(1)}, bf16[256,1536]{0,1:T(8,128)(2,1)S(1)}, u32[]{:S(2)}, u32[]{:S(2)}) collective-permute-start(bf16[256,1536]{0,1:T(8,128)(2,1)S(1)} %collective-permute-done.30), channel_id=1, source_target_pairs={{0,1},{1,0},{2,3},{3,2},{4,5},{5,4},{6,7},{7,6},{8,9},{9,8},{10,11... | collective-permute-start | bytes 2359304 | tf_op jit(solution)/shard_map/ppermute | solution.py:173
  217.3 30.9 %collective-permute-start.27 = (bf16[256,1536]{0,1:T(8,128)(2,1)S(1)}, bf16[256,1536]{0,1:T(8,128)(2,1)S(1)}, u32[]{:S(2)}, u32[]{:S(2)}) collective-permute-start(bf16[256,1536]{0,1:T(8,128)(2,1)S(1)} %collective-permute-done.26), channel_id=1, source_target_pairs={{0,4},{4,0},{8,12},{12,8},{1,5},{5,1},{9,13},{13,9},{2,6},{6,2},{1... | collective-permute-start | bytes 2359304 | tf_op jit(solution)/shard_map/ppermute | solution.py:93
  265.0 67.4 %collective-permute-start.39 = (bf16[256,1664]{0,1:T(8,128)(2,1)}, bf16[256,1664]{0,1:T(8,128)(2,1)}, u32[]{:S(2)}, u32[]{:S(2)}) collective-permute-start(bf16[256,1664]{0,1:T(8,128)(2,1)} %slice.410), channel_id=1, source_target_pairs={{0,4},{4,0},{8,12},{12,8},{1,5},{5,1},{9,13},{13,9},{2,6},{6,2},{1... | collective-permute-start | bytes 2555912 | tf_op jit(solution)/shard_map/ppermute | solution.py:93
  269.1 65.1 %collective-permute-start.40 = (bf16[256,1664]{0,1:T(8,128)(2,1)}, bf16[256,1664]{0,1:T(8,128)(2,1)}, u32[]{:S(2)}, u32[]{:S(2)}) collective-permute-start(bf16[256,1664]{0,1:T(8,128)(2,1)} %slice.412), channel_id=1, source_target_pairs={{0,4},{4,0},{8,12},{12,8},{1,5},{5,1},{9,13},{13,9},{2,6},{6,2},{1... | collective-permute-start | bytes 2555912 | tf_op jit(solution)/shard_map/ppermute | solution.py:93
  308.3 41.3 %collective-permute-start.68 = (bf16[2,576,768]{2,1,0:T(8,128)(2,1)}, bf16[2,576,768]{2,1,0:T(8,128)(2,1)}, u32[]{:S(2)}, u32[]{:S(2)}) collective-permute-start(bf16[2,576,768]{2,1,0:T(8,128)(2,1)} %pad_maximum_fusion.7), channel_id=1, source_target_pairs={{0,16},{16,0},{1,17},{17,1},{2,18},{18,2},{3,19},{19,3},{4,20},{20... | collective-permute-start | bytes 5308424 | tf_op jit(solution)/shard_map/ppermute | solution.py:88
  313.1 41.0 %collective-permute-start.70 = (bf16[2,576,768]{2,1,0:T(8,128)(2,1)}, bf16[2,576,768]{2,1,0:T(8,128)(2,1)}, u32[]{:S(2)}, u32[]{:S(2)}) collective-permute-start(bf16[2,576,768]{2,1,0:T(8,128)(2,1)} %pad_maximum_fusion.8), channel_id=1, source_target_pairs={{0,8},{4,12},{8,0},{12,4},{1,9},{5,13},{9,1},{13,5},{2,10},{6,14},... | collective-permute-start | bytes 5308424 | tf_op jit(solution)/shard_map/ppermute | solution.py:88
  334.3 67.3 %collective-permute-start.42 = (bf16[4,256,1536]{1,2,0:T(8,128)(2,1)}, bf16[4,256,1536]{1,2,0:T(8,128)(2,1)S(1)}, u32[]{:S(2)}, u32[]{:S(2)}) collective-permute-start(bf16[4,256,1536]{1,2,0:T(8,128)(2,1)} %bitcast.379), channel_id=1, source_target_pairs={{0,4},{4,0},{8,12},{12,8},{1,5},{5,1},{9,13},{13,9},{2,6},{6,2},{1... | collective-permute-start | bytes 9437192 | tf_op jit(solution)/shard_map/ppermute | solution.py:93
  342.9 31.4 %collective-permute-start.43 = (bf16[256,1664]{0,1:T(8,128)(2,1)S(1)}, bf16[256,1664]{0,1:T(8,128)(2,1)S(1)}, u32[]{:S(2)}, u32[]{:S(2)}) collective-permute-start(bf16[256,1664]{0,1:T(8,128)(2,1)S(1)} %fusion.167), channel_id=1, source_target_pairs={{0,1},{1,0},{2,3},{3,2},{4,5},{5,4},{6,7},{7,6},{8,9},{9,8},{10,11... | collective-permute-start | bytes 2555912 | tf_op jit(solution)/shard_map/ppermute | solution.py:173
  349.6 39.7 %collective-permute-start.45 = (bf16[256,1664]{0,1:T(8,128)(2,1)S(1)}, bf16[256,1664]{0,1:T(8,128)(2,1)S(1)}, u32[]{:S(2)}, u32[]{:S(2)}) collective-permute-start(bf16[256,1664]{0,1:T(8,128)(2,1)S(1)} %add_convert_fusion.6), channel_id=1, source_target_pairs={{0,2},{1,3},{2,0},{3,1},{4,6},{5,7},{6,4},{7,5},{8,10},{9,11},{10,... | collective-permute-start | bytes 2555912 | tf_op jit(solution)/shard_map/ppermute | solution.py:173
  354.2 39.6 %collective-permute-start.69 = (bf16[576,768]{1,0:T(8,128)(2,1)S(1)}, bf16[576,768]{1,0:T(8,128)(2,1)S(1)}, u32[]{:S(2)}, u32[]{:S(2)}) collective-permute-start(bf16[576,768]{1,0:T(8,128)(2,1)S(1)} %dynamic-slice_bitcast_fusion.5), channel_id=1, source_target_pairs={{0,8},{4,12},{8,0},{12,4},{1,9},{5,13},{9,1},{13,5},{2,10},{6,14},... | collective-permute-start | bytes 2654216 | tf_op jit(solution)/shard_map/ppermute | solution.py:88
  357.1 38.1 %collective-permute-start.71 = (bf16[576,768]{1,0:T(8,128)(2,1)S(1)}, bf16[576,768]{1,0:T(8,128)(2,1)S(1)}, u32[]{:S(2)}, u32[]{:S(2)}) collective-permute-start(bf16[576,768]{1,0:T(8,128)(2,1)S(1)} %dynamic-slice_bitcast_fusion.4), channel_id=1, source_target_pairs={{0,16},{16,0},{1,17},{17,1},{2,18},{18,2},{3,19},{19,3},{4,20},{20... | collective-permute-start | bytes 2654216 | tf_op jit(solution)/shard_map/ppermute | solution.py:88
  399.1 53.1 %collective-permute-start.72 = (bf16[288,1536]{1,0:T(8,128)(2,1)}, bf16[288,1536]{1,0:T(8,128)(2,1)}, u32[]{:S(2)}, u32[]{:S(2)}) collective-permute-start(bf16[288,1536]{1,0:T(8,128)(2,1)} %pad_maximum_fusion.26), channel_id=1, source_target_pairs={{0,4},{4,0},{8,12},{12,8},{1,5},{5,1},{9,13},{13,9},{2,6},{6,2},{1... | collective-permute-start | bytes 2654216 | tf_op jit(solution)/shard_map/ppermute | solution.py:93
  460.3 84.4 %collective-permute-start.47 = (bf16[256,1536]{0,1:T(8,128)(2,1)}, bf16[256,1536]{0,1:T(8,128)(2,1)}, u32[]{:S(2)}, u32[]{:S(2)}) collective-permute-start(bf16[256,1536]{0,1:T(8,128)(2,1)} %get-tuple-element.123), channel_id=1, source_target_pairs={{0,1},{1,0},{2,3},{3,2},{4,5},{5,4},{6,7},{7,6},{8,9},{9,8},{10,11... | collective-permute-start | bytes 2359304 | tf_op jit(solution)/shard_map/ppermute | solution.py:173
  478.3 55.8 %collective-permute-start.53 = (bf16[384,512]{1,0:T(8,128)(2,1)}, bf16[384,512]{1,0:T(8,128)(2,1)}, u32[]{:S(2)}, u32[]{:S(2)}) collective-permute-start(bf16[384,512]{1,0:T(8,128)(2,1)} %dynamic-slice_bitcast_fusion.15), channel_id=1, source_target_pairs={{0,8},{4,12},{8,0},{12,4},{1,9},{5,13},{9,1},{13,5},{2,10},{6,14},... | collective-permute-start | bytes 1179656 | tf_op jit(solution)/shard_map/ppermute | solution.py:88
  485.7 36.1 %collective-permute-start.64 = (bf16[2,48,768]{2,1,0:T(8,128)(2,1)}, bf16[2,48,768]{2,1,0:T(8,128)(2,1)}, u32[]{:S(2)}, u32[]{:S(2)}) collective-permute-start(bf16[2,48,768]{2,1,0:T(8,128)(2,1)} %get-tuple-element.147), channel_id=1, source_target_pairs={{0,1},{1,0},{2,3},{3,2},{4,5},{5,4},{6,7},{7,6},{8,9},{9,8},{10,11... | collective-permute-start | bytes 442376 | tf_op jit(solution)/shard_map/ppermute | solution.py:173
  521.8 33.9 %collective-permute-start.49 = (bf16[256,1536]{0,1:T(8,128)(2,1)}, bf16[256,1536]{0,1:T(8,128)(2,1)S(1)}, u32[]{:S(2)}, u32[]{:S(2)}) collective-permute-start(bf16[256,1536]{0,1:T(8,128)(2,1)} %fusion.53), channel_id=1, source_target_pairs={{0,2},{1,3},{2,0},{3,1},{4,6},{5,7},{6,4},{7,5},{8,10},{9,11},{10,... | collective-permute-start | bytes 2359304 | tf_op jit(solution)/shard_map/ppermute | solution.py:173
  (163 other events, 1907.3 us)

commit v2 on v1

v2 whole, which is shorter than its diff:
```python
import math

import jax
import jax.numpy as jnp
from jax import lax
from jax.experimental import pallas as pl
from jax.experimental.pallas import tpu as pltpu
from jax.sharding import PartitionSpec as P

QUERY_HEADS = 12
KEY_VALUE_HEADS = 2
HEAD_SIZE = 128
TOP = 4
CORES = 2
LANES = 128
ROUTER_LANE = 2


EPS = 1e-06
BASE = 1000000.0
BF16 = jnp.bfloat16
F32 = jnp.float32


def norm_rows(v, gain):
    return v * lax.rsqrt(jnp.mean(v * v, axis=-1, keepdims=True) + EPS) * gain


def norm_back(v, gain, grad):
    root = lax.rsqrt(jnp.mean(v * v, axis=-1, keepdims=True) + EPS)
    unit = v * root
    scaled = grad * gain
    along = jnp.mean(scaled * unit, axis=-1, keepdims=True)
    return root * (scaled - unit * along), (grad * unit).astype(BF16)


def rotation_tables(slot_position):
    half = HEAD_SIZE // 2
    freq = jnp.exp(jnp.arange(half, dtype=F32) * (-2.0 * math.log(BASE) / HEAD_SIZE))
    angle = slot_position.astype(F32)[:, None] * freq[None, :]
    cosine, sine = jnp.cos(angle), jnp.sin(angle)
    return jnp.concatenate([cosine, cosine], axis=1), jnp.concatenate([-sine, sine], axis=1)


def rotate(t, cosine, sine):
    half = HEAD_SIZE // 2
    return t * cosine + jnp.concatenate([t[:, half:], t[:, :half]], axis=1) * sine


def doc_starts(packed, lengths):
    ends = jnp.cumsum(lengths)
    return jnp.max(jnp.where(packed[:, None] >= ends[None, :], ends[None, :], 0), axis=1)


def dot(a, b):
    return jnp.dot(a, b, preferred_element_type=F32)


def dot_turned(a, b):
    return lax.dot_general(a, b, (((1,), (1,)), ((), ())), preferred_element_type=F32)


def dot_rows(a, b):
    return lax.dot_general(a, b, (((0,), (0,)), ((), ())), preferred_element_type=F32)


def after(value, *others):
    values, tree = jax.tree.flatten(value)
    others = jax.tree.leaves(others)

    def kernel(*refs):
        pass

    anywhere = pl.BlockSpec(memory_space=pl.ANY)
    tied = pl.pallas_call(
        kernel,
        out_shape=[jax.ShapeDtypeStruct(v.shape, v.dtype) for v in values],
        in_specs=[anywhere] * (len(values) + len(others)),
        out_specs=[anywhere] * len(values),
        input_output_aliases={i: i for i in range(len(values))},
        cost_estimate=pl.CostEstimate(flops=1, bytes_accessed=1, transcendentals=0),
        name="after",
    )(*values, *others)
    return jax.tree.unflatten(tree, tied)


def axis_len(axis):
    if axis == "y":
        return lax.axis_size("ctx") // CORES
    return lax.axis_size(axis)


def axis_place(axis):
    if axis == "y":
        return lax.axis_index("ctx") // CORES
    return lax.axis_index(axis)


def shifted(value, axis, step):
    name, stride = ("ctx", CORES) if axis == "y" else (axis, 1)
    n = lax.axis_size(name)
    return lax.ppermute(value, name, [(i, (i + step * stride) % n) for i in range(n)])


def core_swap(value):
    n = lax.axis_size("ctx")
    return lax.ppermute(value, "ctx", [(i, i ^ 1) for i in range(n)])


def both_cores(value):
    return jnp.concatenate([value, core_swap(value)], axis=0)


def core_sum(value):
    half = value.shape[0] // 2
    other = core_swap(value[half:].astype(BF16))
    return value[:half].astype(F32) + other.astype(F32)


def in_core_order(mine, other):
    core = lax.axis_index("ctx") % CORES
    return jnp.where(core == 0, jnp.stack([mine, other]), jnp.stack([other, mine]))


def plane_first(first, second):
    nx, ny = axis_len("dp"), axis_len("y")
    return (
        {(s, 0): shifted(first, "dp", s) for s in range(1, nx)},
        {(0, t): shifted(second, "y", t) for t in range(1, ny)},
    )


def plane_second(first, second):
    nx, ny = axis_len("dp"), axis_len("y")
    return (
        {(0, t): shifted(first, "y", t) for t in range(1, ny)},
        {(s, 0): shifted(second, "dp", s) for s in range(1, nx)},
    )


def plane_third(came):
    nx, ny = axis_len("dp"), axis_len("y")
    return (
        {(s, t): shifted(came[0][s, 0], "y", t) for s in range(1, nx) for t in range(1, ny)},
        {(s, t): shifted(came[1][0, t], "dp", s) for s in range(1, nx) for t in range(1, ny)},
    )


def place_blocks(halves, came, parts):
    nx, ny = axis_len("dp"), axis_len("y")
    steps = [(s, t) for s in range(nx) for t in range(ny)]
    blocks = []
    for k, half in enumerate(halves):
        known = {(0, 0): half}
        for pair in came:
            known.update(pair[k])
        blocks.append([known[step] for step in steps])

    def kernel(place_ref, *refs):
        first_refs, second_refs = refs[: len(steps)], refs[len(steps) : 2 * len(steps)]
        outs = refs[2 * len(steps) :]
        at = pl.program_id(0)
        x_step = lax.rem(place_ref[0] - at // ny + nx, nx)
        y_step = lax.rem(place_ref[1] - at % ny + ny, ny)
        left = first_refs[0].shape[1]
        for step, first, second in zip(steps, first_refs, second_refs):

            @pl.when((x_step == step[0]) & (y_step == step[1]))
            def _(first=first, second=second):
                for (row, n_rows, column, columns), out in zip(parts, outs):
                    for block, low, high in (
                        (first, 0, left),
                        (second, left, left + second.shape[1]),
                    ):
                        begin, end = max(column, low), min(column + columns, high)
                        if begin < end:
                            out[:, begin - column : end - column] = block[
                                row : row + n_rows, begin - low : end - low
                            ]

    whole = [pl.BlockSpec(v.shape, lambda i, place_ref: (0, 0)) for v in (*blocks[0], *blocks[1])]
    return pl.pallas_call(
        kernel,
        grid_spec=pltpu.PrefetchScalarGridSpec(
            num_scalar_prefetch=1,
            grid=(nx * ny,),
            in_specs=whole,
            out_specs=[
                pl.BlockSpec((n_rows, columns), lambda i, place_ref: (i, 0))
                for _, n_rows, _, columns in parts
            ],
        ),
        out_shape=[
            jax.ShapeDtypeStruct((nx * ny * n_rows, columns), BF16)
            for _, n_rows, _, columns in parts
        ],
        compiler_params=pltpu.CompilerParams(vmem_limit_bytes=48 * 1024 * 1024),
        cost_estimate=pl.CostEstimate(flops=1, bytes_accessed=1, transcendentals=0),
        name="place_blocks",
    )(jnp.stack([axis_place("dp"), axis_place("y")]).astype(jnp.int32), *blocks[0], *blocks[1])


def xor_shift(value, step):
    n = lax.axis_size("exp")
    return lax.ppermute(value, "exp", [(i, i ^ step) for i in range(n)])


def line_gather(value, n, *waits):
    blocks = [value]
    for step in range(1, n):
        if step % 2 == 1:
            handed = blocks[step - 1]
            if waits and step > 1:
                handed = blocks[step - 1] = after(handed, *waits)
            blocks.append(xor_shift(handed, 1))
        else:
            blocks.append(xor_shift(value, step))
    return blocks


def line_pairs(blocks, handed):
    return [
        (blocks[step].astype(F32) + other.astype(F32)).astype(BF16)
        for step, other in zip(range(2, len(blocks), 2), handed)
    ]


def line_far(blocks, near, pairs):
    total = blocks[0].astype(F32) + near.astype(F32)
    for step, pair in zip(range(2, len(blocks), 2), pairs):
        total = total + xor_shift(pair, step).astype(F32)
    return total


def line_scatter(blocks):
    odd = xor_shift(jnp.stack(blocks[1::2]), 1)
    pairs = line_pairs(blocks, odd[1:])
    return line_far(blocks, odd[0], pairs), pairs


PLANE_AXES = (("dp", "y"), ("y", "dp"))


def plane_places():
    return jnp.stack([axis_place("dp"), axis_place("y")]).astype(jnp.int32)


def plane_blocks(parts, axes):
    half = []
    for near in range(axis_len(axes[0])):
        blocks = []
        for far in range(axis_len(axes[1])):
            s, t = (near, far) if axes[0] == "dp" else (far, near)
            x = lax.rem(axis_place("dp") + s, axis_len("dp"))
            y = lax.rem(axis_place("y") + t, axis_len("y"))
            taken = [
                lax.dynamic_slice(part, (x, y, 0, 0), (1, 1, *part.shape[2:])).reshape(
                    part.shape[2:]
                )
                for part in parts
            ]
            blocks.append(jnp.concatenate(taken, axis=0))
        half.append(blocks)
    return half


def plane_moved(halves):
    return [
        [shifted(blocks, axes[0], near) for near, blocks in enumerate(half) if near > 0]
        for half, axes in zip(halves, PLANE_AXES)
    ]


def plane_moved_part(halves, handed_on):
    return [
        [
            [shifted(block, axes[0], near) for block in (blocks[1:] if handed_on else blocks[:1])]
            for near, blocks in enumerate(half)
            if near > 0
        ]
        for half, axes in zip(halves, PLANE_AXES)
    ]


def plane_joined(stay, handed_on):
    return [[a + b for a, b in zip(*half)] for half in zip(stay, handed_on)]


def half_sum(half, received, far):
    total = half[0][far].astype(F32)
    for blocks in received:
        total = total + blocks[far].astype(F32)
    return total


def plane_hand_on(halves, received):
    return [
        [half_sum(half, came, far).astype(BF16) for far in range(1, len(half[0]))]
        for half, came in zip(halves, received)
    ]


def plane_handed(handed):
    return [
        [shifted(block, axes[1], far) for far, block in enumerate(blocks, 1)]
        for blocks, axes in zip(handed, PLANE_AXES)
    ]


def plane_sum(halves, received, handed):
    sums = []
    for half, came, last in zip(halves, received, handed):
        total = half_sum(half, came, 0)
        for block in last:
            total = total + block.astype(F32)
        sums.append(total)
    return sums


def half_shapes(shapes):
    counts = [(axis_len(axes[0]), axis_len(axes[1])) for axes in PLANE_AXES]
    return [(far, *shape) for (near, far), shape in zip(counts, shapes) for _ in range(near)]


def two_halves(arrays):
    n = axis_len("dp")
    return [list(arrays[:n]), list(arrays[n:])]


def store_blocks(place_ref, at, outs, first, second):
    nx, ny = axis_len("dp"), axis_len("y")
    x_step, y_step = step_to(place_ref, at)
    for s in range(nx):

        @pl.when(x_step == s)
        def _(s=s):
            first(outs[s].at[y_step])

    for t in range(ny):

        @pl.when(y_step == t)
        def _(t=t):
            second(outs[nx + t].at[x_step])


def blocks_a_step(block_rows):
    n = 1
    while n * block_rows % LANES != 0:
        n += 1
    return n


def step_to(place_ref, at):
    nx, ny = axis_len("dp"), axis_len("y")
    return lax.rem(at // ny - place_ref[0] + nx, nx), lax.rem(at % ny - place_ref[1] + ny, ny)


SMALL = pl.CostEstimate(flops=1, bytes_accessed=1, transcendentals=0)
LOG2_E = 1.4426950408889634
GELU_ROOT = math.sqrt(2.0 / math.pi)
GELU_CUBE = 0.044715
ROW_TILE = 256


def kernel_params(n_axes=1):
    return pltpu.CompilerParams(
        dimension_semantics=("arbitrary",) * n_axes, vmem_limit_bytes=56 * 1024 * 1024
    )


def contract(a, b, a_dim, b_dim):
    return lax.dot_general(a, b, (((a_dim,), (b_dim,)), ((), ())), preferred_element_type=F32)


def turned(t, cosine, sine):
    return t * cosine + pltpu.roll(t, HEAD_SIZE // 2, 1) * sine


def fill_keys(parts, keys_ref, values_ref):
    for i, part in enumerate(parts):
        n = part.shape[0]
        keys_ref[i * n : (i + 1) * n, :] = part[:, :HEAD_SIZE]
        values_ref[i * n : (i + 1) * n, :] = part[:, HEAD_SIZE:]


def fill_bias(key_place_ref, bounds_ref, bias_ref):
    place = key_place_ref[...]
    allowed = (place >= bounds_ref[0:1, :]) & (place <= bounds_ref[1:2, :])
    bias_ref[...] = jnp.where(allowed, 0.0, -1e30)


def unit_rows(rows, *waits):
    def kernel(rows_ref, *refs):
        value = rows_ref[...]
        root = lax.rsqrt(jnp.mean(value * value, axis=-1, keepdims=True) + EPS)
        refs[-1][...] = (value * root).astype(BF16)

    return pl.pallas_call(
        kernel,
        in_specs=[pl.BlockSpec(memory_space=pltpu.VMEM)]
        + [pl.BlockSpec(memory_space=pl.ANY)] * len(waits),
        out_specs=pl.BlockSpec(memory_space=pltpu.VMEM),
        out_shape=jax.ShapeDtypeStruct(rows.shape, BF16),
        compiler_params=pltpu.CompilerParams(vmem_limit_bytes=32 * 1024 * 1024),
        cost_estimate=SMALL,
        name="unit_rows",
    )(rows, *waits)


def attention_forward(projected, key_value, cosine, sine, key_place, bounds, heads, *waits):
    rows = projected.shape[0]
    n_keys = key_place.shape[0]
    n_parts = len(key_value)
    factor = HEAD_SIZE ** (-0.5) * LOG2_E

    def kernel(projected_ref, cos_ref, sin_ref, place_ref, bounds_ref, *refs):
        parts = refs[:n_parts]
        query_ref, mixed_ref, lse_ref, keys_ref, values_ref, bias_ref = refs[n_parts + len(waits) :]
        head = pl.program_id(0)

        @pl.when(head == 0)
        def _():
            fill_keys(parts, keys_ref, values_ref)
            fill_bias(place_ref, bounds_ref, bias_ref)

        for start in range(0, rows, ROW_TILE):
            tile = slice(start, start + ROW_TILE)
            query = turned(projected_ref[tile, :], cos_ref[tile, :], sin_ref[tile, :]).astype(BF16)
            query_ref[tile, :] = query
            scores = contract(keys_ref[...], query, 1, 1) * factor + bias_ref[:, tile]
            top = jnp.max(scores, axis=0, keepdims=True)
            weights = jnp.exp2(scores - top)
            total = jnp.sum(weights, axis=0, keepdims=True)
            probs = (weights * (1.0 / total)).astype(BF16)
            mixed_ref[tile, :] = contract(probs, values_ref[...], 0, 0).astype(BF16)
            lse_ref[pl.ds(head, 1), tile] = top + jnp.log2(total)

    def fixed(shape):
        return pl.BlockSpec(shape, lambda h: (0,) * len(shape))

    by_head = pl.BlockSpec((rows, HEAD_SIZE), lambda h: (0, h))
    return pl.pallas_call(
        kernel,
        grid=(heads,),
        in_specs=[
            by_head,
            fixed(cosine.shape),
            fixed(sine.shape),
            fixed(key_place.shape),
            fixed(bounds.shape),
        ]
        + [fixed(p.shape) for p in key_value]
        + [pl.BlockSpec(memory_space=pl.ANY)] * len(waits),
        out_specs=[by_head, by_head, fixed((8, rows))],
        out_shape=[
            jax.ShapeDtypeStruct((rows, heads * HEAD_SIZE), BF16),
            jax.ShapeDtypeStruct((rows, heads * HEAD_SIZE), BF16),
            jax.ShapeDtypeStruct((8, rows), F32),
        ],
        scratch_shapes=[
            pltpu.VMEM((n_keys, HEAD_SIZE), BF16),
            pltpu.VMEM((n_keys, HEAD_SIZE), BF16),
            pltpu.VMEM((n_keys, rows), F32),
        ],
        compiler_params=kernel_params(),
        cost_estimate=SMALL,
        name="attention_forward",
    )(projected, cosine, sine, key_place, bounds, *key_value, *waits)


def attention_backward(
    query, head_gradient, lse, key_value, cosine, sine, key_place, bounds, heads
):
    rows = query.shape[0]
    n_keys = key_place.shape[0]
    n_parts = len(key_value)
    scale = HEAD_SIZE ** (-0.5)
    factor = scale * LOG2_E

    def kernel(query_ref, grad_ref, lse_ref, cos_ref, sin_ref, place_ref, bounds_ref, *refs):
        parts = refs[:n_parts]
        out_ref = refs[n_parts]
        part_outs = refs[n_parts + 1 : 2 * n_parts + 1]
        keys_ref, values_ref, bias_ref, grad_keys_ref, grad_values_ref = refs[2 * n_parts + 1 :]
        head = pl.program_id(0)

        @pl.when(head == 0)
        def _():
            fill_keys(parts, keys_ref, values_ref)
            fill_bias(place_ref, bounds_ref, bias_ref)
            grad_keys_ref[...] = jnp.zeros_like(grad_keys_ref)
            grad_values_ref[...] = jnp.zeros_like(grad_values_ref)

        for start in range(0, rows, ROW_TILE):
            tile = slice(start, start + ROW_TILE)
            query, grad = query_ref[tile, :], grad_ref[tile, :]
            scores = contract(keys_ref[...], query, 1, 1) * factor + bias_ref[:, tile]
            probs = jnp.exp2(scores - lse_ref[pl.ds(head, 1), tile])
            weighted = probs * contract(values_ref[...], grad, 1, 1)
            offset = jnp.sum(weighted, axis=0, keepdims=True)
            grad_scores = (weighted - probs * offset).astype(BF16)
            grad_keys_ref[...] += contract(grad_scores, query, 1, 0)
            grad_values_ref[...] += contract(probs.astype(BF16), grad, 1, 0)
            grad_query = contract(grad_scores, keys_ref[...], 0, 0) * scale
            out_ref[tile, :] = turned(grad_query, cos_ref[tile, :], -sin_ref[tile, :]).astype(BF16)

        @pl.when(head == heads - 1)
        def _():
            for i, out in enumerate(part_outs):
                n = out.shape[0]
                out[:, :HEAD_SIZE] = (grad_keys_ref[i * n : (i + 1) * n, :] * scale).astype(out.dtype)
                out[:, HEAD_SIZE:] = grad_values_ref[i * n : (i + 1) * n, :].astype(out.dtype)

    def fixed(shape):
        return pl.BlockSpec(shape, lambda h: (0,) * len(shape))

    by_head = pl.BlockSpec((rows, HEAD_SIZE), lambda h: (0, h))
    return pl.pallas_call(
        kernel,
        grid=(heads,),
        in_specs=[
            by_head,
            by_head,
            fixed(lse.shape),
            fixed(cosine.shape),
            fixed(sine.shape),
            fixed(key_place.shape),
            fixed(bounds.shape),
        ]
        + [fixed(p.shape) for p in key_value],
        out_specs=[by_head] + [fixed(p.shape) for p in key_value],
        out_shape=[jax.ShapeDtypeStruct((rows, heads * HEAD_SIZE), BF16)]
        + [
            jax.ShapeDtypeStruct(p.shape, F32 if i == 0 else BF16)
            for i, p in enumerate(key_value)
        ],
        scratch_shapes=[
            pltpu.VMEM((n_keys, HEAD_SIZE), BF16),
            pltpu.VMEM((n_keys, HEAD_SIZE), BF16),
            pltpu.VMEM((n_keys, rows), F32),
            pltpu.VMEM((n_keys, HEAD_SIZE), F32),
            pltpu.VMEM((n_keys, HEAD_SIZE), F32),
        ],
        compiler_params=kernel_params(),
        cost_estimate=SMALL,
        name="attention_backward",
    )(query, head_gradient, lse, cosine, sine, key_place, bounds, *key_value)


def expert_step(expert, chunk, cot, gate_up, down, router, index, n_steps, buffers):
    rows, width = chunk[0].shape
    units = down.shape[0]
    tile = min(256, units)
    steps = units // tile
    n_chunk = len(chunk)
    half_lanes = LANES // 2

    def kernel(expert_ref, *refs):
        chunk_refs, cot_refs = refs[:n_chunk], refs[n_chunk : 2 * n_chunk]
        gate_ref, up_ref, down_ref, router_ref = refs[2 * n_chunk : 2 * n_chunk + 4]
        refs = refs[2 * n_chunk + 4 + len(buffers) :]
        part_refs = refs[:n_chunk]
        rows_ref, cot_ref, gated_ref, grad_gate_ref, grad_up_ref = refs[n_chunk : n_chunk + 5]
        total_ref, weight_ref, share_ref = refs[n_chunk + 5 :]
        step = pl.program_id(0)
        lane = lax.broadcasted_iota(jnp.int32, (rows, LANES), 1)
        places = [slice(i * rows, (i + 1) * rows) for i in range(n_chunk)]

        @pl.when(step == 0)
        def _():
            for i, at in enumerate(places):
                rows_ref[at, :] = chunk_refs[i][...]
                cot_ref[at, :] = cot_refs[i][0, :, :width]
                logits = jnp.dot(chunk_refs[i][...], router_ref[...], preferred_element_type=F32)
                named = cot_refs[i][0, :, width:].astype(F32) > 0
                logits = jnp.where(named, logits, -jnp.inf)
                top = jnp.max(logits, axis=1, keepdims=True)
                weights = jnp.exp(logits - top)
                total = jnp.sum(weights, axis=1, keepdims=True)
                own = jnp.sum(
                    jnp.where(lane == expert_ref[0] + ROUTER_LANE, weights, 0.0), axis=1, keepdims=True
                )
                weight_ref[at, :] = jnp.broadcast_to(own / total, (rows, LANES))
                share_ref[at, :] = jnp.zeros((rows, LANES), F32)
                total_ref[at, :] = jnp.zeros((rows, width), F32)

        for i, at in enumerate(places):
            row = chunk_refs[i][...]
            weight = weight_ref[at, 0:1]
            gate = jnp.dot(row, gate_ref[...], preferred_element_type=F32)
            up = jnp.dot(row, up_ref[...], preferred_element_type=F32)
            grad_act = contract(cot_refs[i][0, :, :width], down_ref[...], 1, 1)
            square = gate * gate
            curve = jnp.tanh(GELU_ROOT * gate * (1.0 + GELU_CUBE * square))
            lifted = 0.5 + 0.5 * curve
            gelu = gate * lifted
            slope = lifted + (0.5 * GELU_ROOT) * gate * (1.0 - curve * curve) * (
                1.0 + (3.0 * GELU_CUBE) * square
            )
            act = gelu * up
            share_ref[at, :] += jnp.broadcast_to(
                jnp.sum(act * grad_act, axis=1, keepdims=True), (rows, LANES)
            )
            gated_ref[at, :] = (act * weight).astype(BF16)
            grad_act = grad_act * weight
            grad_up = (grad_act * gelu).astype(BF16)
            grad_gate = (grad_act * up * slope).astype(BF16)
            grad_gate_ref[at, :] = grad_gate
            grad_up_ref[at, :] = grad_up
            total_ref[at, :] += contract(grad_gate, gate_ref[...], 1, 1) + contract(
                grad_up, up_ref[...], 1, 1
            )

        @pl.when(step == steps - 1)
        def _():
            for i, at in enumerate(places):
                part_refs[i][:, :width] = total_ref[at, :].astype(BF16)
                share = share_ref[at, :]
                high = share.astype(BF16).astype(F32)
                part_refs[i][:, width:] = jnp.where(
                    lane == expert_ref[0],
                    high,
                    jnp.where(lane == expert_ref[0] + half_lanes, share - high, 0.0),
                ).astype(BF16)

    def fixed(shape):
        return pl.BlockSpec(shape, lambda j, scalars: (0,) * len(shape))

    n_rows = n_chunk * rows
    whole_rows = pl.BlockSpec((n_rows, width), lambda j, scalars: (index, 0))
    unit_tile = pl.BlockSpec((n_rows, tile), lambda j, scalars: (index, j))
    first_buffer = 1 + 2 * n_chunk + 4
    grid_spec = pltpu.PrefetchScalarGridSpec(
        num_scalar_prefetch=1,
        grid=(steps,),
        in_specs=[fixed(v.shape) for v in chunk]
        + [
            pl.BlockSpec((1, rows, width + LANES), lambda j, scalars: (scalars[1], 0, 0))
            for _ in cot
        ]
        + [
            pl.BlockSpec((width, tile), lambda j, scalars: (0, j)),
            pl.BlockSpec((width, tile), lambda j, scalars: (0, j + steps)),
            pl.BlockSpec((tile, width), lambda j, scalars: (j, 0)),
            fixed(router.shape),
        ]
        + [pl.BlockSpec(memory_space=pl.ANY)] * len(buffers),
        out_specs=[fixed((rows, width + LANES))] * n_chunk + [whole_rows] * 2 + [unit_tile] * 3,
        scratch_shapes=[
            pltpu.VMEM((n_rows, width), F32),
            pltpu.VMEM((n_rows, LANES), F32),
            pltpu.VMEM((n_rows, LANES), F32),
        ],
    )
    outs = pl.pallas_call(
        kernel,
        grid_spec=grid_spec,
        out_shape=[jax.ShapeDtypeStruct((rows, width + LANES), BF16)] * n_chunk
        + [jax.ShapeDtypeStruct((n_steps * n_rows, width), BF16)] * 2
        + [jax.ShapeDtypeStruct((n_steps * n_rows, units), BF16)] * 3,
        input_output_aliases={first_buffer + i: n_chunk + i for i in range(len(buffers))},
        compiler_params=kernel_params(),
        cost_estimate=SMALL,
        name="expert_step",
    )(expert, *chunk, *cot, gate_up, gate_up, down, router, *buffers)
    return outs[:n_chunk], outs[n_chunk:]


def gate_up_grads(rows, grad_gate, grad_up):
    n_rows, width = rows.shape
    units = grad_gate.shape[1]
    chunk, tile = n_rows // 4, 256

    def kernel(rows_ref, gate_ref, up_ref, gate_out, up_out, gate_sum, up_sum):
        step = pl.program_id(0)

        @pl.when(step == 0)
        def _():
            gate_sum[...] = jnp.zeros_like(gate_sum)
            up_sum[...] = jnp.zeros_like(up_sum)

        for right, total in ((gate_ref, gate_sum), (up_ref, up_sum)):
            for at in range(0, units, tile):
                total[:, at : at + tile] += contract(rows_ref[...], right[:, at : at + tile], 0, 0)

        @pl.when(step == 3)
        def _():
            gate_out[...] = gate_sum[...].astype(BF16)
            up_out[...] = up_sum[...].astype(BF16)

    def by_chunk(columns):
        return pl.BlockSpec((chunk, columns), lambda j: (j, 0))

    whole = pl.BlockSpec((width, units), lambda j: (0, 0))
    return pl.pallas_call(
        kernel,
        grid=(4,),
        in_specs=[by_chunk(width), by_chunk(units), by_chunk(units)],
        out_specs=[whole, whole],
        out_shape=[jax.ShapeDtypeStruct((width, units), BF16)] * 2,
        scratch_shapes=[pltpu.VMEM((width, units), F32)] * 2,
        compiler_params=kernel_params(),
        cost_estimate=SMALL,
        name="gate_up_grads",
    )(rows, grad_gate, grad_up)


def expert_weight_grads(gate_grad, up_grad, cot, gated):
    n_rows, width = cot.shape
    units = gated.shape[1]
    half = width // 2
    nx, ny = axis_len("dp"), axis_len("y")
    n_blocks = nx * ny
    gu_rows, down_rows = width // n_blocks, units // n_blocks
    n_out = 2 * n_blocks
    block_shape = (gu_rows + down_rows, half)
    chunk, tile = n_rows // 4, 256

    def kernel(place_ref, gate_ref, up_ref, cot_ref, gated_ref, *refs):
        outs, down_sum = refs[:n_out], refs[n_out]
        step = pl.program_id(0)

        @pl.when(step == 0)
        def _():
            down_sum[...] = jnp.zeros_like(down_sum)

        for at in range(0, width, tile):
            down_sum[:, at : at + tile] += contract(gated_ref[...], cot_ref[:, at : at + tile], 0, 0)

        def store(out, grad_ref, at, columns):
            out[:gu_rows, :] = grad_ref[at * gu_rows : (at + 1) * gu_rows, :]
            down = down_sum[at * down_rows : (at + 1) * down_rows, columns]
            out[gu_rows:, :] = down.astype(BF16)

        @pl.when(step == 3)
        def _():
            for at in range(n_blocks):
                x_step, y_step = step_to(place_ref, at)
                for s in range(nx):
                    for t in range(ny):

                        @pl.when((x_step == s) & (y_step == t))
                        def _(at=at, s=s, t=t):
                            store(outs[s * ny + t], gate_ref, at, slice(0, half))
                            store(outs[n_blocks + t * nx + s], up_ref, at, slice(half, width))

    def by_chunk(columns):
        return pl.BlockSpec((chunk, columns), lambda j, place: (j, 0))

    whole = pl.BlockSpec((width, units), lambda j, place: (0, 0))
    outs = pl.pallas_call(
        kernel,
        grid_spec=pltpu.PrefetchScalarGridSpec(
            num_scalar_prefetch=1,
            grid=(4,),
            in_specs=[whole, whole, by_chunk(width), by_chunk(units)],
            out_specs=[pl.BlockSpec(block_shape, lambda j, place: (0, 0))] * n_out,
            scratch_shapes=[pltpu.VMEM((units, width), F32)],
        ),
        out_shape=[jax.ShapeDtypeStruct(block_shape, BF16)] * n_out,
        compiler_params=kernel_params(),
        cost_estimate=SMALL,
        name="expert_weight_grads",
    )(plane_places(), gate_grad, up_grad, cot, gated)
    return [
        [outs[s * ny : (s + 1) * ny] for s in range(nx)],
        [outs[n_blocks + t * nx : n_blocks + (t + 1) * nx] for t in range(ny)],
    ]


def expert_results(gated, down):
    n_rows, units = gated.shape
    width = down.shape[1]
    half = n_rows // 8

    def kernel(gated_ref, down_ref, own_ref, other_ref):
        for i, out in enumerate((own_ref, other_ref)):
            rows = gated_ref[i * half : (i + 1) * half, :]
            out[...] = jnp.dot(rows, down_ref[...], preferred_element_type=F32).astype(BF16)

    out = pl.BlockSpec((half, width), lambda j: (2 * (1 - j % 2) + j // 2, 0))
    return pl.pallas_call(
        kernel,
        grid=(4,),
        in_specs=[
            pl.BlockSpec((2 * half, units), lambda j: (j, 0)),
            pl.BlockSpec(down.shape, lambda j: (0, 0)),
        ],
        out_specs=[out, out],
        out_shape=[jax.ShapeDtypeStruct((4 * half, width), BF16)] * 2,
        compiler_params=kernel_params(),
        cost_estimate=SMALL,
        name="expert_results",
    )(gated, down)


def branch_backward(grads, mixed, weight):
    rows, columns = mixed.shape
    width = weight.shape[0]
    half, chip_half = columns // 2, rows // 2
    block_rows = width // (axis_len("dp") * axis_len("y"))
    shapes = half_shapes([(block_rows, half)] * 2)
    n_out = len(shapes)
    together = blocks_a_step(block_rows)
    tile = together * block_rows
    n_tiles = width // tile

    def kernel(place_ref, own_ref, other_ref, mixed_ref, weight_ref, *refs):
        out_ref, outs, total_ref = refs[0], refs[1 : 1 + n_out], refs[1 + n_out]
        at = pl.program_id(0)
        both = jnp.concatenate([own_ref[...], other_ref[...]], axis=0)
        part = jnp.dot(both, weight_ref[...], preferred_element_type=F32)

        @pl.when(at == 0)
        def _():
            total_ref[...] = part

        @pl.when(at > 0)
        def _():
            total_ref[...] += part

        product = contract(both, mixed_ref[...], 0, 0).astype(BF16)
        for i in range(together):
            block = product[i * block_rows : (i + 1) * block_rows]

            def first(out, block=block):
                out[...] = block[:, :half]

            def second(out, block=block):
                out[...] = block[:, half:]

            store_blocks(place_ref, at * together + i, outs, first, second)

        @pl.when(at == n_tiles - 1)
        def _():
            out_ref[...] = total_ref[...].astype(BF16)

    def fixed(shape):
        return pl.BlockSpec(shape, lambda j, place: (0,) * len(shape))

    by_columns = pl.BlockSpec((chip_half, tile), lambda j, place: (0, j))
    outs = pl.pallas_call(
        kernel,
        grid_spec=pltpu.PrefetchScalarGridSpec(
            num_scalar_prefetch=1,
            grid=(n_tiles,),
            in_specs=[
                by_columns,
                by_columns,
                fixed(mixed.shape),
                pl.BlockSpec((tile, columns), lambda j, place: (j, 0)),
            ],
            out_specs=[fixed(mixed.shape)] + [fixed(shape) for shape in shapes],
            scratch_shapes=[pltpu.VMEM((rows, columns), F32)],
        ),
        out_shape=[jax.ShapeDtypeStruct((rows, columns), BF16)]
        + [jax.ShapeDtypeStruct(shape, BF16) for shape in shapes],
        compiler_params=kernel_params(),
        cost_estimate=SMALL,
        name="branch_backward",
    )(plane_places(), *grads, mixed, weight)
    return outs[0], two_halves(outs[1:])


def projection_backward(
    normed, units, weight, grad_query, grad_key_value, split, extra_rows, extra_columns
):
    rows, width = normed.shape
    own_query = grad_query.shape[1]
    columns = own_query + grad_key_value.shape[1]
    half = rows // 2
    block_rows = width // (axis_len("dp") * axis_len("y"))
    shapes = half_shapes([(block_rows, split), (block_rows, columns - split + LANES)])
    together = blocks_a_step(block_rows)
    tile = together * block_rows

    def kernel(
        place_ref, normed_ref, unit_ref, other_unit_ref, weight_ref, query_ref, key_value_ref, *refs
    ):
        extra_refs, column_ref = refs[: len(extra_rows)], refs[len(extra_rows)]
        own_ref, other_ref = refs[len(extra_rows) + 1 : len(extra_rows) + 3]
        outs = refs[len(extra_rows) + 3 :]
        at = pl.program_id(0)
        part = contract(query_ref[...], weight_ref[:, :own_query], 1, 1) + contract(
            key_value_ref[...], weight_ref[:, own_query:], 1, 1
        )
        own_ref[...] = part[:half]
        other_ref[...] = part[half:].astype(BF16)
        both_units = jnp.concatenate([unit_ref[...], other_unit_ref[...]], axis=0)
        terms = (part * both_units.astype(F32)).astype(BF16)
        first = (lax.broadcasted_iota(jnp.int32, (rows, LANES), 1) == 0).astype(F32).astype(BF16)
        extra = contract(terms, first, 0, 0)
        row = 0
        for extra_ref in extra_refs:
            n = extra_ref.shape[0]
            extra += contract(extra_ref[...], column_ref[row : row + n, :], 0, 0)
            row += n
        by_query = contract(normed_ref[...], query_ref[...], 0, 0).astype(BF16)
        by_key_value = contract(normed_ref[...], key_value_ref[...], 0, 0).astype(BF16)
        extra = extra.astype(BF16)
        for i in range(together):
            these = slice(i * block_rows, (i + 1) * block_rows)

            def first(out, these=these):
                out[...] = by_query[these, :split]

            def second(out, these=these):
                out[:, : own_query - split] = by_query[these, split:]
                out[:, own_query - split : columns - split] = by_key_value[these]
                out[:, columns - split :] = extra[these]

            store_blocks(place_ref, at * together + i, outs, first, second)

    def fixed(shape):
        return pl.BlockSpec(shape, lambda j, place: (0,) * len(shape))

    def by_columns(n):
        return pl.BlockSpec((n, tile), lambda j, place: (0, j))

    outs = pl.pallas_call(
        kernel,
        grid_spec=pltpu.PrefetchScalarGridSpec(
            num_scalar_prefetch=1,
            grid=(width // tile,),
            in_specs=[
                by_columns(rows),
                by_columns(half),
                by_columns(half),
                pl.BlockSpec((tile, columns), lambda j, place: (j, 0)),
                fixed(grad_query.shape),
                fixed(grad_key_value.shape),
            ]
            + [by_columns(r.shape[0]) for r in extra_rows]
            + [fixed(extra_columns.shape)],
            out_specs=[by_columns(half), by_columns(half)] + [fixed(shape) for shape in shapes],
        ),
        out_shape=[
            jax.ShapeDtypeStruct((half, width), F32),
            jax.ShapeDtypeStruct((half, width), BF16),
        ]
        + [jax.ShapeDtypeStruct(shape, BF16) for shape in shapes],
        compiler_params=kernel_params(),
        cost_estimate=SMALL,
        name="projection_backward",
    )(
        plane_places(),
        normed,
        *units,
        weight,
        grad_query,
        grad_key_value,
        *extra_rows,
        extra_columns,
    )
    return (
        outs[0],
        outs[1],
        two_halves(outs[2:]),
    )


def middle_backward(backs, gates, middle, gain, router, grad_out):
    rows, width = middle.shape
    half_lanes = LANES // 2
    arrays = jax.tree.leaves(backs)
    n_backs = len(arrays)
    sizes = [len(jax.tree.leaves(back)) for back in backs]

    def kernel(*refs):
        gate_ref, middle_ref, gain_ref, router_ref, out_ref = refs[n_backs : n_backs + 5]
        grad_ref, rounded_ref, terms_ref, logits_ref = refs[n_backs + 5 :]
        came, at = 0.0, 0
        for n in sizes:
            pieces = [r[...].astype(F32) for r in refs[at : at + n]]
            came = came + (jnp.concatenate(pieces, axis=0) if n > 1 else pieces[0])
            at += n
        shares = came[:, width:]
        lane = lax.broadcasted_iota(jnp.int32, (rows, LANES), 1)
        shares = shares + pltpu.roll(shares, half_lanes, 1)
        shares = jnp.where(lane < half_lanes, shares, 0.0)
        shares = pltpu.roll(shares, ROUTER_LANE, 1)
        gate = gate_ref[...]
        mean = jnp.sum(gate * shares, axis=1, keepdims=True)
        logits = (gate * (shares - mean)).astype(BF16)
        logits_ref[...] = logits
        grad = came[:, :width] + contract(logits, router_ref[...], 1, 1)
        value = middle_ref[...]
        root = lax.rsqrt(jnp.mean(value * value, axis=-1, keepdims=True) + EPS)
        unit = value * root
        scaled = grad * gain_ref[...]
        along_unit = jnp.mean(scaled * unit, axis=-1, keepdims=True)
        total = out_ref[...] + root * (scaled - unit * along_unit)
        grad_ref[...] = total
        rounded_ref[...] = total.astype(BF16)
        terms_ref[...] = (grad * unit).astype(BF16)

    vmem = pl.BlockSpec(memory_space=pltpu.VMEM)
    return pl.pallas_call(
        kernel,
        in_specs=[vmem] * (n_backs + 5),
        out_specs=[vmem] * 4,
        out_shape=[
            jax.ShapeDtypeStruct((rows, width), F32),
            jax.ShapeDtypeStruct((rows, width), BF16),
            jax.ShapeDtypeStruct((rows, width), BF16),
            jax.ShapeDtypeStruct((rows, LANES), BF16),
        ],
        compiler_params=pltpu.CompilerParams(vmem_limit_bytes=48 * 1024 * 1024),
        cost_estimate=SMALL,
        name="middle_backward",
    )(*arrays, gates, middle, gain, router, grad_out)


def on_device(
    hidden_in,
    lengths,
    order,
    routes,
    cotangent,
    attn_gain,
    qkv_weight,
    out_weight,
    ffn_gain,
    router_weight,
    gate_up_weight,
    down_weight,
):
    hidden = hidden_in[0]
    grad_out = cotangent[0]
    rows, width = hidden.shape
    n_experts = router_weight.shape[1]
    nx, ny, nz = axis_len("dp"), axis_len("y"), axis_len("exp")
    core = lax.axis_index("ctx") % CORES
    other_core = 1 - core
    shard = qkv_weight.shape[0]
    chip_rows = CORES * rows
    query_width = QUERY_HEADS * HEAD_SIZE
    heads = QUERY_HEADS // KEY_VALUE_HEADS
    own_query = heads * HEAD_SIZE
    own_width = own_query + 2 * HEAD_SIZE
    hidden_units = gate_up_weight.shape[2] // 2
    scale = HEAD_SIZE ** (-0.5)

    extra = jnp.concatenate([attn_gain[:, None], ffn_gain[:, None], router_weight], axis=1)
    extra = jnp.pad(extra, ((0, 0), (0, LANES - extra.shape[1])))
    split = 5 * HEAD_SIZE

    def gather_z(pair, *waits):
        blocks = line_gather(pair.reshape(CORES * shard, -1), nz, *waits)
        place = lax.axis_index("exp")
        whole = jnp.zeros((CORES, nz, shard, pair.shape[2]), BF16)
        for step, block in enumerate(blocks):
            at = jnp.bitwise_xor(place, step)
            whole = lax.dynamic_update_slice_in_dim(
                whole, block.reshape(CORES, 1, shard, -1), at, 1
            )
        return whole.reshape(CORES * nz * shard, -1)

    weights = jnp.concatenate([qkv_weight, extra, out_weight.T], axis=1)
    weights = in_core_order(weights, core_swap(weights))
    key_at = query_width + core * HEAD_SIZE
    value_at = key_at + KEY_VALUE_HEADS * HEAD_SIZE
    extra_at = qkv_weight.shape[1]
    out_at = extra_at + LANES + core * own_query
    weights = jnp.concatenate(
        [
            lax.dynamic_slice_in_dim(weights, core * own_query, own_query, 2),
            lax.dynamic_slice_in_dim(weights, key_at, HEAD_SIZE, 2),
            lax.dynamic_slice_in_dim(weights, value_at, HEAD_SIZE, 2),
            weights[:, :, extra_at : extra_at + LANES],
            lax.dynamic_slice_in_dim(weights, out_at, own_query, 2),
        ],
        axis=2,
    )
    def expert_rows(which):
        return (
            lax.dynamic_index_in_dim(gate_up_weight, which, 0, keepdims=False),
            lax.dynamic_index_in_dim(down_weight, which, 0, keepdims=False),
        )

    gu_mine, down_mine = expert_rows(core)
    gu_shard, down_shard = gu_mine.shape[0], down_mine.shape[0]
    received = core_swap(after(jnp.concatenate(expert_rows(other_core), axis=0), weights))
    gu_pair = in_core_order(gu_mine, received[:gu_shard]).reshape(CORES * gu_shard, -1)
    down_pair = in_core_order(down_mine, received[gu_shard:]).reshape(CORES * down_shard, -1)
    half_width = width // 2
    expert_halves = (
        jnp.concatenate([gu_pair[:, :hidden_units], down_pair[:, :half_width]], axis=0),
        jnp.concatenate([gu_pair[:, hidden_units:], down_pair[:, half_width:]], axis=0),
    )
    expert_first = plane_first(*expert_halves)

    weights_z = after(gather_z(weights), expert_first)
    block_rows = CORES * nz * shard
    half_query = own_query // 2
    group = 4 if nz % 4 == 0 else nz
    phased = group == nz
    qkv_z, out_z = weights_z[:, : own_width + LANES], weights_z[:, own_width + LANES :]
    qkv_halves = (qkv_z[:, :split], qkv_z[:, split:])
    out_halves = (out_z[:, :half_query], out_z[:, half_query:])

    expert_ids = jnp.arange(n_experts, dtype=jnp.int32)
    used = jnp.any(routes[0][:, :, None] == expert_ids[None, None, :], axis=1)
    marks = jnp.pad(
        used.astype(BF16), ((0, 0), (ROUTER_LANE, LANES - ROUTER_LANE - n_experts))
    )
    cot_rows = jnp.concatenate([grad_out.astype(BF16), marks], axis=1)
    cot_all = lax.all_gather(after(cot_rows, weights_z), "exp", axis=0, tiled=False)

    units = unit_rows(hidden, weights_z)
    units_other = core_swap(units)
    qkv_first, qkv_second = plane_first(*qkv_halves), plane_second(*qkv_halves)
    qkv_first, qkv_second, out_halves = after((qkv_first, qkv_second, out_halves), units_other)
    qkv_third = plane_third(qkv_first)
    w_all, extra_all = place_blocks(
        qkv_halves,
        (qkv_first, qkv_second, qkv_third),
        ((0, block_rows, 0, own_width), (0, block_rows, own_width, LANES)),
    )
    out_halves = after(out_halves, w_all)
    out_first, out_second = plane_first(*out_halves), plane_second(*out_halves)
    gain_one = extra_all[:, 0].astype(F32)
    gain_two = extra_all[:, 1].astype(F32)
    lanes = jnp.arange(LANES)
    is_router = (lanes >= ROUTER_LANE) & (lanes < ROUTER_LANE + n_experts)
    router_all = jnp.where(is_router[None, :], extra_all, 0)

    normed = jnp.concatenate([units, units_other], axis=0)
    normed = (normed.astype(F32) * gain_one).astype(BF16)
    packed_all, all_lengths = after((order[0], lengths[0]), weights_z)
    starts_all = doc_starts(packed_all, all_lengths)

    def own_first(values):
        y_place, y_rows = axis_place("y"), chip_rows
        parts = []
        for t in range(ny):
            at = lax.rem(y_place - t + ny, ny) * y_rows
            for which in (core, other_core):
                parts.append(lax.dynamic_slice_in_dim(values, at + which * rows, rows, 0))
        return jnp.concatenate(parts, axis=0)

    packed_keys, starts = own_first(packed_all), own_first(starts_all)[:chip_rows]
    packed = packed_keys[:chip_rows]
    cosine, sine = rotation_tables(packed - starts)
    bounds = jnp.concatenate(
        [starts[None, :], packed[None, :], jnp.zeros((6, chip_rows), jnp.int32)], axis=0
    )
    key_place = packed_keys[:, None]
    projected = dot(normed, w_all)
    key_value = jnp.concatenate(
        [
            rotate(projected[:, own_query : own_query + HEAD_SIZE], cosine, sine),
            projected[:, own_query + HEAD_SIZE : own_width],
        ],
        axis=1,
    ).astype(BF16)
    key_value = [key_value] + [shifted(key_value, "y", t) for t in range(1, ny)]
    out_first, expert_halves, projected, cot_all = after(
        (out_first, expert_halves, projected, cot_all), key_value, out_second
    )
    out_third = plane_third(out_first)
    cot_other = core_swap(cot_all)
    expert_second = plane_second(*expert_halves)
    query_rows, mixed, lse = attention_forward(
        projected, key_value, cosine, sine, key_place, bounds, heads
    )
    mixed, expert_first = after((mixed, expert_first), out_third, cot_other)
    expert_third = plane_third(after(expert_first, expert_second))
    (out_turned,) = place_blocks(
        out_halves, (out_first, out_second, out_third), ((0, block_rows, 0, own_query),)
    )
    middle = hidden + core_sum(dot_turned(mixed, out_turned))
    inner = norm_rows(middle, gain_two).astype(BF16)
    gate_up_all, down_all = place_blocks(
        expert_halves,
        (expert_first, expert_second, expert_third),
        (
            (0, CORES * gu_shard, 0, 2 * hidden_units),
            (CORES * gu_shard, CORES * down_shard, 0, width),
        ),
    )

    logits = jnp.where(marks > 0, dot(inner, extra_all), -jnp.inf)
    gates = jax.nn.softmax(logits, axis=-1)
    place_z = lax.axis_index("exp")
    own_expert = place_z * CORES + core

    def expert_group(inner_rows, from_place):
        buffers = []

        def run(index, chunk):
            scalars = jnp.stack([own_expert, jnp.bitwise_xor(from_place, index)])
            (mine, other), filled = expert_step(
                scalars.astype(jnp.int32),
                chunk,
                [cot_all, cot_other],
                gate_up_all,
                down_all,
                extra_all,
                index,
                4,
                buffers,
            )
            buffers[:] = filled
            return mine, other

        def joined(mine, other):
            return (mine.astype(F32) + other.astype(F32)).astype(BF16)

        rows_1, rows_2 = xor_shift(inner_rows, 1), xor_shift(inner_rows, 2)
        mine_0, other_0 = run(0, [inner_rows, core_swap(inner_rows)])

        rows_1, rows_2 = after((rows_1, rows_2), other_0)
        rows_3 = xor_shift(rows_2, 1)
        swapped = [core_swap(rows_1), core_swap(rows_2)]
        rows_1, other_1_rows, other_2_rows = after((rows_1, *swapped))
        other_0 = core_swap(other_0)
        mine_1, other_1 = run(1, [rows_1, other_1_rows])

        rows_2, rows_3, other_1 = after((rows_2, rows_3, other_1), other_0)
        other_3_rows = core_swap(rows_3)
        other_1 = core_swap(other_1)
        mine_2, other_2 = run(2, [rows_2, other_2_rows])

        rows_3, other_2, mine_1 = after((rows_3, other_2, mine_1), other_3_rows, other_1)
        other_2 = core_swap(other_2)
        back_1 = joined(mine_1, other_1)
        near = xor_shift(back_1, 1)
        rows_3 = after(rows_3, back_1)
        mine_3, other_3 = run(3, [rows_3, other_3_rows])

        mine_3, other_3 = after((mine_3, other_3), other_2, near)
        back_3 = joined(mine_3, core_swap(other_3))
        handed = xor_shift(back_3, 1)
        all_rows, all_cots, gated_all, grad_gates, grad_ups = after(buffers, back_3)
        if phased:
            grad_gate, grad_up = gate_up_grads(all_rows, grad_gates, grad_ups)
            grad_gate, grad_up, handed = after((grad_gate, grad_up, handed))
        mine_0, mine_2 = after((mine_0, mine_2), back_3)
        back_2 = joined(mine_2, other_2)
        (pair,) = line_pairs([None, None, back_2, None], [handed])
        if phased:
            grad_gate, gated_all, pair = after((grad_gate, gated_all, pair), gates)
        pieces = [pair[: rows // 2], pair[rows // 2 :]]
        moved, received = xor_shift(pieces[0], 2), []
        if phased:
            weight_grads = expert_weight_grads(grad_gate, grad_up, all_cots, gated_all)
            weight_grads, gated_all, moved, pieces = after((weight_grads, gated_all, moved, pieces))
            received = plane_moved_part(weight_grads, True)
        else:
            weight_grads = (
                dot_rows(all_rows, grad_gates),
                dot_rows(all_rows, grad_ups),
                dot_rows(gated_all, all_cots),
            )
        moved_more = xor_shift(pieces[1], 2)
        back_0 = joined(mine_0, other_0)
        outs, outs_other = expert_results(gated_all, down_all)
        outs, outs_other, moved_more, received, weight_grads = after(
            (outs, outs_other, moved_more, received, weight_grads), back_0
        )
        if phased:
            received = plane_joined(plane_moved_part(weight_grads, False), received)
        outs_other = core_swap(outs_other)
        outs = [
            (outs[half].astype(F32) + outs_other[half].astype(F32)).astype(BF16)
            for half in (slice(0, 2 * rows), slice(2 * rows, 4 * rows))
        ]
        return (back_0, near, (moved, moved_more)), outs, weight_grads, received

    if phased:
        backs, outs, expert_grads, expert_received = expert_group(inner, place_z)
    else:

        def visit(turn, state):
            inner_here, back, out, sums = state
            more_back, outs, more, _ = expert_group(
                inner_here, lax.rem(place_z + turn * group, nz)
            )
            back = back + more_back[0].astype(F32) + more_back[1].astype(F32)
            back = back + jnp.concatenate(more_back[2], axis=0).astype(F32)
            odd, even = (o.reshape(2, rows, width) for o in outs)
            out = out + line_scatter([even[0], odd[0], even[1], odd[1]])[0]
            sums = tuple(a + b for a, b in zip(sums, more))
            return (*(shifted(v, "exp", nz - group) for v in (inner_here, back, out)), sums)

        sums = (
            jnp.zeros((width, hidden_units), F32),
            jnp.zeros((width, hidden_units), F32),
            jnp.zeros((hidden_units, width), F32),
        )
        start = (jnp.zeros((rows, width + LANES), F32), jnp.zeros((rows, width), F32), sums)
        _, back, moe, sums = lax.fori_loop(0, nz // group, visit, (inner, *start))
        backs = (back,)
        gate, up, down = (w.astype(BF16) for w in sums)
        gate, up = (w.reshape(nx, ny, CORES * gu_shard, hidden_units) for w in (gate, up))
        down = down.reshape(nx, ny, CORES * down_shard, width)
        expert_grads = [
            plane_blocks([gate, down[..., :half_width]], PLANE_AXES[0]),
            plane_blocks([up, down[..., half_width:]], PLANE_AXES[1]),
        ]
        expert_received = plane_joined(
            plane_moved_part(expert_grads, False), plane_moved_part(expert_grads, True)
        )
    gu_block = CORES * gu_shard

    if phased:
        results_near, results_handed = (
            xor_shift(outs[0][low : low + rows], 1) for low in (0, rows)
        )

    grad_middle, grad_branch, ffn_terms, grad_logits = middle_backward(
        backs, gates, middle, gain_two[None, :], router_all, grad_out
    )
    grad_branch = [grad_branch, core_swap(grad_branch)]
    blended_gradient, out_grads = branch_backward(grad_branch, mixed, out_turned)
    if phased:
        blended_gradient, results_handed = after((blended_gradient, results_handed))
        pair = (outs[1][rows:].astype(F32) + results_handed.astype(F32)).astype(BF16)
        cuts = [0, rows // 128 * 48, rows // 128 * 80, rows]
        pieces = [pair[low:high] for low, high in zip(cuts, cuts[1:])]
        blended_gradient, pieces = after((blended_gradient, pieces))
        moe_far = [xor_shift(pieces[0], 2)]
    blended_gradient, out_grads, expert_received = after(
        (blended_gradient, out_grads, expert_received)
    )
    out_received = plane_moved(out_grads)
    grad_query, grad_kv_own, *grad_kv_parts = attention_backward(
        query_rows, blended_gradient, lse, key_value, cosine, sine, key_place, bounds, heads
    )

    if phased:
        grad_query, grad_kv_parts, pieces, results_near = after(
            (grad_query, grad_kv_parts, pieces, results_near), moe_far
        )
        moe_far.append(xor_shift(pieces[1], 2))
    grad_kv_parts, out_received = after((grad_kv_parts, out_received))
    grad_kv_parts = [shifted(part, "y", ny - t) for t, part in enumerate(grad_kv_parts, 1)]
    out_received = after(out_received, grad_query)
    if phased:
        grad_query, pieces = after((grad_query, pieces), moe_far, grad_kv_parts)
        moe_far.append(xor_shift(pieces[2], 2))
    out_handed = plane_handed(plane_hand_on(out_grads, out_received))

    for part in grad_kv_parts:
        grad_kv_own = grad_kv_own + part.astype(F32)
    grad_key_value = jnp.concatenate(
        [rotate(grad_kv_own[:, :HEAD_SIZE], cosine, -sine), grad_kv_own[:, HEAD_SIZE:]], axis=1
    ).astype(BF16)
    is_ffn = (lax.broadcasted_iota(jnp.int32, (rows, LANES), 1) == 1).astype(BF16)
    grad_normed, grad_normed_other, qkv_grads = projection_backward(
        normed,
        [units, units_other],
        w_all,
        grad_query,
        grad_key_value,
        split,
        [ffn_terms, inner],
        jnp.concatenate([is_ffn, grad_logits], axis=0),
    )
    if phased:
        qkv_grads, moe_far = after((qkv_grads, moe_far))
        moe = outs[1][:rows].astype(F32) + results_near.astype(F32)
        moe = moe + jnp.concatenate(moe_far, axis=0).astype(F32)
    qkv_grads, out_handed = after((qkv_grads, out_handed))

    def line_sum(first, second):
        summed = jnp.concatenate([first, second], axis=1).astype(BF16)
        summed = summed.reshape(CORES, nz, shard, -1)
        place = lax.axis_index("exp")
        return line_scatter(
            [
                lax.dynamic_index_in_dim(summed, jnp.bitwise_xor(place, step), 1, keepdims=False)
                for step in range(nz)
            ]
        )

    def of_core(value, which):
        return lax.dynamic_index_in_dim(value, which, 0, keepdims=False)

    qkv_received = plane_moved(qkv_grads)
    out_received, out_handed = after((out_received, out_handed), qkv_grads)
    out_sum, out_pairs = line_sum(*plane_sum(out_grads, out_received, out_handed))
    qkv_hand_on = plane_hand_on(qkv_grads, qkv_received)
    qkv_handed = plane_handed(qkv_hand_on)
    expert_hand_on = plane_hand_on(expert_grads, after(expert_received, qkv_grads))
    grad_normed_other, moe = after((grad_normed_other, moe), qkv_hand_on)
    grad_normed = grad_normed + core_swap(grad_normed_other).astype(F32)
    grad_hidden_norm, _ = norm_back(hidden, gain_one, grad_normed)
    grad_input = grad_middle + grad_hidden_norm
    output = middle + moe
    expert_handed = plane_handed(after(expert_hand_on, qkv_hand_on))
    qkv_sum, qkv_pairs = line_sum(*plane_sum(qkv_grads, qkv_received, qkv_handed))
    out_sum = after(out_sum, qkv_pairs)
    out_other = core_swap(of_core(out_sum, other_core).astype(BF16)).astype(F32)
    out_sum = in_core_order(of_core(out_sum, core), out_other)
    grad_out_proj = out_sum.swapaxes(0, 1).reshape(shard, query_width).T

    first_sum, second_sum = plane_sum(expert_grads, expert_received, expert_handed)
    gu_sum = jnp.concatenate([first_sum[:gu_block], second_sum[:gu_block]], axis=1)
    down_sum = jnp.concatenate([first_sum[gu_block:], second_sum[gu_block:]], axis=1)
    gu_sum = gu_sum.reshape(CORES, gu_shard, 2 * hidden_units)
    down_sum = down_sum.reshape(CORES, down_shard, width)
    received = core_swap(
        jnp.concatenate([of_core(gu_sum, other_core), of_core(down_sum, other_core)], 0).astype(BF16)
    ).astype(F32)
    grad_gate_up = in_core_order(of_core(gu_sum, core), received[:gu_shard])
    grad_down = in_core_order(of_core(down_sum, core), received[gu_shard:])

    qkv_other = core_swap(of_core(qkv_sum, other_core).astype(BF16)).astype(F32)
    qkv_mine = of_core(qkv_sum, core)
    extra_sum = qkv_mine[:, own_width:] + qkv_other[:, own_width:]
    pair = in_core_order(qkv_mine[:, :own_width], qkv_other[:, :own_width])
    key_at, value_at = own_query, own_query + HEAD_SIZE
    grad_qkv = jnp.concatenate(
        [
            pair[:, :, :key_at].swapaxes(0, 1).reshape(shard, -1),
            pair[:, :, key_at:value_at].swapaxes(0, 1).reshape(shard, -1),
            pair[:, :, value_at:].swapaxes(0, 1).reshape(shard, -1),
        ],
        axis=1,
    )
    return (
        output[None],
        grad_input[None],
        extra_sum[:, 0],
        grad_qkv,
        grad_out_proj,
        extra_sum[:, 1],
        extra_sum[:, 2 : 2 + n_experts],
        grad_gate_up,
        grad_down,
    )


def solution(mesh):
    return jax.shard_map(
        on_device,
        mesh=mesh,
        in_specs=(
            P(("dp", "exp"), "ctx", None),
            P(("dp", "exp"), None),
            P(("dp", "exp"), None),
            P(("dp", "exp"), "ctx", None),
            P(("dp", "exp"), "ctx", None),
            P(("dp", "ctx", "exp")),
            P(("dp", "ctx", "exp"), None),
            P(None, ("dp", "ctx", "exp")),
            P(("dp", "ctx", "exp")),
            P(("dp", "ctx", "exp"), None),
            P("exp", ("dp", "ctx"), None),
            P("exp", ("dp", "ctx"), None),
        ),
        out_specs=(
            P(("dp", "exp"), "ctx", None),
            P(("dp", "exp"), "ctx", None),
            P(("dp", "ctx", "exp")),
            P(("dp", "ctx", "exp"), None),
            P(None, ("dp", "ctx", "exp")),
            P(("dp", "ctx", "exp")),
            P(("dp", "ctx", "exp"), None),
            P("exp", ("dp", "ctx"), None),
            P("exp", ("dp", "ctx"), None),
        ),
        check_vma=False,
    )
```

time: 588 us -> 528 us (0.90)
  Pallas kernels: 8.97 us -> 172 us
  matrix products: 123 us -> 6.69 us
  waiting for transfers between devices: 189 us -> 126 us
  local copies, waits for them, and re-layouts: 112 us -> 67.8 us
  other arithmetic: 84.1 us -> 70.3 us
  between operations: 3.7 us -> 15.8 us
  starting transfers between devices: 58.2 us -> 64.2 us
    pallas_call x0 -> x48, Pallas kernels: none -> 160 us  [the longest x4 64.8 us: expert_step(): pl.pallas_call(kernel, grid_spec=grid_spec, out_shape=[jax.ShapeDtypeStru...]
    ppermute x24 -> x19, waiting for transfers between devices: 158 us -> 60 us  [xor_shift(): return lax.ppermute(value, 'exp', [(i, i ^ step) for i in range(n)])]
    dot_general x13 -> x0, matrix products: 58.6 us -> none  [the longest x7 26.1 us: dot_rows(): lax.dot_general(a, b, (((0,), (0,)), ((), ())), preferred_element_type=F32)]
    dot_general x12 -> x2, matrix products: 36.5 us -> 3.36 us  [dot(): return jnp.dot(a, b, preferred_element_type=F32)]
    ppermute x26 -> x34, waiting for transfers between devices: 29.2 us -> 59 us  [shifted(): lax.ppermute(value, name, [(i, (i + step * stride) % n) for i in range(n)])]
    dot_general x11 -> x1, matrix products: 27.8 us -> 3.33 us  [dot_turned(): lax.dot_general(a, b, (((1,), (1,)), ((), ())), preferred_element_type=F32)]
    dynamic_slice x4 -> x0, local copies, waits for them, and re-layouts: 9.27 us -> none  [the longest x1 5.92 us: take_block(): lax.dynamic_index_in_dim(part, place, dim, keepdims=False)]
    squeeze x13 -> x0, local copies, waits for them, and re-layouts: 8.09 us -> none  [take_block(): lax.dynamic_index_in_dim(part, place, dim, keepdims=False)]
  transfers between devices with their start and end apart: 73 -> 73, of which waited for: 27 -> 24; matrix products, arithmetic and copies ran while one was open for 51% -> 16% of each run, Pallas kernels for 2% -> 33%
where the time goes in v2:
time: 528 us; the launch traced here: 523 us
  Pallas kernels  172 us (33%)
  waiting for transfers between devices  126 us (24%)
  other arithmetic  70.3 us (13%)
  local copies, waits for them, and re-layouts  67.8 us (13%)
  starting transfers between devices  64.2 us (12%)
  between operations  15.8 us (3%)
  matrix products  6.69 us (1%)
    pallas_call x4, Pallas kernels, expert_step(): pl.pallas_call(kernel, grid_spec=grid_spec, out_shape=[jax.ShapeDtypeStru...  64.8 us
    ppermute x19, waiting for transfers between devices, xor_shift(): return lax.ppermute(value, 'exp', [(i, i ^ step) for i in range(n)])  60 us
    ppermute x34, waiting for transfers between devices, shifted(): lax.ppermute(value, name, [(i, (i + step * stride) % n) for i in range(n)])  59 us
    unnamed x245, local copies, waits for them, and re-layouts  47.9 us
    ppermute x34, starting transfers between devices, shifted(): lax.ppermute(value, name, [(i, (i + step * stride) % n) for i in range(n)])  35.9 us
    ppermute x19, starting transfers between devices, xor_shift(): return lax.ppermute(value, 'exp', [(i, i ^ step) for i in range(n)])  25.7 us
    pallas_call x1, Pallas kernels, gate_up_grads(): pl.pallas_call(kernel, grid=(4,), in_specs=[by_chunk(width), by_chunk(uni...  15.8 us
    pallas_call x1, Pallas kernels, attention_forward(): pl.pallas_call(kernel, grid=(heads,), in_specs=[by_head, fixed(cosine.sha...  15.6 us
  transfers between devices with their start and end apart: 73, of which 24 were waited for; matrix products, arithmetic and copies ran while one was open for 16% of the time, Pallas kernels for 33%

profile of v2, /device:TPU:0, one launch (start us, length us, event | category | flops | bytes accessed | tf_op | source)
XLA Modules:
  0.0 522.6 jit_solution(15472167310679320360)
XLA Ops:
  29.0 13.0 %collective-permute-done.2 = bf16[96,1920]{1,0:T(8,128)(2,1)S(1)} collective-permute-done((bf16[96,1920]{1,0:T(8,128)(2,1)S(1)}, bf16[96,1920]{1,0:T(8,128)(2,1)S(1)}, u32[]{:S(2)}, u32[]{:S(2)}) %collective-permute-start.2) | collective-permute-done | bytes 368672 | tf_op jit(solution)/shard_map/ppermute | solution.py:205
  42.6 8.3 %collective-permute-done.3 = bf16[96,1920]{1,0:T(8,128)(2,1)S(1)} collective-permute-done((bf16[96,1920]{1,0:T(8,128)(2,1)S(1)}, bf16[96,1920]{1,0:T(8,128)(2,1)S(1)}, u32[]{:S(2)}, u32[]{:S(2)}) %collective-permute-start.3) | collective-permute-done | bytes 368672 | tf_op jit(solution)/shard_map/ppermute | solution.py:205
  64.1 15.8 %collective-permute-done.8.refs_1_ = bf16[384,512]{1,0:T(8,128)(2,1)S(1)} collective-permute-done((bf16[384,512]{1,0:T(8,128)(2,1)}, bf16[384,512]{1,0:T(8,128)(2,1)S(1)}, u32[]{:S(2)}, u32[]{:S(2)}) %collective-permute-start.8) | collective-permute-done | bytes 393248 | tf_op jit(solution)/shard_map/ppermute | solution.py:102
  85.2 7.8 %collective-permute-done.13.refs_7_ = bf16[384,512]{1,0:T(8,128)(2,1)S(1)} collective-permute-done((bf16[384,512]{1,0:T(8,128)(2,1)}, bf16[384,512]{1,0:T(8,128)(2,1)S(1)}, u32[]{:S(2)}, u32[]{:S(2)}) %collective-permute-start.13) | collective-permute-done | bytes 393248 | tf_op jit(solution)/shard_map/ppermute | solution.py:102
  96.8 4.2 place_blocks.3
  112.8 8.3 %collective-permute-done.16.refs_7_.refs_1_ = bf16[512,256]{1,0:T(8,128)(2,1)S(1)} collective-permute-done((bf16[512,256]{1,0:T(8,128)(2,1)S(1)}, bf16[512,256]{1,0:T(8,128)(2,1)S(1)}, u32[]{:S(2)}, u32[]{:S(2)}) %collective-permute-start.16) | collective-permute-done | bytes 262176 | tf_op jit(solution)/shard_map/ppermute | solution.py:102
  128.0 15.6 %attention_forward.1 = (bf16[512,768]{1,0:T(8,128)(2,1)}, bf16[512,768]{1,0:T(8,128)(2,1)}, f32[8,512]{1,0:T(8,128)}) custom-call(f32[512,1024]{1,0:T(8,128)} %get-tuple-element.206.projected_ref, f32[512,128]{1,0:T(8,128)} %get-tuple-element.452.cos_ref, f32[512,128]{1,0:T(8,128)} %get-tuple-element.422.sin_ref, s32[1024,1]{1,0:T(8,128)} %copy.212.place_ref, ...), custom_call_target="tpu_custom_call" | custom-call | flops 1 | bytes 1 | tf_op jit(solution)/shard_map/attention_forward/pallas_call | solution.py:442
  147.1 3.3 fusion.59
  167.0 9.5 %collective-permute-done.26.refs_3_ = bf16[576,768]{1,0:T(8,128)(2,1)} collective-permute-done((bf16[576,768]{1,0:T(8,128)(2,1)}, bf16[576,768]{1,0:T(8,128)(2,1)}, u32[]{:S(2)}, u32[]{:S(2)}) %collective-permute-start.26) | collective-permute-done | bytes 884768 | tf_op jit(solution)/shard_map/ppermute | solution.py:102
  181.3 5.5 %place_blocks.5 = (bf16[1536,1536]{1,0:T(8,128)(2,1)}, bf16[768,1536]{1,0:T(8,128)(2,1)}) custom-call(s32[2]{0:T(128)S(1)} %pad_add_fusion.3.place_ref, bf16[576,768]{1,0:T(8,128)(2,1)S(1)} %copy-done.12, bf16[576,768]{1,0:T(8,128)(2,1)S(1)} %copy-done.19, bf16[576,768]{1,0:T(8,128)(2,1)S(1)} %copy-done.6, bf16[576,768]{1,0:T(8,128)(2,1)} %collective-permute-done.26.refs_3_, ...), custom_call_target="tpu_custom_call" | custom-call | flops 1 | bytes 1 | tf_op jit(solution)/shard_map/place_blocks/pallas_call | solution.py:182
  186.8 16.5 %expert_step.4 = (bf16[256,1664]{1,0:T(8,128)(2,1)}, bf16[256,1664]{1,0:T(8,128)(2,1)}, bf16[2048,1536]{1,0:T(8,128)(2,1)}, bf16[2048,1536]{1,0:T(8,128)(2,1)}, ...) custom-call(s32[2]{0:T(128)} %pad_add_fusion.4.expert_ref, ...), custom_call_target="tpu_custom_call" | custom-call | flops 1 | bytes 1 | tf_op jit(solution)/shard_map/expert_step/pallas_call | solution.py:655
  208.3 16.0 %expert_step.5 = (bf16[256,1664]{1,0:T(8,128)(2,1)}, bf16[256,1664]{1,0:T(8,128)(2,1)}, bf16[2048,1536]{1,0:T(8,128)(2,1)}, bf16[2048,1536]{1,0:T(8,128)(2,1)}, ...) custom-call(s32[2]{0:T(128)} %pad_add_fusion.6.expert_ref, ...), custom_call_target="tpu_custom_call", output_to_operand_aliasing={{2}: (9, {}), {3}: (10, {}), {4}: (11, {}), {5}: (12, {}), ... | custom-call | flops 1 | bytes 1 | tf_op jit(solution)/shard_map/expert_step/pallas_call | solution.py:655
  226.6 16.0 %expert_step.6 = (bf16[256,1664]{1,0:T(8,128)(2,1)}, bf16[256,1664]{1,0:T(8,128)(2,1)}, bf16[2048,1536]{1,0:T(8,128)(2,1)}, bf16[2048,1536]{1,0:T(8,128)(2,1)}, ...) custom-call(s32[2]{0:T(128)} %pad_add_fusion.5.expert_ref, ...), custom_call_target="tpu_custom_call", output_to_operand_aliasing={{2}: (9, {}), {3}: (10, {}), {4}: (11, {}), {5}: (12, {}), ... | custom-call | flops 1 | bytes 1 | tf_op jit(solution)/shard_map/expert_step/pallas_call | solution.py:655
  247.6 16.4 %expert_step.7 = (bf16[256,1664]{1,0:T(8,128)(2,1)}, bf16[256,1664]{1,0:T(8,128)(2,1)}, bf16[2048,1536]{1,0:T(8,128)(2,1)}, bf16[2048,1536]{1,0:T(8,128)(2,1)}, ...) custom-call(s32[2]{0:T(128)} %pad_add_fusion.7.expert_ref, ...), custom_call_target="tpu_custom_call", output_to_operand_aliasing={{2}: (9, {}), {3}: (10, {}), {4}: (11, {}), {5}: (12, {}), ... | custom-call | flops 1 | bytes 1 | tf_op jit(solution)/shard_map/expert_step/pallas_call | solution.py:655
  264.0 2.8 collective-permute-done.37.refs_3_.refs_1_
  275.8 15.8 %gate_up_grads.1 = (bf16[1536,768]{1,0:T(8,128)(2,1)}, bf16[1536,768]{1,0:T(8,128)(2,1)}) custom-call(bf16[2048,1536]{1,0:T(8,128)(2,1)} %get-tuple-element.263.rows_ref, bf16[2048,768]{1,0:T(8,128)(2,1)} %get-tuple-element.264.gate_ref, bf16[2048,768]{1,0:T(8,128)(2,1)} %get-tuple-element.265.up_ref), custom_call_target="tpu_custom_call" | custom-call | flops 1 | bytes 1 | tf_op jit(solution)/shard_map/gate_up_grads/pallas_call | solution.py:695
  300.9 13.8 %expert_weight_grads.1 = (bf16[576,768]{1,0:T(8,128)(2,1)}, bf16[576,768]{1,0:T(8,128)(2,1)}, bf16[576,768]{1,0:T(8,128)(2,1)}, bf16[576,768]{1,0:T(8,128)(2,1)}...) custom-call(s32[2]{0:T(128)} %copy-done.43, ...), custom_call_target="tpu_custom_call" | custom-call | flops 1 | bytes 1 | tf_op jit(solution)/shard_map/expert_weight_grads/pallas_call | solution.py:751
  314.7 4.9 collective-permute-done.40.refs_9_
  324.7 8.5 %expert_results.1 = (bf16[1024,1536]{1,0:T(8,128)(2,1)}, bf16[1024,1536]{1,0:T(8,128)(2,1)}) custom-call(bf16[2048,768]{1,0:T(8,128)(2,1)} %get-tuple-element.286.gated_ref, bf16[768,1536]{1,0:T(8,128)(2,1)} %get-tuple-element.220.refs_6_.down_ref), custom_call_target="tpu_custom_call" | custom-call | flops 1 | bytes 1 | tf_op jit(solution)/shard_map/expert_results/pallas_call | solution.py:782
  333.1 9.8 %collective-permute-done.41.refs_2_ = bf16[128,1664]{1,0:T(8,128)(2,1)S(1)} collective-permute-done((bf16[128,1664]{1,0:T(8,128)(2,1)}, bf16[128,1664]{1,0:T(8,128)(2,1)S(1)}, u32[]{:S(2)}, u32[]{:S(2)}) %collective-permute-start.41) | collective-permute-done | bytes 426016 | tf_op jit(solution)/shard_map/ppermute | solution.py:205
  348.6 4.5 middle_backward.1
  359.2 10.0 %branch_backward.1 = (bf16[512,768]{1,0:T(8,128)(2,1)}, bf16[2,384,384]{2,1,0:T(8,128)(2,1)}, bf16[2,384,384]{2,1,0:T(8,128)(2,1)}, bf16[2,384,384]{2,1,0:T(8,128)(2,1)}, bf16[2,384,384]{2,1,0:T(8,128)(2,1)}) custom-call(s32[2]{0:T(128)} %copy-done.43, bf16[256,1536]{1,0:T(8,128)(2,1)} %copy-done.42, bf16[256,1536]{1,0:T(8,128)(2,1)} %copy-done.106, ...), custom_call_target="tpu_custom_call" | custom-call | flops 1 | bytes 1 | tf_op jit(solution)/shard_map/branch_backward/pallas_call | solution.py:842
  371.2 5.5 %collective-permute-done.46.refs_1_ = bf16[256,1536]{1,0:T(8,128)(2,1)} collective-permute-done((bf16[256,1536]{1,0:T(8,128)(2,1)S(1)}, bf16[256,1536]{1,0:T(8,128)(2,1)}, u32[]{:S(2)}, u32[]{:S(2)}) %collective-permute-start.46) | collective-permute-done | bytes 786464 | tf_op jit(solution)/shard_map/ppermute | solution.py:205
  385.9 14.9 %attention_backward.1 = (bf16[512,768]{1,0:T(8,128)(2,1)}, f32[512,256]{1,0:T(8,128)}, bf16[512,256]{1,0:T(8,128)(2,1)}) custom-call(bf16[512,768]{1,0:T(8,128)(2,1)} %get-tuple-element.212.query_ref, bf16[512,768]{1,0:T(8,128)(2,1)} %get-tuple-element.314.grad_ref, f32[8,512]{1,0:T(8,128)} %get-tuple-element.315.lse_ref, ...), custom_call_target="tpu_custom_call" | custom-call | flops 1 | bytes 1 | tf_op jit(solution)/shard_map/attention_backward/pallas_call | solution.py:518
  420.2 11.0 %projection_backward.1 = (f32[256,1536]{1,0:T(8,128)}, bf16[256,1536]{1,0:T(8,128)(2,1)}, bf16[2,384,640]{2,1,0:T(8,128)(2,1)}, bf16[2,384,640]{2,1,0:T(8,128)(2...) custom-call(s32[2]{0:T(128)} %copy-done.43, bf16[512,1536]{1,0:T(8,128)(2,1)} %copy-done.71, ...), custom_call_target="tpu_custom_call" | custom-call | flops 1 | bytes 1 | tf_op jit(solution)/shard_map/projection_backward/pallas_call | solution.py:920
  439.7 2.7 convert_add_fusion.2.refs_1_
  448.4 6.2 %collective-permute-done.67 = bf16[2,48,768]{2,1,0:T(8,128)(2,1)S(1)} collective-permute-done((bf16[2,48,768]{2,1,0:T(8,128)(2,1)S(1)}, bf16[2,48,768]{2,1,0:T(8,128)(2,1)S(1)}, u32[]{:S(2)}, u32[]{:S(2)}) %collective-permute-start.67) | collective-permute-done | bytes 147488 | tf_op jit(solution)/shard_map/ppermute | solution.py:205
  462.8 2.7 add_bitcast_fusion.1
  468.3 3.3 collective-permute-done.61
  474.8 2.9 add_bitcast_fusion
  477.8 10.0 %collective-permute-done.70 = bf16[576,768]{1,0:T(8,128)(2,1)S(1)} collective-permute-done((bf16[576,768]{1,0:T(8,128)(2,1)}, bf16[576,768]{1,0:T(8,128)(2,1)S(1)}, u32[]{:S(2)}, u32[]{:S(2)}) %collective-permute-start.70) | collective-permute-done | bytes 884768 | tf_op jit(solution)/shard_map/ppermute | solution.py:102
  499.2 8.2 %collective-permute-done.64 = bf16[2,48,1152]{2,1,0:T(8,128)(2,1)S(1)} collective-permute-done((bf16[2,48,1152]{2,1,0:T(8,128)(2,1)S(1)}, bf16[2,48,1152]{2,1,0:T(8,128)(2,1)S(1)}, u32[]{:S(2)}, u32[]{:S(2)}) %collective-permute-start.64) | collective-permute-done | bytes 221216 | tf_op jit(solution)/shard_map/ppermute | solution.py:205
  (555 shorter events, 213.1 us)
Async XLA Ops:
  7.2 114.6 %all-gather.3.cloned.1.call-start = ((), (), s32[]{:S(2)}) async-start(), calls=%async_computation | async-start | bytes 4259840 | tf_op jit(solution)/shard_map/all_gather | solution.py:1108
  19.9 22.6 %collective-permute-start.1 = (bf16[96,1920]{1,0:T(8,128)(2,1)S(1)}, bf16[96,1920]{1,0:T(8,128)(2,1)S(1)}, u32[]{:S(2)}, u32[]{:S(2)}) collective-permute-start(bf16[96,1920]{1,0:T(8,128)(2,1)S(1)} %bitcast.218), channel_id=1, source_target_pairs={{0,1},{1,0},{2,3},{3,2},{4,5},{5,4},{6,7},{7,6},{8,9},{9,8},{10,11... | collective-permute-start | bytes 1105928 | tf_op jit(solution)/shard_map/ppermute | solution.py:205
  25.6 25.3 %collective-permute-start.5 = (bf16[576,768]{1,0:T(8,128)(2,1)S(1)}, bf16[576,768]{1,0:T(8,128)(2,1)S(1)}, u32[]{:S(2)}, u32[]{:S(2)}) collective-permute-start(bf16[576,768]{1,0:T(8,128)(2,1)S(1)} %pad_maximum_fusion.3.refs_2_), channel_id=1, source_target_pairs={{0,16},{16,0},{1,17},{17,1},{2,18},{18,2},{3,19},{19,3},{4,20},{20... | collective-permute-start | bytes 2654216 | tf_op jit(solution)/shard_map/ppermute | solution.py:102
  27.3 23.7 %collective-permute-start.6 = (bf16[576,768]{1,0:T(8,128)(2,1)S(1)}, bf16[576,768]{1,0:T(8,128)(2,1)S(1)}, u32[]{:S(2)}, u32[]{:S(2)}) collective-permute-start(bf16[576,768]{1,0:T(8,128)(2,1)S(1)} %pad_maximum_fusion.4.refs_3_), channel_id=1, source_target_pairs={{0,8},{4,12},{8,0},{12,4},{1,9},{5,13},{9,1},{13,5},{2,10},{6,14},... | collective-permute-start | bytes 2654216 | tf_op jit(solution)/shard_map/ppermute | solution.py:102
  55.6 24.3 %collective-permute-start.11 = (bf16[256,1536]{1,0:T(8,128)(2,1)}, bf16[256,1536]{1,0:T(8,128)(2,1)}, u32[]{:S(2)}, u32[]{:S(2)}) collective-permute-start(bf16[256,1536]{1,0:T(8,128)(2,1)} %unit_rows.1.unit_ref), channel_id=1, source_target_pairs={{0,4},{4,0},{8,12},{12,8},{1,5},{5,1},{9,13},{13,9},{2,6},{6,2},{1... | collective-permute-start | bytes 2359304 | tf_op jit(solution)/shard_map/ppermute | solution.py:107
  56.4 23.5 %collective-permute-start.7 = (bf16[384,640]{1,0:T(8,128)(2,1)}, bf16[384,640]{1,0:T(8,128)(2,1)S(1)}, u32[]{:S(2)}, u32[]{:S(2)}) collective-permute-start(bf16[384,640]{1,0:T(8,128)(2,1)} %slice.310.refs_0_), channel_id=1, source_target_pairs={{0,16},{16,0},{1,17},{17,1},{2,18},{18,2},{3,19},{19,3},{4,20},{20... | collective-permute-start | bytes 1474568 | tf_op jit(solution)/shard_map/ppermute | solution.py:102
  57.9 22.0 %collective-permute-start.9 = (bf16[384,640]{1,0:T(8,128)(2,1)}, bf16[384,640]{1,0:T(8,128)(2,1)}, u32[]{:S(2)}, u32[]{:S(2)}) collective-permute-start(bf16[384,640]{1,0:T(8,128)(2,1)} %slice.310.refs_0_), channel_id=1, source_target_pairs={{0,8},{4,12},{8,0},{12,4},{1,9},{5,13},{9,1},{13,5},{2,10},{6,14},... | collective-permute-start | bytes 1474568 | tf_op jit(solution)/shard_map/ppermute | solution.py:102
  122.1 24.9 %collective-permute-start.21 = (bf16[4,256,1664]{2,1,0:T(8,128)(2,1)}, bf16[4,256,1664]{2,1,0:T(8,128)(2,1)}, u32[]{:S(2)}, u32[]{:S(2)}) collective-permute-start(bf16[4,256,1664]{2,1,0:T(8,128)(2,1)} %get-tuple-element.210.refs_2_), channel_id=1, source_target_pairs={{0,4},{4,0},{8,12},{12,8},{1,5},{5,1},{9,13},{13,9},{2,6},{6,2},{1... | collective-permute-start | bytes 10223624 | tf_op jit(solution)/shard_map/ppermute | solution.py:107
  122.2 21.4 %collective-permute-start.19 = (bf16[384,384]{1,0:T(8,128)(2,1)}, bf16[384,384]{1,0:T(8,128)(2,1)}, u32[]{:S(2)}, u32[]{:S(2)}) collective-permute-start(bf16[384,384]{1,0:T(8,128)(2,1)} %get-tuple-element.208.refs_2_), channel_id=1, source_target_pairs={{0,8},{4,12},{8,0},{12,4},{1,9},{5,13},{9,1},{13,5},{2,10},{6,14},... | collective-permute-start | bytes 884744 | tf_op jit(solution)/shard_map/ppermute | solution.py:102
  126.9 27.2 %collective-permute-start.24 = (bf16[576,768]{1,0:T(8,128)(2,1)}, bf16[576,768]{1,0:T(8,128)(2,1)S(1)}, u32[]{:S(2)}, u32[]{:S(2)}) collective-permute-start(bf16[576,768]{1,0:T(8,128)(2,1)} %get-tuple-element.213.refs_0_), channel_id=1, source_target_pairs={{0,8},{4,12},{8,0},{12,4},{1,9},{5,13},{9,1},{13,5},{2,10},{6,14},... | collective-permute-start | bytes 2654216 | tf_op jit(solution)/shard_map/ppermute | solution.py:102
  127.4 26.7 %collective-permute-start.25 = (bf16[576,768]{1,0:T(8,128)(2,1)}, bf16[576,768]{1,0:T(8,128)(2,1)}, u32[]{:S(2)}, u32[]{:S(2)}) collective-permute-start(bf16[576,768]{1,0:T(8,128)(2,1)} %get-tuple-element.216.refs_4_), channel_id=1, source_target_pairs={{0,16},{16,0},{1,17},{17,1},{2,18},{18,2},{3,19},{19,3},{4,20},{20... | collective-permute-start | bytes 2654216 | tf_op jit(solution)/shard_map/ppermute | solution.py:102
  155.0 21.5 %collective-permute-start.26 = (bf16[576,768]{1,0:T(8,128)(2,1)}, bf16[576,768]{1,0:T(8,128)(2,1)}, u32[]{:S(2)}, u32[]{:S(2)}) collective-permute-start(bf16[576,768]{1,0:T(8,128)(2,1)} %get-tuple-element.217), channel_id=1, source_target_pairs={{0,8},{4,12},{8,0},{12,4},{1,9},{5,13},{9,1},{13,5},{2,10},{6,14},... | collective-permute-start | bytes 2654216 | tf_op jit(solution)/shard_map/ppermute | solution.py:102
  156.6 21.3 %collective-permute-start.27 = (bf16[576,768]{1,0:T(8,128)(2,1)}, bf16[576,768]{1,0:T(8,128)(2,1)}, u32[]{:S(2)}, u32[]{:S(2)}) collective-permute-start(bf16[576,768]{1,0:T(8,128)(2,1)} %get-tuple-element.218), channel_id=1, source_target_pairs={{0,16},{16,0},{1,17},{17,1},{2,18},{18,2},{3,19},{19,3},{4,20},{20... | collective-permute-start | bytes 2654216 | tf_op jit(solution)/shard_map/ppermute | solution.py:102
  162.4 24.5 %collective-permute-start.23 = (bf16[256,1536]{1,0:T(8,128)(2,1)}, bf16[256,1536]{1,0:T(8,128)(2,1)}, u32[]{:S(2)}, u32[]{:S(2)}) collective-permute-start(bf16[256,1536]{1,0:T(8,128)(2,1)} %multiply_convert_fusion.1.refs_0_.refs_1_), channel_id=1, source_target_pairs={{0,4},{4,0},{8,12},{12,8},{1,5},{5,1},{9,13},{13,9},{2,6},{6,2},{1... | collective-permute-start | bytes 2359304 | tf_op jit(solution)/shard_map/ppermute | solution.py:107
  162.4 41.0 %collective-permute-start.28 = (bf16[256,1536]{1,0:T(8,128)(2,1)}, bf16[256,1536]{1,0:T(8,128)(2,1)}, u32[]{:S(2)}, u32[]{:S(2)}) collective-permute-start(bf16[256,1536]{1,0:T(8,128)(2,1)} %multiply_convert_fusion.1.refs_0_.refs_1_), channel_id=1, source_target_pairs={{0,1},{1,0},{2,3},{3,2},{4,5},{5,4},{6,7},{7,6},{8,9},{9,8},{10,11... | collective-permute-start | bytes 2359304 | tf_op jit(solution)/shard_map/ppermute | solution.py:205
  163.8 39.6 %collective-permute-start.29 = (bf16[256,1536]{1,0:T(8,128)(2,1)}, bf16[256,1536]{1,0:T(8,128)(2,1)}, u32[]{:S(2)}, u32[]{:S(2)}) collective-permute-start(bf16[256,1536]{1,0:T(8,128)(2,1)} %multiply_convert_fusion.1.refs_0_.refs_1_), channel_id=1, source_target_pairs={{0,2},{1,3},{2,0},{3,1},{4,6},{5,7},{6,4},{7,5},{8,10},{9,11},{10,... | collective-permute-start | bytes 2359304 | tf_op jit(solution)/shard_map/ppermute | solution.py:205
  245.5 21.3 %collective-permute-start.37 = (bf16[256,1664]{1,0:T(8,128)(2,1)S(1)}, bf16[256,1664]{1,0:T(8,128)(2,1)S(1)}, u32[]{:S(2)}, u32[]{:S(2)}) collective-permute-start(bf16[256,1664]{1,0:T(8,128)(2,1)S(1)} %add_convert_fusion.8.refs_1_), channel_id=1, source_target_pairs={{0,1},{1,0},{2,3},{3,2},{4,5},{5,4},{6,7},{7,6},{8,9},{9,8},{10,11... | collective-permute-start | bytes 2555912 | tf_op jit(solution)/shard_map/ppermute | solution.py:205
  271.7 21.2 %collective-permute-start.39 = (bf16[256,1664]{1,0:T(8,128)(2,1)S(1)}, bf16[256,1664]{1,0:T(8,128)(2,1)}, u32[]{:S(2)}, u32[]{:S(2)}) collective-permute-start(bf16[256,1664]{1,0:T(8,128)(2,1)S(1)} %add_convert_fusion.7.refs_2_.refs_5_), channel_id=1, source_target_pairs={{0,1},{1,0},{2,3},{3,2},{4,5},{5,4},{6,7},{7,6},{8,9},{9,8},{10,11... | collective-permute-start | bytes 2555912 | tf_op jit(solution)/shard_map/ppermute | solution.py:205
  298.6 21.1 %collective-permute-start.40 = (bf16[128,1664]{1,0:T(8,128)(2,1)S(1)}, bf16[128,1664]{1,0:T(8,128)(2,1)S(1)}, u32[]{:S(2)}, u32[]{:S(2)}) collective-permute-start(bf16[128,1664]{1,0:T(8,128)(2,1)S(1)} %get-tuple-element.439.refs_10_), channel_id=1, source_target_pairs={{0,2},{1,3},{2,0},{3,1},{4,6},{5,7},{6,4},{7,5},{8,10},{9,11},{10,... | collective-permute-start | bytes 1277960 | tf_op jit(solution)/shard_map/ppermute | solution.py:205
  320.4 22.5 %collective-permute-start.42 = (bf16[576,768]{1,0:T(8,128)(2,1)}, bf16[576,768]{1,0:T(8,128)(2,1)S(1)}, u32[]{:S(2)}, u32[]{:S(2)}) collective-permute-start(bf16[576,768]{1,0:T(8,128)(2,1)} %get-tuple-element.290.refs_8_), channel_id=1, source_target_pairs={{0,16},{16,0},{1,17},{17,1},{2,18},{18,2},{3,19},{19,3},{4,20},{20... | collective-permute-start | bytes 2654216 | tf_op jit(solution)/shard_map/ppermute | solution.py:102
  321.9 21.0 %collective-permute-start.43 = (bf16[576,768]{1,0:T(8,128)(2,1)}, bf16[576,768]{1,0:T(8,128)(2,1)S(1)}, u32[]{:S(2)}, u32[]{:S(2)}) collective-permute-start(bf16[576,768]{1,0:T(8,128)(2,1)} %get-tuple-element.291.refs_12_), channel_id=1, source_target_pairs={{0,8},{4,12},{8,0},{12,4},{1,9},{5,13},{9,1},{13,5},{2,10},{6,14},... | collective-permute-start | bytes 2654216 | tf_op jit(solution)/shard_map/ppermute | solution.py:102
  356.7 23.1 %collective-permute-start.47 = (bf16[576,768]{1,0:T(8,128)(2,1)}, bf16[576,768]{1,0:T(8,128)(2,1)S(1)}, u32[]{:S(2)}, u32[]{:S(2)}) collective-permute-start(bf16[576,768]{1,0:T(8,128)(2,1)} %get-tuple-element.310), channel_id=1, source_target_pairs={{0,16},{16,0},{1,17},{17,1},{2,18},{18,2},{3,19},{19,3},{4,20},{20... | collective-permute-start | bytes 2654216 | tf_op jit(solution)/shard_map/ppermute | solution.py:102
  357.2 22.6 %collective-permute-start.48 = (bf16[576,768]{1,0:T(8,128)(2,1)}, bf16[576,768]{1,0:T(8,128)(2,1)S(1)}, u32[]{:S(2)}, u32[]{:S(2)}) collective-permute-start(bf16[576,768]{1,0:T(8,128)(2,1)} %get-tuple-element.312), channel_id=1, source_target_pairs={{0,8},{4,12},{8,0},{12,4},{1,9},{5,13},{9,1},{13,5},{2,10},{6,14},... | collective-permute-start | bytes 2654216 | tf_op jit(solution)/shard_map/ppermute | solution.py:102
  369.2 33.4 %collective-permute-start.49 = (bf16[256,1536]{1,0:T(8,128)(2,1)}, bf16[256,1536]{1,0:T(8,128)(2,1)}, u32[]{:S(2)}, u32[]{:S(2)}) collective-permute-start(bf16[256,1536]{1,0:T(8,128)(2,1)} %get-tuple-element.428), channel_id=1, source_target_pairs={{0,1},{1,0},{2,3},{3,2},{4,5},{5,4},{6,7},{7,6},{8,9},{9,8},{10,11... | collective-permute-start | bytes 2359304 | tf_op jit(solution)/shard_map/ppermute | solution.py:205
  381.0 23.1 %collective-permute-start.52 = (bf16[2,384,384]{2,1,0:T(8,128)(2,1)}, bf16[2,384,384]{2,1,0:T(8,128)(2,1)S(1)}, u32[]{:S(2)}, u32[]{:S(2)}) collective-permute-start(bf16[2,384,384]{2,1,0:T(8,128)(2,1)} %get-tuple-element.326), channel_id=1, source_target_pairs={{0,16},{16,0},{1,17},{17,1},{2,18},{18,2},{3,19},{19,3},{4,20},{20... | collective-permute-start | bytes 1769480 | tf_op jit(solution)/shard_map/ppermute | solution.py:102
  381.5 22.6 %collective-permute-start.53 = (bf16[2,384,384]{2,1,0:T(8,128)(2,1)}, bf16[2,384,384]{2,1,0:T(8,128)(2,1)S(1)}, u32[]{:S(2)}, u32[]{:S(2)}) collective-permute-start(bf16[2,384,384]{2,1,0:T(8,128)(2,1)} %get-tuple-element.327), channel_id=1, source_target_pairs={{0,8},{4,12},{8,0},{12,4},{1,9},{5,13},{9,1},{13,5},{2,10},{6,14},... | collective-permute-start | bytes 1769480 | tf_op jit(solution)/shard_map/ppermute | solution.py:102
  408.0 23.3 %collective-permute-start.56 = (bf16[384,384]{1,0:T(8,128)(2,1)}, bf16[384,384]{1,0:T(8,128)(2,1)S(1)}, u32[]{:S(2)}, u32[]{:S(2)}) collective-permute-start(bf16[384,384]{1,0:T(8,128)(2,1)} %fusion.14), channel_id=1, source_target_pairs={{0,8},{4,12},{8,0},{12,4},{1,9},{5,13},{9,1},{13,5},{2,10},{6,14},... | collective-permute-start | bytes 884744 | tf_op jit(solution)/shard_map/ppermute | solution.py:102
  432.1 27.3 %collective-permute-start.58 = (bf16[2,384,640]{2,1,0:T(8,128)(2,1)}, bf16[2,384,640]{2,1,0:T(8,128)(2,1)}, u32[]{:S(2)}, u32[]{:S(2)}) collective-permute-start(bf16[2,384,640]{2,1,0:T(8,128)(2,1)} %get-tuple-element.354.refs_5_), channel_id=1, source_target_pairs={{0,16},{16,0},{1,17},{17,1},{2,18},{18,2},{3,19},{19,3},{4,20},{20... | collective-permute-start | bytes 2949128 | tf_op jit(solution)/shard_map/ppermute | solution.py:102
  432.8 23.5 %collective-permute-start.59 = (bf16[2,384,512]{2,1,0:T(8,128)(2,1)}, bf16[2,384,512]{2,1,0:T(8,128)(2,1)}, u32[]{:S(2)}, u32[]{:S(2)}) collective-permute-start(bf16[2,384,512]{2,1,0:T(8,128)(2,1)} %get-tuple-element.356.refs_7_), channel_id=1, source_target_pairs={{0,8},{4,12},{8,0},{12,4},{1,9},{5,13},{9,1},{13,5},{2,10},{6,14},... | collective-permute-start | bytes 2359304 | tf_op jit(solution)/shard_map/ppermute | solution.py:102
  465.5 22.3 %collective-permute-start.70 = (bf16[576,768]{1,0:T(8,128)(2,1)}, bf16[576,768]{1,0:T(8,128)(2,1)S(1)}, u32[]{:S(2)}, u32[]{:S(2)}) collective-permute-start(bf16[576,768]{1,0:T(8,128)(2,1)} %get-tuple-element.378), channel_id=1, source_target_pairs={{0,16},{16,0},{1,17},{17,1},{2,18},{18,2},{3,19},{19,3},{4,20},{20... | collective-permute-start | bytes 2654216 | tf_op jit(solution)/shard_map/ppermute | solution.py:102
  466.3 23.0 %collective-permute-start.69 = (bf16[576,768]{1,0:T(8,128)(2,1)}, bf16[576,768]{1,0:T(8,128)(2,1)S(1)}, u32[]{:S(2)}, u32[]{:S(2)}) collective-permute-start(bf16[576,768]{1,0:T(8,128)(2,1)} %get-tuple-element.376), channel_id=1, source_target_pairs={{0,8},{4,12},{8,0},{12,4},{1,9},{5,13},{9,1},{13,5},{2,10},{6,14},... | collective-permute-start | bytes 2654216 | tf_op jit(solution)/shard_map/ppermute | solution.py:102
  473.0 21.4 %collective-permute-start.63 = (bf16[2,2,48,1152]{3,2,1,0:T(8,128)(2,1)S(1)}, bf16[2,2,48,1152]{3,2,1,0:T(8,128)(2,1)S(1)}, u32[]{:S(2)}, u32[]{:S(2)}) collective-permute-start(bf16[2,2,48,1152]{3,2,1,0:T(8,128)(2,1)S(1)} %pad_maximum_fusion.7), channel_id=1, source_target_pairs={{0,1},{1,0},{2,3},{3,2},{4,5},{5,4},{6,7},{7,6},{8,9},{9,8},{10,11... | collective-permute-start | bytes 1327112 | tf_op jit(solution)/shard_map/ppermute | solution.py:205
  (159 other events, 1154.5 us)
Sparse Core Ops, SparseCore 0:
  52.8 68.9 all-gather.2

commit v3 on v2

--- a/solution.py
+++ b/solution.py
@@ -359,7 +359,7 @@
 LOG2_E = 1.4426950408889634
 GELU_ROOT = math.sqrt(2.0 / math.pi)
 GELU_CUBE = 0.044715
-ROW_TILE = 256
+ROW_TILE = 512
 
 
 def kernel_params(n_axes=1):
@@ -547,49 +547,64 @@
     )(query, head_gradient, lse, cosine, sine, key_place, bounds, *key_value)
 
 
-def expert_step(expert, chunk, cot, gate_up, down, router, index, n_steps, buffers):
+def expert_step(scalars, chunk, cot, gate_up, down, router, index, n_steps, buffers):
     rows, width = chunk[0].shape
     units = down.shape[0]
-    tile = min(256, units)
-    steps = units // tile
     n_chunk = len(chunk)
+    n_rows = n_chunk * rows
     half_lanes = LANES // 2
-
-    def kernel(expert_ref, *refs):
+    places = [slice(i * rows, (i + 1) * rows) for i in range(n_chunk)]
+
+    def kernel(scalar_ref, router_ref, *refs):
         chunk_refs, cot_refs = refs[:n_chunk], refs[n_chunk : 2 * n_chunk]
-        gate_ref, up_ref, down_ref, router_ref = refs[2 * n_chunk : 2 * n_chunk + 4]
-        refs = refs[2 * n_chunk + 4 + len(buffers) :]
-        part_refs = refs[:n_chunk]
-        rows_ref, cot_ref, gated_ref, grad_gate_ref, grad_up_ref = refs[n_chunk : n_chunk + 5]
-        total_ref, weight_ref, share_ref = refs[n_chunk + 5 :]
-        step = pl.program_id(0)
+        gate_up_ref, down_ref = refs[2 * n_chunk : 2 * n_chunk + 2]
+        refs = refs[2 * n_chunk + 2 + len(buffers) :]
+        part_outs, buffer_outs = refs[:n_chunk], refs[n_chunk : n_chunk + 5]
+        row, cots, gate_w, up_w, down_w, part, gated, grad_gates, grad_ups, in_sems, out_sems = refs[
+            n_chunk + 5 :
+        ]
+        loads, stores = [], []
+
+        def load(source, target):
+            copy = pltpu.make_async_copy(source, target, in_sems.at[len(loads)])
+            copy.start()
+            loads.append(copy)
+
+        def store(source, target):
+            copy = pltpu.make_async_copy(source, target, out_sems.at[len(stores)])
+            copy.start()
+            stores.append(copy)
+
+        for ref, at in zip(chunk_refs, places):
+            load(ref, row.at[at])
+        load(gate_up_ref.at[:, :units], gate_w)
+        load(gate_up_ref.at[:, units:], up_w)
+        for ref, at in zip(cot_refs, places):
+            load(ref.at[scalar_ref[1]], cots.at[at])
+        load(down_ref, down_w)
+        in_buffer = [slice(index * n_rows + at.start, index * n_rows + at.stop) for at in places]
+
+        for copy in loads[: n_chunk + 1]:
+            copy.wait()
+        store(row, buffer_outs[0].at[index * n_rows : (index + 1) * n_rows])
+        gates = [jnp.dot(row[at, :], gate_w[...], preferred_element_type=F32) for at in places]
+        loads[n_chunk + 1].wait()
+        ups = [jnp.dot(row[at, :], up_w[...], preferred_element_type=F32) for at in places]
+        for copy in loads[n_chunk + 2 :]:
+            copy.wait()
+        store(cots.at[:, :width], buffer_outs[1].at[index * n_rows : (index + 1) * n_rows])
+
         lane = lax.broadcasted_iota(jnp.int32, (rows, LANES), 1)
-        places = [slice(i * rows, (i + 1) * rows) for i in range(n_chunk)]
-
-        @pl.when(step == 0)
-        def _():
-            for i, at in enumerate(places):
-                rows_ref[at, :] = chunk_refs[i][...]
-                cot_ref[at, :] = cot_refs[i][0, :, :width]
-                logits = jnp.dot(chunk_refs[i][...], router_ref[...], preferred_element_type=F32)
-                named = cot_refs[i][0, :, width:].astype(F32) > 0
-                logits = jnp.where(named, logits, -jnp.inf)
-                top = jnp.max(logits, axis=1, keepdims=True)
-                weights = jnp.exp(logits - top)
-                total = jnp.sum(weights, axis=1, keepdims=True)
-                own = jnp.sum(
-                    jnp.where(lane == expert_ref[0] + ROUTER_LANE, weights, 0.0), axis=1, keepdims=True
-                )
-                weight_ref[at, :] = jnp.broadcast_to(own / total, (rows, LANES))
-                share_ref[at, :] = jnp.zeros((rows, LANES), F32)
-                total_ref[at, :] = jnp.zeros((rows, width), F32)
-
-        for i, at in enumerate(places):
-            row = chunk_refs[i][...]
-            weight = weight_ref[at, 0:1]
-            gate = jnp.dot(row, gate_ref[...], preferred_element_type=F32)
-            up = jnp.dot(row, up_ref[...], preferred_element_type=F32)
-            grad_act = contract(cot_refs[i][0, :, :width], down_ref[...], 1, 1)
+        for at, gate, up, out, buffer_at in zip(places, gates, ups, part_outs, in_buffer):
+            logits = jnp.dot(row[at, :], router_ref[...], preferred_element_type=F32)
+            logits = jnp.where(cots[at, width:].astype(F32) > 0, logits, -jnp.inf)
+            top = jnp.max(logits, axis=1, keepdims=True)
+            weights = jnp.exp(logits - top)
+            total = jnp.sum(weights, axis=1, keepdims=True)
+            own = jnp.where(lane == scalar_ref[0] + ROUTER_LANE, weights, 0.0)
+            weight = jnp.sum(own, axis=1, keepdims=True) / total
+
+            grad_act = contract(cots[at, :width], down_w[...], 1, 1)
             square = gate * gate
             curve = jnp.tanh(GELU_ROOT * gate * (1.0 + GELU_CUBE * square))
             lifted = 0.5 + 0.5 * curve
@@ -598,107 +613,75 @@
                 1.0 + (3.0 * GELU_CUBE) * square
             )
             act = gelu * up
-            share_ref[at, :] += jnp.broadcast_to(
-                jnp.sum(act * grad_act, axis=1, keepdims=True), (rows, LANES)
-            )
-            gated_ref[at, :] = (act * weight).astype(BF16)
+            share = jnp.sum(act * grad_act, axis=1, keepdims=True)
+            gated[at, :] = (act * weight).astype(BF16)
             grad_act = grad_act * weight
             grad_up = (grad_act * gelu).astype(BF16)
             grad_gate = (grad_act * up * slope).astype(BF16)
-            grad_gate_ref[at, :] = grad_gate
-            grad_up_ref[at, :] = grad_up
-            total_ref[at, :] += contract(grad_gate, gate_ref[...], 1, 1) + contract(
-                grad_up, up_ref[...], 1, 1
-            )
-
-        @pl.when(step == steps - 1)
-        def _():
-            for i, at in enumerate(places):
-                part_refs[i][:, :width] = total_ref[at, :].astype(BF16)
-                share = share_ref[at, :]
-                high = share.astype(BF16).astype(F32)
-                part_refs[i][:, width:] = jnp.where(
-                    lane == expert_ref[0],
-                    high,
-                    jnp.where(lane == expert_ref[0] + half_lanes, share - high, 0.0),
-                ).astype(BF16)
-
-    def fixed(shape):
-        return pl.BlockSpec(shape, lambda j, scalars: (0,) * len(shape))
-
-    n_rows = n_chunk * rows
-    whole_rows = pl.BlockSpec((n_rows, width), lambda j, scalars: (index, 0))
-    unit_tile = pl.BlockSpec((n_rows, tile), lambda j, scalars: (index, j))
-    first_buffer = 1 + 2 * n_chunk + 4
-    grid_spec = pltpu.PrefetchScalarGridSpec(
-        num_scalar_prefetch=1,
-        grid=(steps,),
-        in_specs=[fixed(v.shape) for v in chunk]
-        + [
-            pl.BlockSpec((1, rows, width + LANES), lambda j, scalars: (scalars[1], 0, 0))
-            for _ in cot
-        ]
-        + [
-            pl.BlockSpec((width, tile), lambda j, scalars: (0, j)),
-            pl.BlockSpec((width, tile), lambda j, scalars: (0, j + steps)),
-            pl.BlockSpec((tile, width), lambda j, scalars: (j, 0)),
-            fixed(router.shape),
-        ]
-        + [pl.BlockSpec(memory_space=pl.ANY)] * len(buffers),
-        out_specs=[fixed((rows, width + LANES))] * n_chunk + [whole_rows] * 2 + [unit_tile] * 3,
-        scratch_shapes=[
-            pltpu.VMEM((n_rows, width), F32),
-            pltpu.VMEM((n_rows, LANES), F32),
-            pltpu.VMEM((n_rows, LANES), F32),
-        ],
-    )
+            grad_gates[at, :] = grad_gate
+            grad_ups[at, :] = grad_up
+            for source, target in zip((gated, grad_gates, grad_ups), buffer_outs[2:]):
+                store(source.at[at], target.at[buffer_at])
+            grad_row = contract(grad_gate, gate_w[...], 1, 1) + contract(grad_up, up_w[...], 1, 1)
+            part[at, :width] = grad_row.astype(BF16)
+            high = share.astype(BF16).astype(F32)
+            part[at, width:] = jnp.where(
+                lane == scalar_ref[0],
+                high,
+                jnp.where(lane == scalar_ref[0] + half_lanes, share - high, 0.0),
+            ).astype(BF16)
+            store(part.at[at], out)
+        for copy in stores:
+            copy.wait()
+
+    anywhere = pl.BlockSpec(memory_space=pl.ANY)
+    first_buffer = 2 + 2 * n_chunk + 2
     outs = pl.pallas_call(
         kernel,
-        grid_spec=grid_spec,
+        in_specs=[pl.BlockSpec(memory_space=pltpu.SMEM), pl.BlockSpec(memory_space=pltpu.VMEM)]
+        + [anywhere] * (2 * n_chunk + 2 + len(buffers)),
+        out_specs=[anywhere] * (n_chunk + 5),
         out_shape=[jax.ShapeDtypeStruct((rows, width + LANES), BF16)] * n_chunk
         + [jax.ShapeDtypeStruct((n_steps * n_rows, width), BF16)] * 2
         + [jax.ShapeDtypeStruct((n_steps * n_rows, units), BF16)] * 3,
         input_output_aliases={first_buffer + i: n_chunk + i for i in range(len(buffers))},
-        compiler_params=kernel_params(),
+        scratch_shapes=[
+            pltpu.VMEM((n_rows, width), BF16),
+            pltpu.VMEM((n_rows, width + LANES), BF16),
+            pltpu.VMEM((width, units), BF16),
+            pltpu.VMEM((width, units), BF16),
+            pltpu.VMEM((units, width), BF16),
+            pltpu.VMEM((n_rows, width + LANES), BF16),
+        ]
+        + [pltpu.VMEM((n_rows, units), BF16)] * 3
+        + [
+            pltpu.SemaphoreType.DMA((2 * n_chunk + 3,)),
+            pltpu.SemaphoreType.DMA((4 * n_chunk + 2,)),
+        ],
+        compiler_params=pltpu.CompilerParams(vmem_limit_bytes=56 * 1024 * 1024),
         cost_estimate=SMALL,
         name="expert_step",
-    )(expert, *chunk, *cot, gate_up, gate_up, down, router, *buffers)
+    )(scalars, router, *chunk, *cot, gate_up, down, *buffers)
     return outs[:n_chunk], outs[n_chunk:]
 
 
 def gate_up_grads(rows, grad_gate, grad_up):
     n_rows, width = rows.shape
     units = grad_gate.shape[1]
-    chunk, tile = n_rows // 4, 256
-
-    def kernel(rows_ref, gate_ref, up_ref, gate_out, up_out, gate_sum, up_sum):
-        step = pl.program_id(0)
-
-        @pl.when(step == 0)
-        def _():
-            gate_sum[...] = jnp.zeros_like(gate_sum)
-            up_sum[...] = jnp.zeros_like(up_sum)
-
-        for right, total in ((gate_ref, gate_sum), (up_ref, up_sum)):
-            for at in range(0, units, tile):
-                total[:, at : at + tile] += contract(rows_ref[...], right[:, at : at + tile], 0, 0)
-
-        @pl.when(step == 3)
-        def _():
-            gate_out[...] = gate_sum[...].astype(BF16)
-            up_out[...] = up_sum[...].astype(BF16)
-
-    def by_chunk(columns):
-        return pl.BlockSpec((chunk, columns), lambda j: (j, 0))
-
-    whole = pl.BlockSpec((width, units), lambda j: (0, 0))
+    tile = 256
+
+    def kernel(rows_ref, gate_ref, up_ref, gate_out, up_out):
+        for right, out in ((gate_ref, gate_out), (up_ref, up_out)):
+            out[...] = contract(rows_ref[...], right[...], 0, 0).astype(BF16)
+
+    whole = pl.BlockSpec((n_rows, units), lambda j: (0, 0))
+    out = pl.BlockSpec((tile, units), lambda j: (j, 0))
     return pl.pallas_call(
         kernel,
-        grid=(4,),
-        in_specs=[by_chunk(width), by_chunk(units), by_chunk(units)],
-        out_specs=[whole, whole],
+        grid=(width // tile,),
+        in_specs=[pl.BlockSpec((n_rows, tile), lambda j: (0, j)), whole, whole],
+        out_specs=[out, out],
         out_shape=[jax.ShapeDtypeStruct((width, units), BF16)] * 2,
-        scratch_shapes=[pltpu.VMEM((width, units), F32)] * 2,
         compiler_params=kernel_params(),
         cost_estimate=SMALL,
         name="gate_up_grads",
@@ -801,7 +784,7 @@
     block_rows = width // (axis_len("dp") * axis_len("y"))
     shapes = half_shapes([(block_rows, half)] * 2)
     n_out = len(shapes)
-    together = blocks_a_step(block_rows)
+    together = width // block_rows
     tile = together * block_rows
     n_tiles = width // tile
 
@@ -1217,16 +1200,16 @@
         other_0 = core_swap(other_0)
         mine_1, other_1 = run(1, [rows_1, other_1_rows])
 
-        rows_2, rows_3, other_1 = after((rows_2, rows_3, other_1), other_0)
+        rows_2, other_1, mine_1 = after((rows_2, other_1, mine_1), other_0)
+        other_1 = core_swap(other_1)
+        back_1 = joined(mine_1, other_1)
+        rows_2, rows_3 = after((rows_2, rows_3), back_1)
+        near = xor_shift(back_1, 1)
         other_3_rows = core_swap(rows_3)
-        other_1 = core_swap(other_1)
         mine_2, other_2 = run(2, [rows_2, other_2_rows])
 
-        rows_3, other_2, mine_1 = after((rows_3, other_2, mine_1), other_3_rows, other_1)
+        rows_3, other_2 = after((rows_3, other_2), other_3_rows)
         other_2 = core_swap(other_2)
-        back_1 = joined(mine_1, other_1)
-        near = xor_shift(back_1, 1)
-        rows_3 = after(rows_3, back_1)
         mine_3, other_3 = run(3, [rows_3, other_3_rows])
 
         mine_3, other_3 = after((mine_3, other_3), other_2, near)
@@ -1305,9 +1288,7 @@
     gu_block = CORES * gu_shard
 
     if phased:
-        results_near, results_handed = (
-            xor_shift(outs[0][low : low + rows], 1) for low in (0, rows)
-        )
+        results_handed = xor_shift(outs[0][rows:], 1)
 
     grad_middle, grad_branch, ffn_terms, grad_logits = middle_backward(
         backs, gates, middle, gain_two[None, :], router_all, grad_out
@@ -1315,38 +1296,31 @@
     grad_branch = [grad_branch, core_swap(grad_branch)]
     blended_gradient, out_grads = branch_backward(grad_branch, mixed, out_turned)
     if phased:
-        blended_gradient, results_handed = after((blended_gradient, results_handed))
-        pair = (outs[1][rows:].astype(F32) + results_handed.astype(F32)).astype(BF16)
-        cuts = [0, rows // 128 * 48, rows // 128 * 80, rows]
-        pieces = [pair[low:high] for low, high in zip(cuts, cuts[1:])]
-        blended_gradient, pieces = after((blended_gradient, pieces))
-        moe_far = [xor_shift(pieces[0], 2)]
-    blended_gradient, out_grads, expert_received = after(
-        (blended_gradient, out_grads, expert_received)
-    )
-    out_received = plane_moved(out_grads)
+        blended_gradient = after(blended_gradient, outs[0])
     grad_query, grad_kv_own, *grad_kv_parts = attention_backward(
         query_rows, blended_gradient, lse, key_value, cosine, sine, key_place, bounds, heads
     )
 
     if phased:
-        grad_query, grad_kv_parts, pieces, results_near = after(
-            (grad_query, grad_kv_parts, pieces, results_near), moe_far
+        grad_query, grad_kv_own, grad_kv_parts, results_handed = after(
+            (grad_query, grad_kv_own, grad_kv_parts, results_handed)
         )
-        moe_far.append(xor_shift(pieces[1], 2))
-    grad_kv_parts, out_received = after((grad_kv_parts, out_received))
     grad_kv_parts = [shifted(part, "y", ny - t) for t, part in enumerate(grad_kv_parts, 1)]
-    out_received = after(out_received, grad_query)
+    out_grads = after(out_grads, grad_kv_parts)
+    out_received = plane_moved(out_grads)
     if phased:
-        grad_query, pieces = after((grad_query, pieces), moe_far, grad_kv_parts)
-        moe_far.append(xor_shift(pieces[2], 2))
-    out_handed = plane_handed(plane_hand_on(out_grads, out_received))
+        pair = (outs[1][rows:].astype(F32) + results_handed.astype(F32)).astype(BF16)
+        cut = rows // 4
+        moe_far = [xor_shift(pair[:cut], 2)]
+        results_near = xor_shift(after(outs[0][:rows], pair), 1)
 
     for part in grad_kv_parts:
         grad_kv_own = grad_kv_own + part.astype(F32)
     grad_key_value = jnp.concatenate(
         [rotate(grad_kv_own[:, :HEAD_SIZE], cosine, -sine), grad_kv_own[:, HEAD_SIZE:]], axis=1
     ).astype(BF16)
+    if phased:
+        grad_key_value = after(grad_key_value, pair)
     is_ffn = (lax.broadcasted_iota(jnp.int32, (rows, LANES), 1) == 1).astype(BF16)
     grad_normed, grad_normed_other, qkv_grads = projection_backward(
         normed,
@@ -1359,10 +1333,9 @@
         jnp.concatenate([is_ffn, grad_logits], axis=0),
     )
     if phased:
-        qkv_grads, moe_far = after((qkv_grads, moe_far))
-        moe = outs[1][:rows].astype(F32) + results_near.astype(F32)
-        moe = moe + jnp.concatenate(moe_far, axis=0).astype(F32)
-    qkv_grads, out_handed = after((qkv_grads, out_handed))
+        qkv_grads, moe_far, pair = after((qkv_grads, moe_far, pair))
+        moe_far.append(xor_shift(pair[cut:], 2))
+    qkv_grads, out_received = after((qkv_grads, out_received))
 
     def line_sum(first, second):
         summed = jnp.concatenate([first, second], axis=1).astype(BF16)
@@ -1379,19 +1352,26 @@
         return lax.dynamic_index_in_dim(value, which, 0, keepdims=False)
 
     qkv_received = plane_moved(qkv_grads)
-    out_received, out_handed = after((out_received, out_handed), qkv_grads)
-    out_sum, out_pairs = line_sum(*plane_sum(out_grads, out_received, out_handed))
     qkv_hand_on = plane_hand_on(qkv_grads, qkv_received)
     qkv_handed = plane_handed(qkv_hand_on)
-    expert_hand_on = plane_hand_on(expert_grads, after(expert_received, qkv_grads))
-    grad_normed_other, moe = after((grad_normed_other, moe), qkv_hand_on)
+    expert_received = after(expert_received, qkv_grads)
+    expert_hand_on = plane_hand_on(expert_grads, expert_received)
+    out_received = after(out_received, qkv_hand_on)
+    out_handed = plane_handed(plane_hand_on(out_grads, out_received))
+    if phased:
+        moe_far, results_near = after((moe_far, results_near), qkv_hand_on)
+        moe = outs[1][:rows].astype(F32) + results_near.astype(F32)
+        moe = moe + jnp.concatenate(moe_far, axis=0).astype(F32)
+    grad_normed_other = after(grad_normed_other, qkv_hand_on)
     grad_normed = grad_normed + core_swap(grad_normed_other).astype(F32)
     grad_hidden_norm, _ = norm_back(hidden, gain_one, grad_normed)
     grad_input = grad_middle + grad_hidden_norm
     output = middle + moe
-    expert_handed = plane_handed(after(expert_hand_on, qkv_hand_on))
+    expert_handed = plane_handed(after(expert_hand_on, out_handed))
     qkv_sum, qkv_pairs = line_sum(*plane_sum(qkv_grads, qkv_received, qkv_handed))
-    out_sum = after(out_sum, qkv_pairs)
+    out_handed = after(out_handed, qkv_handed)
+    out_sum, out_pairs = line_sum(*plane_sum(out_grads, out_received, out_handed))
+    expert_handed = after(expert_handed, qkv_pairs, out_pairs)
     out_other = core_swap(of_core(out_sum, other_core).astype(BF16)).astype(F32)
     out_sum = in_core_order(of_core(out_sum, core), out_other)
     grad_out_proj = out_sum.swapaxes(0, 1).reshape(shard, query_width).T
@@ -1401,9 +1381,10 @@
     down_sum = jnp.concatenate([first_sum[gu_block:], second_sum[gu_block:]], axis=1)
     gu_sum = gu_sum.reshape(CORES, gu_shard, 2 * hidden_units)
     down_sum = down_sum.reshape(CORES, down_shard, width)
-    received = core_swap(
-        jnp.concatenate([of_core(gu_sum, other_core), of_core(down_sum, other_core)], 0).astype(BF16)
-    ).astype(F32)
+    to_other = jnp.concatenate([of_core(gu_sum, other_core), of_core(down_sum, other_core)], 0)
+    to_other = to_other.astype(BF16)
+    qkv_sum = after(qkv_sum, to_other)
+    received = core_swap(to_other).astype(F32)
     grad_gate_up = in_core_order(of_core(gu_sum, core), received[:gu_shard])
     grad_down = in_core_order(of_core(down_sum, core), received[gu_shard:])
 

time: 528 us -> 506 us (0.958)
  Pallas kernels: 172 us -> 151 us
  waiting for transfers between devices: 126 us -> 137 us
  local copies, waits for them, and re-layouts: 67.8 us -> 59.9 us
    pallas_call x5, Pallas kernels: 80.6 us -> 64.4 us  [the longest x4 49.4 us: expert_step(): pl.pallas_call(kernel, in_specs=[pl.BlockSpec(memory_space=pltpu.SMEM), p...]
    ppermute x34, waiting for transfers between devices: 59 us -> 67.5 us  [shifted(): lax.ppermute(value, name, [(i, (i + step * stride) % n) for i in range(n)])]
    unnamed x245 -> x221, local copies, waits for them, and re-layouts: 47.9 us -> 40.9 us
    ppermute x19 -> x18, waiting for transfers between devices: 60 us -> 60.8 us  [xor_shift(): return lax.ppermute(value, 'exp', [(i, i ^ step) for i in range(n)])]
    ppermute x19 -> x18, starting transfers between devices: 25.7 us -> 25.4 us  [xor_shift(): return lax.ppermute(value, 'exp', [(i, i ^ step) for i in range(n)])]
  transfers between devices with their start and end apart: 73 -> 72, of which waited for: 24 -> 29; matrix products, arithmetic and copies ran while one was open for 16% -> 15% of each run, Pallas kernels for 33% -> 30%
where the time goes in v3:
time: 506 us; the launch traced here: 500 us
  Pallas kernels  151 us (30%)
  waiting for transfers between devices  137 us (27%)
  other arithmetic  66.4 us (13%)
  starting transfers between devices  63.6 us (13%)
  local copies, waits for them, and re-layouts  59.9 us (12%)
  between operations  15.7 us (3%)
  matrix products  6.75 us (1%)
    ppermute x34, waiting for transfers between devices, shifted(): lax.ppermute(value, name, [(i, (i + step * stride) % n) for i in range(n)])  67.5 us
    ppermute x18, waiting for transfers between devices, xor_shift(): return lax.ppermute(value, 'exp', [(i, i ^ step) for i in range(n)])  60.8 us
    pallas_call x4, Pallas kernels, expert_step(): pl.pallas_call(kernel, in_specs=[pl.BlockSpec(memory_space=pltpu.SMEM), p...  49.4 us
    unnamed x221, local copies, waits for them, and re-layouts  40.9 us
    ppermute x34, starting transfers between devices, shifted(): lax.ppermute(value, name, [(i, (i + step * stride) % n) for i in range(n)])  36 us
    ppermute x18, starting transfers between devices, xor_shift(): return lax.ppermute(value, 'exp', [(i, i ^ step) for i in range(n)])  25.4 us
    pallas_call x1, Pallas kernels, gate_up_grads(): pl.pallas_call(kernel, grid=(width // tile,), in_specs=[pl.BlockSpec((n_r...  15 us
    pallas_call x1, Pallas kernels, attention_backward(): pl.pallas_call(kernel, grid=(heads,), in_specs=[by_head, by_head, fixed(l...  14.2 us
  transfers between devices with their start and end apart: 72, of which 29 were waited for; matrix products, arithmetic and copies ran while one was open for 15% of the time, Pallas kernels for 30%

profile of v3, /device:TPU:0, one launch (start us, length us, event | category | flops | bytes accessed | tf_op | source)
XLA Modules:
  0.0 500.2 jit_solution(3343250651435899935)
XLA Ops:
  27.3 12.9 %collective-permute-done.2 = bf16[96,1920]{1,0:T(8,128)(2,1)S(1)} collective-permute-done((bf16[96,1920]{1,0:T(8,128)(2,1)S(1)}, bf16[96,1920]{1,0:T(8,128)(2,1)S(1)}, u32[]{:S(2)}, u32[]{:S(2)}) %collective-permute-start.2) | collective-permute-done | bytes 368672 | tf_op jit(solution)/shard_map/ppermute | solution.py:205
  40.8 8.2 %collective-permute-done.3 = bf16[96,1920]{1,0:T(8,128)(2,1)S(1)} collective-permute-done((bf16[96,1920]{1,0:T(8,128)(2,1)S(1)}, bf16[96,1920]{1,0:T(8,128)(2,1)S(1)}, u32[]{:S(2)}, u32[]{:S(2)}) %collective-permute-start.3) | collective-permute-done | bytes 368672 | tf_op jit(solution)/shard_map/ppermute | solution.py:205
  62.2 14.6 %collective-permute-done.10.refs_3_ = bf16[384,512]{1,0:T(8,128)(2,1)S(1)} collective-permute-done((bf16[384,512]{1,0:T(8,128)(2,1)}, bf16[384,512]{1,0:T(8,128)(2,1)S(1)}, u32[]{:S(2)}, u32[]{:S(2)}) %collective-permute-start.10) | collective-permute-done | bytes 393248 | tf_op jit(solution)/shard_map/ppermute | solution.py:102
  83.4 7.7 %collective-permute-done.13.refs_7_ = bf16[384,512]{1,0:T(8,128)(2,1)S(1)} collective-permute-done((bf16[384,512]{1,0:T(8,128)(2,1)}, bf16[384,512]{1,0:T(8,128)(2,1)S(1)}, u32[]{:S(2)}, u32[]{:S(2)}) %collective-permute-start.13) | collective-permute-done | bytes 393248 | tf_op jit(solution)/shard_map/ppermute | solution.py:102
  94.8 4.2 place_blocks.3
  110.8 8.7 %collective-permute-done.16.refs_7_.refs_1_ = bf16[512,256]{1,0:T(8,128)(2,1)S(1)} collective-permute-done((bf16[512,256]{1,0:T(8,128)(2,1)S(1)}, bf16[512,256]{1,0:T(8,128)(2,1)S(1)}, u32[]{:S(2)}, u32[]{:S(2)}) %collective-permute-start.16) | collective-permute-done | bytes 262176 | tf_op jit(solution)/shard_map/ppermute | solution.py:102
  126.5 12.8 %attention_forward.1 = (bf16[512,768]{1,0:T(8,128)(2,1)}, bf16[512,768]{1,0:T(8,128)(2,1)}, f32[8,512]{1,0:T(8,128)}) custom-call(f32[512,1024]{1,0:T(8,128)} %get-tuple-element.191.projected_ref, f32[512,128]{1,0:T(8,128)} %get-tuple-element.420.cos_ref, f32[512,128]{1,0:T(8,128)} %get-tuple-element.392.sin_ref, s32[1024,1]{1,0:T(8,128)} %copy.194.place_ref, ...), custom_call_target="tpu_custom_call" | custom-call | flops 1 | bytes 1 | tf_op jit(solution)/shard_map/attention_forward/pallas_call | solution.py:442
  142.7 3.4 fusion.58
  161.8 10.5 %collective-permute-done.28.refs_3_ = bf16[576,768]{1,0:T(8,128)(2,1)} collective-permute-done((bf16[576,768]{1,0:T(8,128)(2,1)}, bf16[576,768]{1,0:T(8,128)(2,1)}, u32[]{:S(2)}, u32[]{:S(2)}) %collective-permute-start.28) | collective-permute-done | bytes 884768 | tf_op jit(solution)/shard_map/ppermute | solution.py:102
  177.1 6.1 %place_blocks.5 = (bf16[1536,1536]{1,0:T(8,128)(2,1)}, bf16[768,1536]{1,0:T(8,128)(2,1)}) custom-call(s32[2]{0:T(128)S(1)} %pad_add_fusion.3.place_ref, bf16[576,768]{1,0:T(8,128)(2,1)S(1)} %copy-done.14, bf16[576,768]{1,0:T(8,128)(2,1)S(1)} %copy-done.19, bf16[576,768]{1,0:T(8,128)(2,1)S(1)} %copy-done.9, bf16[576,768]{1,0:T(8,128)(2,1)} %collective-permute-done.28.refs_3_, ...), custom_call_target="tpu_custom_call" | custom-call | flops 1 | bytes 1 | tf_op jit(solution)/shard_map/place_blocks/pallas_call | solution.py:182
  183.2 12.2 %expert_step.4 = (bf16[256,1664]{1,0:T(8,128)(2,1)}, bf16[256,1664]{1,0:T(8,128)(2,1)}, bf16[2048,1536]{1,0:T(8,128)(2,1)}, bf16[2048,1536]{1,0:T(8,128)(2,1)}, ...) custom-call(s32[2]{0:T(128)} %pad_add_fusion.5.scalar_ref, ...), custom_call_target="tpu_custom_call" | custom-call | flops 1 | bytes 1 | tf_op jit(solution)/shard_map/expert_step/pallas_call | solution.py:639
  200.5 12.4 %expert_step.5 = (bf16[256,1664]{1,0:T(8,128)(2,1)}, bf16[256,1664]{1,0:T(8,128)(2,1)}, bf16[2048,1536]{1,0:T(8,128)(2,1)}, bf16[2048,1536]{1,0:T(8,128)(2,1)}, ...) custom-call(s32[2]{0:T(128)} %pad_add_fusion.6.scalar_ref, ...), custom_call_target="tpu_custom_call", output_to_operand_aliasing={{2}: (8, {}), {3}: (9, {}), {4}: (10, {}), {5}: (11, {}), {... | custom-call | flops 1 | bytes 1 | tf_op jit(solution)/shard_map/expert_step/pallas_call | solution.py:639
  212.9 3.7 collective-permute-done.33.refs_1_
  224.7 12.3 %expert_step.6 = (bf16[256,1664]{1,0:T(8,128)(2,1)}, bf16[256,1664]{1,0:T(8,128)(2,1)}, bf16[2048,1536]{1,0:T(8,128)(2,1)}, bf16[2048,1536]{1,0:T(8,128)(2,1)}, ...) custom-call(s32[2]{0:T(128)} %pad_add_fusion.7.scalar_ref, ...), custom_call_target="tpu_custom_call", output_to_operand_aliasing={{2}: (8, {}), {3}: (9, {}), {4}: (10, {}), {5}: (11, {}), {... | custom-call | flops 1 | bytes 1 | tf_op jit(solution)/shard_map/expert_step/pallas_call | solution.py:639
  237.6 12.5 %expert_step.7 = (bf16[256,1664]{1,0:T(8,128)(2,1)}, bf16[256,1664]{1,0:T(8,128)(2,1)}, bf16[2048,1536]{1,0:T(8,128)(2,1)}, bf16[2048,1536]{1,0:T(8,128)(2,1)}, ...) custom-call(s32[2]{0:T(128)} %pad_add_fusion.4.scalar_ref, ...), custom_call_target="tpu_custom_call", output_to_operand_aliasing={{2}: (8, {}), {3}: (9, {}), {4}: (10, {}), {5}: (11, {}), {... | custom-call | flops 1 | bytes 1 | tf_op jit(solution)/shard_map/expert_step/pallas_call | solution.py:639
  258.7 15.0 %gate_up_grads.1 = (bf16[1536,768]{1,0:T(8,128)(2,1)}, bf16[1536,768]{1,0:T(8,128)(2,1)}) custom-call(bf16[2048,1536]{1,0:T(8,128)(2,1)} %get-tuple-element.245.rows_ref, bf16[2048,768]{1,0:T(8,128)(2,1)} %get-tuple-element.246.gate_ref, bf16[2048,768]{1,0:T(8,128)(2,1)} %get-tuple-element.247.up_ref), custom_call_target="tpu_custom_call" | custom-call | flops 1 | bytes 1 | tf_op jit(solution)/shard_map/gate_up_grads/pallas_call | solution.py:679
  273.7 2.9 collective-permute-done.39.refs_2_
  284.9 13.6 %expert_weight_grads.1 = (bf16[576,768]{1,0:T(8,128)(2,1)}, bf16[576,768]{1,0:T(8,128)(2,1)}, bf16[576,768]{1,0:T(8,128)(2,1)}, bf16[576,768]{1,0:T(8,128)(2,1)}...) custom-call(s32[2]{0:T(128)} %copy-done.43, ...), custom_call_target="tpu_custom_call" | custom-call | flops 1 | bytes 1 | tf_op jit(solution)/shard_map/expert_weight_grads/pallas_call | solution.py:734
  298.5 5.1 %collective-permute-done.40.refs_9_ = bf16[128,1664]{1,0:T(8,128)(2,1)S(1)} collective-permute-done((bf16[128,1664]{1,0:T(8,128)(2,1)S(1)}, bf16[128,1664]{1,0:T(8,128)(2,1)S(1)}, u32[]{:S(2)}, u32[]{:S(2)}) %collective-permute-start.40) | collective-permute-done | bytes 426016 | tf_op jit(solution)/shard_map/ppermute | solution.py:205
  308.3 8.8 %expert_results.1 = (bf16[1024,1536]{1,0:T(8,128)(2,1)}, bf16[1024,1536]{1,0:T(8,128)(2,1)}) custom-call(bf16[2048,768]{1,0:T(8,128)(2,1)} %get-tuple-element.269.gated_ref, bf16[768,1536]{1,0:T(8,128)(2,1)} %get-tuple-element.204.refs_5_.down_ref), custom_call_target="tpu_custom_call" | custom-call | flops 1 | bytes 1 | tf_op jit(solution)/shard_map/expert_results/pallas_call | solution.py:765
  317.1 8.8 %collective-permute-done.41.refs_2_ = bf16[128,1664]{1,0:T(8,128)(2,1)S(1)} collective-permute-done((bf16[128,1664]{1,0:T(8,128)(2,1)}, bf16[128,1664]{1,0:T(8,128)(2,1)S(1)}, u32[]{:S(2)}, u32[]{:S(2)}) %collective-permute-start.41) | collective-permute-done | bytes 426016 | tf_op jit(solution)/shard_map/ppermute | solution.py:205
  331.8 4.5 middle_backward.1
  343.3 7.7 %branch_backward.1 = (bf16[512,768]{1,0:T(8,128)(2,1)}, bf16[2,384,384]{2,1,0:T(8,128)(2,1)}, bf16[2,384,384]{2,1,0:T(8,128)(2,1)}, bf16[2,384,384]{2,1,0:T(8,128)(2,1)}, bf16[2,384,384]{2,1,0:T(8,128)(2,1)}) custom-call(s32[2]{0:T(128)} %copy-done.43, bf16[256,1536]{1,0:T(8,128)(2,1)} %copy-done.42, bf16[256,1536]{1,0:T(8,128)(2,1)} %copy-done.96, ...), custom_call_target="tpu_custom_call" | custom-call | flops 1 | bytes 1 | tf_op jit(solution)/shard_map/branch_backward/pallas_call | solution.py:825
  351.0 14.2 %attention_backward.1 = (bf16[512,768]{1,0:T(8,128)(2,1)}, f32[512,256]{1,0:T(8,128)}, bf16[512,256]{1,0:T(8,128)(2,1)}) custom-call(bf16[512,768]{1,0:T(8,128)(2,1)} %get-tuple-element.284.query_ref, bf16[512,768]{1,0:T(8,128)(2,1)} %after.57.grad_ref, f32[8,512]{1,0:T(8,128)} %get-tuple-element.289.lse_ref, f32[512,128]{1,0:T(8,128)} %get-tuple-element.420.cos_ref, ...), custom_call_target="tpu_custom_call" | custom-call | flops 1 | bytes 1 | tf_op jit(solution)/shard_map/attention_backward/pallas_call | solution.py:518
  371.7 2.8 collective-permute-done.47.refs_4_
  379.3 11.3 %projection_backward.1 = (f32[256,1536]{1,0:T(8,128)}, bf16[256,1536]{1,0:T(8,128)(2,1)}, bf16[2,384,640]{2,1,0:T(8,128)(2,1)}, bf16[2,384,640]{2,1,0:T(8,128)(2...) custom-call(s32[2]{0:T(128)} %copy-done.43, bf16[512,1536]{1,0:T(8,128)(2,1)} %copy-done.67, ...), custom_call_target="tpu_custom_call" | custom-call | flops 1 | bytes 1 | tf_op jit(solution)/shard_map/projection_backward/pallas_call | solution.py:903
  402.9 7.5 %collective-permute-done.54 = bf16[2,384,512]{2,1,0:T(8,128)(2,1)} collective-permute-done((bf16[2,384,512]{2,1,0:T(8,128)(2,1)}, bf16[2,384,512]{2,1,0:T(8,128)(2,1)}, u32[]{:S(2)}, u32[]{:S(2)}) %collective-permute-start.54) | collective-permute-done | bytes 786464 | tf_op jit(solution)/shard_map/ppermute | solution.py:102
  412.7 5.7 %collective-permute-done.53 = bf16[2,384,640]{2,1,0:T(8,128)(2,1)} collective-permute-done((bf16[2,384,640]{2,1,0:T(8,128)(2,1)}, bf16[2,384,640]{2,1,0:T(8,128)(2,1)}, u32[]{:S(2)}, u32[]{:S(2)}) %collective-permute-start.53) | collective-permute-done | bytes 983072 | tf_op jit(solution)/shard_map/ppermute | solution.py:102
  427.2 3.1 add_bitcast_fusion.1
  431.6 4.9 collective-permute-done.62.refs_2_.refs_0_
  444.7 6.6 %collective-permute-done.66 = bf16[2,2,48,768]{3,2,1,0:T(8,128)(2,1)S(1)} collective-permute-done((bf16[2,2,48,768]{3,2,1,0:T(8,128)(2,1)S(1)}, bf16[2,2,48,768]{3,2,1,0:T(8,128)(2,1)S(1)}, u32[]{:S(2)}, u32[]{:S(2)}) %collective-permute-start.66) | collective-permute-done | bytes 294944 | tf_op jit(solution)/shard_map/ppermute | solution.py:205
  461.4 10.0 %collective-permute-done.59 = bf16[2,48,1152]{2,1,0:T(8,128)(2,1)S(1)} collective-permute-done((bf16[2,48,1152]{2,1,0:T(8,128)(2,1)S(1)}, bf16[2,48,1152]{2,1,0:T(8,128)(2,1)S(1)}, u32[]{:S(2)}, u32[]{:S(2)}) %collective-permute-start.59) | collective-permute-done | bytes 221216 | tf_op jit(solution)/shard_map/ppermute | solution.py:205
  (530 shorter events, 209.6 us)
Async XLA Ops:
  7.2 112.7 %all-gather.3.cloned.1.call-start = ((), (), s32[]{:S(2)}) async-start(), calls=%async_computation | async-start | bytes 4259840 | tf_op jit(solution)/shard_map/all_gather | solution.py:1091
  18.1 22.6 %collective-permute-start.1 = (bf16[96,1920]{1,0:T(8,128)(2,1)S(1)}, bf16[96,1920]{1,0:T(8,128)(2,1)S(1)}, u32[]{:S(2)}, u32[]{:S(2)}) collective-permute-start(bf16[96,1920]{1,0:T(8,128)(2,1)S(1)} %bitcast.218), channel_id=1, source_target_pairs={{0,1},{1,0},{2,3},{3,2},{4,5},{5,4},{6,7},{7,6},{8,9},{9,8},{10,11... | collective-permute-start | bytes 1105928 | tf_op jit(solution)/shard_map/ppermute | solution.py:205
  23.9 25.2 %collective-permute-start.6 = (bf16[576,768]{1,0:T(8,128)(2,1)S(1)}, bf16[576,768]{1,0:T(8,128)(2,1)S(1)}, u32[]{:S(2)}, u32[]{:S(2)}) collective-permute-start(bf16[576,768]{1,0:T(8,128)(2,1)S(1)} %pad_maximum_fusion.4.refs_3_), channel_id=1, source_target_pairs={{0,8},{4,12},{8,0},{12,4},{1,9},{5,13},{9,1},{13,5},{2,10},{6,14},... | collective-permute-start | bytes 2654216 | tf_op jit(solution)/shard_map/ppermute | solution.py:102
  25.6 23.5 %collective-permute-start.5 = (bf16[576,768]{1,0:T(8,128)(2,1)S(1)}, bf16[576,768]{1,0:T(8,128)(2,1)S(1)}, u32[]{:S(2)}, u32[]{:S(2)}) collective-permute-start(bf16[576,768]{1,0:T(8,128)(2,1)S(1)} %pad_maximum_fusion.3.refs_2_), channel_id=1, source_target_pairs={{0,16},{16,0},{1,17},{17,1},{2,18},{18,2},{3,19},{19,3},{4,20},{20... | collective-permute-start | bytes 2654216 | tf_op jit(solution)/shard_map/ppermute | solution.py:102
  53.7 24.3 %collective-permute-start.11 = (bf16[256,1536]{1,0:T(8,128)(2,1)}, bf16[256,1536]{1,0:T(8,128)(2,1)}, u32[]{:S(2)}, u32[]{:S(2)}) collective-permute-start(bf16[256,1536]{1,0:T(8,128)(2,1)} %unit_rows.1.unit_ref), channel_id=1, source_target_pairs={{0,4},{4,0},{8,12},{12,8},{1,5},{5,1},{9,13},{13,9},{2,6},{6,2},{1... | collective-permute-start | bytes 2359304 | tf_op jit(solution)/shard_map/ppermute | solution.py:107
  54.6 23.5 %collective-permute-start.7 = (bf16[384,640]{1,0:T(8,128)(2,1)}, bf16[384,640]{1,0:T(8,128)(2,1)S(1)}, u32[]{:S(2)}, u32[]{:S(2)}) collective-permute-start(bf16[384,640]{1,0:T(8,128)(2,1)} %slice.306.refs_0_), channel_id=1, source_target_pairs={{0,16},{16,0},{1,17},{17,1},{2,18},{18,2},{3,19},{19,3},{4,20},{20... | collective-permute-start | bytes 1474568 | tf_op jit(solution)/shard_map/ppermute | solution.py:102
  56.0 22.0 %collective-permute-start.9 = (bf16[384,640]{1,0:T(8,128)(2,1)}, bf16[384,640]{1,0:T(8,128)(2,1)}, u32[]{:S(2)}, u32[]{:S(2)}) collective-permute-start(bf16[384,640]{1,0:T(8,128)(2,1)} %slice.306.refs_0_), channel_id=1, source_target_pairs={{0,8},{4,12},{8,0},{12,4},{1,9},{5,13},{9,1},{13,5},{2,10},{6,14},... | collective-permute-start | bytes 1474568 | tf_op jit(solution)/shard_map/ppermute | solution.py:102
  99.0 20.4 %collective-permute-start.14 = (bf16[384,384]{1,0:T(8,128)(2,1)}, bf16[384,384]{1,0:T(8,128)(2,1)S(1)}, u32[]{:S(2)}, u32[]{:S(2)}) collective-permute-start(bf16[384,384]{1,0:T(8,128)(2,1)} %get-tuple-element.186.refs_0_), channel_id=1, source_target_pairs={{0,16},{16,0},{1,17},{17,1},{2,18},{18,2},{3,19},{19,3},{4,20},{20... | collective-permute-start | bytes 884744 | tf_op jit(solution)/shard_map/ppermute | solution.py:102
  120.5 22.1 %collective-permute-start.21 = (bf16[4,256,1664]{2,1,0:T(8,128)(2,1)}, bf16[4,256,1664]{2,1,0:T(8,128)(2,1)}, u32[]{:S(2)}, u32[]{:S(2)}) collective-permute-start(bf16[4,256,1664]{2,1,0:T(8,128)(2,1)} %get-tuple-element.195.refs_2_), channel_id=1, source_target_pairs={{0,4},{4,0},{8,12},{12,8},{1,5},{5,1},{9,13},{13,9},{2,6},{6,2},{1... | collective-permute-start | bytes 10223624 | tf_op jit(solution)/shard_map/ppermute | solution.py:107
  125.0 24.3 %collective-permute-start.26 = (bf16[576,768]{1,0:T(8,128)(2,1)}, bf16[576,768]{1,0:T(8,128)(2,1)S(1)}, u32[]{:S(2)}, u32[]{:S(2)}) collective-permute-start(bf16[576,768]{1,0:T(8,128)(2,1)} %get-tuple-element.197.refs_0_), channel_id=1, source_target_pairs={{0,8},{4,12},{8,0},{12,4},{1,9},{5,13},{9,1},{13,5},{2,10},{6,14},... | collective-permute-start | bytes 2654216 | tf_op jit(solution)/shard_map/ppermute | solution.py:102
  125.5 25.1 %collective-permute-start.27 = (bf16[576,768]{1,0:T(8,128)(2,1)}, bf16[576,768]{1,0:T(8,128)(2,1)}, u32[]{:S(2)}, u32[]{:S(2)}) collective-permute-start(bf16[576,768]{1,0:T(8,128)(2,1)} %get-tuple-element.200.refs_4_), channel_id=1, source_target_pairs={{0,16},{16,0},{1,17},{17,1},{2,18},{18,2},{3,19},{19,3},{4,20},{20... | collective-permute-start | bytes 2654216 | tf_op jit(solution)/shard_map/ppermute | solution.py:102
  150.6 21.8 %collective-permute-start.28 = (bf16[576,768]{1,0:T(8,128)(2,1)}, bf16[576,768]{1,0:T(8,128)(2,1)}, u32[]{:S(2)}, u32[]{:S(2)}) collective-permute-start(bf16[576,768]{1,0:T(8,128)(2,1)} %get-tuple-element.201), channel_id=1, source_target_pairs={{0,8},{4,12},{8,0},{12,4},{1,9},{5,13},{9,1},{13,5},{2,10},{6,14},... | collective-permute-start | bytes 2654216 | tf_op jit(solution)/shard_map/ppermute | solution.py:102
  151.8 21.8 %collective-permute-start.29 = (bf16[576,768]{1,0:T(8,128)(2,1)}, bf16[576,768]{1,0:T(8,128)(2,1)}, u32[]{:S(2)}, u32[]{:S(2)}) collective-permute-start(bf16[576,768]{1,0:T(8,128)(2,1)} %get-tuple-element.202), channel_id=1, source_target_pairs={{0,16},{16,0},{1,17},{17,1},{2,18},{18,2},{3,19},{19,3},{4,20},{20... | collective-permute-start | bytes 2654216 | tf_op jit(solution)/shard_map/ppermute | solution.py:102
  157.2 26.0 %collective-permute-start.25 = (bf16[256,1536]{1,0:T(8,128)(2,1)}, bf16[256,1536]{1,0:T(8,128)(2,1)}, u32[]{:S(2)}, u32[]{:S(2)}) collective-permute-start(bf16[256,1536]{1,0:T(8,128)(2,1)} %multiply_convert_fusion.1.refs_0_.refs_1_), channel_id=1, source_target_pairs={{0,4},{4,0},{8,12},{12,8},{1,5},{5,1},{9,13},{13,9},{2,6},{6,2},{1... | collective-permute-start | bytes 2359304 | tf_op jit(solution)/shard_map/ppermute | solution.py:107
  157.2 38.3 %collective-permute-start.23 = (bf16[256,1536]{1,0:T(8,128)(2,1)}, bf16[256,1536]{1,0:T(8,128)(2,1)}, u32[]{:S(2)}, u32[]{:S(2)}) collective-permute-start(bf16[256,1536]{1,0:T(8,128)(2,1)} %multiply_convert_fusion.1.refs_0_.refs_1_), channel_id=1, source_target_pairs={{0,1},{1,0},{2,3},{3,2},{4,5},{5,4},{6,7},{7,6},{8,9},{9,8},{10,11... | collective-permute-start | bytes 2359304 | tf_op jit(solution)/shard_map/ppermute | solution.py:205
  158.6 37.8 %collective-permute-start.24 = (bf16[256,1536]{1,0:T(8,128)(2,1)}, bf16[256,1536]{1,0:T(8,128)(2,1)}, u32[]{:S(2)}, u32[]{:S(2)}) collective-permute-start(bf16[256,1536]{1,0:T(8,128)(2,1)} %multiply_convert_fusion.1.refs_0_.refs_1_), channel_id=1, source_target_pairs={{0,2},{1,3},{2,0},{3,1},{4,6},{5,7},{6,4},{7,5},{8,10},{9,11},{10,... | collective-permute-start | bytes 2359304 | tf_op jit(solution)/shard_map/ppermute | solution.py:205
  195.4 21.2 %collective-permute-start.32 = (bf16[256,1664]{1,0:T(8,128)(2,1)}, bf16[256,1664]{1,0:T(8,128)(2,1)S(1)}, u32[]{:S(2)}, u32[]{:S(2)}) collective-permute-start(bf16[256,1664]{1,0:T(8,128)(2,1)} %get-tuple-element.205.refs_2_), channel_id=1, source_target_pairs={{0,4},{4,0},{8,12},{12,8},{1,5},{5,1},{9,13},{13,9},{2,6},{6,2},{1... | collective-permute-start | bytes 2555912 | tf_op jit(solution)/shard_map/ppermute | solution.py:107
  223.5 26.6 %collective-permute-start.37 = (bf16[256,1664]{1,0:T(8,128)(2,1)S(1)}, bf16[256,1664]{1,0:T(8,128)(2,1)S(1)}, u32[]{:S(2)}, u32[]{:S(2)}) collective-permute-start(bf16[256,1664]{1,0:T(8,128)(2,1)S(1)} %copy-done.79), channel_id=1, source_target_pairs={{0,1},{1,0},{2,3},{3,2},{4,5},{5,4},{6,7},{7,6},{8,9},{9,8},{10,11... | collective-permute-start | bytes 2555912 | tf_op jit(solution)/shard_map/ppermute | solution.py:205
  255.2 21.4 %collective-permute-start.39 = (bf16[256,1664]{1,0:T(8,128)(2,1)S(1)}, bf16[256,1664]{1,0:T(8,128)(2,1)}, u32[]{:S(2)}, u32[]{:S(2)}) collective-permute-start(bf16[256,1664]{1,0:T(8,128)(2,1)S(1)} %add_convert_fusion.7.refs_5_.refs_2_), channel_id=1, source_target_pairs={{0,1},{1,0},{2,3},{3,2},{4,5},{5,4},{6,7},{7,6},{8,9},{9,8},{10,11... | collective-permute-start | bytes 2555912 | tf_op jit(solution)/shard_map/ppermute | solution.py:205
  282.3 21.3 %collective-permute-start.40 = (bf16[128,1664]{1,0:T(8,128)(2,1)S(1)}, bf16[128,1664]{1,0:T(8,128)(2,1)S(1)}, u32[]{:S(2)}, u32[]{:S(2)}) collective-permute-start(bf16[128,1664]{1,0:T(8,128)(2,1)S(1)} %get-tuple-element.409.refs_10_), channel_id=1, source_target_pairs={{0,2},{1,3},{2,0},{3,1},{4,6},{5,7},{6,4},{7,5},{8,10},{9,11},{10,... | collective-permute-start | bytes 1277960 | tf_op jit(solution)/shard_map/ppermute | solution.py:205
  304.4 21.4 %collective-permute-start.42 = (bf16[576,768]{1,0:T(8,128)(2,1)}, bf16[576,768]{1,0:T(8,128)(2,1)S(1)}, u32[]{:S(2)}, u32[]{:S(2)}) collective-permute-start(bf16[576,768]{1,0:T(8,128)(2,1)} %get-tuple-element.273.refs_8_), channel_id=1, source_target_pairs={{0,16},{16,0},{1,17},{17,1},{2,18},{18,2},{3,19},{19,3},{4,20},{20... | collective-permute-start | bytes 2654216 | tf_op jit(solution)/shard_map/ppermute | solution.py:102
  305.4 21.1 %collective-permute-start.43 = (bf16[576,768]{1,0:T(8,128)(2,1)}, bf16[576,768]{1,0:T(8,128)(2,1)S(1)}, u32[]{:S(2)}, u32[]{:S(2)}) collective-permute-start(bf16[576,768]{1,0:T(8,128)(2,1)} %get-tuple-element.274.refs_12_), channel_id=1, source_target_pairs={{0,8},{4,12},{8,0},{12,4},{1,9},{5,13},{9,1},{13,5},{2,10},{6,14},... | collective-permute-start | bytes 2654216 | tf_op jit(solution)/shard_map/ppermute | solution.py:102
  339.4 25.8 %collective-permute-start.46 = (bf16[256,1536]{1,0:T(8,128)(2,1)S(1)}, bf16[256,1536]{1,0:T(8,128)(2,1)S(1)}, u32[]{:S(2)}, u32[]{:S(2)}) collective-permute-start(bf16[256,1536]{1,0:T(8,128)(2,1)S(1)} %get-tuple-element.399), channel_id=1, source_target_pairs={{0,1},{1,0},{2,3},{3,2},{4,5},{5,4},{6,7},{7,6},{8,9},{9,8},{10,11... | collective-permute-start | bytes 2359304 | tf_op jit(solution)/shard_map/ppermute | solution.py:205
  339.4 57.6 %collective-permute-start.60 = (bf16[576,768]{1,0:T(8,128)(2,1)}, bf16[576,768]{1,0:T(8,128)(2,1)}, u32[]{:S(2)}, u32[]{:S(2)}) collective-permute-start(bf16[576,768]{1,0:T(8,128)(2,1)} %get-tuple-element.326), channel_id=1, source_target_pairs={{0,16},{16,0},{1,17},{17,1},{2,18},{18,2},{3,19},{19,3},{4,20},{20... | collective-permute-start | bytes 2654216 | tf_op jit(solution)/shard_map/ppermute | solution.py:102
  340.5 57.7 %collective-permute-start.61 = (bf16[576,768]{1,0:T(8,128)(2,1)}, bf16[576,768]{1,0:T(8,128)(2,1)}, u32[]{:S(2)}, u32[]{:S(2)}) collective-permute-start(bf16[576,768]{1,0:T(8,128)(2,1)} %get-tuple-element.328), channel_id=1, source_target_pairs={{0,8},{4,12},{8,0},{12,4},{1,9},{5,13},{9,1},{13,5},{2,10},{6,14},... | collective-permute-start | bytes 2654216 | tf_op jit(solution)/shard_map/ppermute | solution.py:102
  369.3 21.3 %collective-permute-start.48 = (bf16[64,1536]{1,0:T(8,128)(2,1)}, bf16[64,1536]{1,0:T(8,128)(2,1)S(1)}, u32[]{:S(2)}, u32[]{:S(2)}) collective-permute-start(bf16[64,1536]{1,0:T(8,128)(2,1)} %slice.325), channel_id=1, source_target_pairs={{0,2},{1,3},{2,0},{3,1},{4,6},{5,7},{6,4},{7,5},{8,10},{9,11},{10,... | collective-permute-start | bytes 589832 | tf_op jit(solution)/shard_map/ppermute | solution.py:205
  393.4 25.0 %collective-permute-start.53 = (bf16[2,384,640]{2,1,0:T(8,128)(2,1)}, bf16[2,384,640]{2,1,0:T(8,128)(2,1)}, u32[]{:S(2)}, u32[]{:S(2)}) collective-permute-start(bf16[2,384,640]{2,1,0:T(8,128)(2,1)} %get-tuple-element.316.refs_5_), channel_id=1, source_target_pairs={{0,16},{16,0},{1,17},{17,1},{2,18},{18,2},{3,19},{19,3},{4,20},{20... | collective-permute-start | bytes 2949128 | tf_op jit(solution)/shard_map/ppermute | solution.py:102
  394.4 31.6 %collective-permute-start.50 = (bf16[256,1536]{1,0:T(8,128)(2,1)}, bf16[256,1536]{1,0:T(8,128)(2,1)}, u32[]{:S(2)}, u32[]{:S(2)}) collective-permute-start(bf16[256,1536]{1,0:T(8,128)(2,1)} %after.61), channel_id=1, source_target_pairs={{0,1},{1,0},{2,3},{3,2},{4,5},{5,4},{6,7},{7,6},{8,9},{9,8},{10,11... | collective-permute-start | bytes 2359304 | tf_op jit(solution)/shard_map/ppermute | solution.py:205
  397.0 30.1 %collective-permute-start.49 = (bf16[192,1536]{1,0:T(8,128)(2,1)}, bf16[192,1536]{1,0:T(8,128)(2,1)}, u32[]{:S(2)}, u32[]{:S(2)}) collective-permute-start(bf16[192,1536]{1,0:T(8,128)(2,1)} %slice.261), channel_id=1, source_target_pairs={{0,2},{1,3},{2,0},{3,1},{4,6},{5,7},{6,4},{7,5},{8,10},{9,11},{10,... | collective-permute-start | bytes 1769480 | tf_op jit(solution)/shard_map/ppermute | solution.py:205
  427.1 24.3 %collective-permute-start.55 = (bf16[256,1536]{1,0:T(8,128)(2,1)}, bf16[256,1536]{1,0:T(8,128)(2,1)}, u32[]{:S(2)}, u32[]{:S(2)}) collective-permute-start(bf16[256,1536]{1,0:T(8,128)(2,1)} %after.65), channel_id=1, source_target_pairs={{0,4},{4,0},{8,12},{12,8},{1,5},{5,1},{9,13},{13,9},{2,6},{6,2},{1... | collective-permute-start | bytes 2359304 | tf_op jit(solution)/shard_map/ppermute | solution.py:107
  436.5 35.8 %collective-permute-start.64 = (bf16[576,768]{1,0:T(8,128)(2,1)}, bf16[576,768]{1,0:T(8,128)(2,1)S(1)}, u32[]{:S(2)}, u32[]{:S(2)}) collective-permute-start(bf16[576,768]{1,0:T(8,128)(2,1)} %get-tuple-element.341), channel_id=1, source_target_pairs={{0,8},{4,12},{8,0},{12,4},{1,9},{5,13},{9,1},{13,5},{2,10},{6,14},... | collective-permute-start | bytes 2654216 | tf_op jit(solution)/shard_map/ppermute | solution.py:102
  437.3 35.1 %collective-permute-start.65 = (bf16[576,768]{1,0:T(8,128)(2,1)}, bf16[576,768]{1,0:T(8,128)(2,1)}, u32[]{:S(2)}, u32[]{:S(2)}) collective-permute-start(bf16[576,768]{1,0:T(8,128)(2,1)} %get-tuple-element.342), channel_id=1, source_target_pairs={{0,16},{16,0},{1,17},{17,1},{2,18},{18,2},{3,19},{19,3},{4,20},{20... | collective-permute-start | bytes 2654216 | tf_op jit(solution)/shard_map/ppermute | solution.py:102
  (148 other events, 1020.1 us)
Sparse Core Ops, SparseCore 0:
  50.9 68.9 all-gather.2

commit v4 on v3

--- a/solution.py
+++ b/solution.py
@@ -992,6 +992,99 @@
         cost_estimate=SMALL,
         name="middle_backward",
     )(*arrays, gates, middle, gain, router, grad_out)
+
+
+def expert_sums(core, halves, gu_shard, down_shard):
+    block_rows, half = halves[0][0].shape
+    counts = [len(blocks) for blocks in halves]
+    kept = gu_shard + down_shard
+
+    def kernel(core_ref, *refs):
+        mine_ref, other_ref, total = refs[sum(counts) :]
+        at = 0
+        for i, n in enumerate(counts):
+            columns = slice(i * half, (i + 1) * half)
+            total[:, columns] = sum(r[...].astype(F32) for r in refs[at : at + n])
+            at += n
+        core = core_ref[0]
+        for which, out in ((core, mine_ref), (1 - core, other_ref)):
+            gu = pl.ds(pl.multiple_of(which * gu_shard, 8), gu_shard)
+            down = pl.ds(pl.multiple_of(CORES * gu_shard + which * down_shard, 8), down_shard)
+            out[:gu_shard, :] = total[gu, :].astype(out.dtype)
+            out[gu_shard:, :] = total[down, :].astype(out.dtype)
+
+    vmem = pl.BlockSpec(memory_space=pltpu.VMEM)
+    return pl.pallas_call(
+        kernel,
+        in_specs=[pl.BlockSpec(memory_space=pltpu.SMEM)] + [vmem] * sum(counts),
+        out_specs=[vmem, vmem],
+        out_shape=[
+            jax.ShapeDtypeStruct((kept, 2 * half), F32),
+            jax.ShapeDtypeStruct((kept, 2 * half), BF16),
+        ],
+        scratch_shapes=[pltpu.VMEM((block_rows, 2 * half), F32)],
+        compiler_params=pltpu.CompilerParams(vmem_limit_bytes=48 * 1024 * 1024),
+        cost_estimate=SMALL,
+        name="expert_sums",
+    )(core.astype(jnp.int32).reshape(1), *halves[0], *halves[1])
+
+
+def expert_shards(core, mine, received, gu_shard, down_shard):
+    width = mine.shape[1]
+
+    def kernel(core_ref, mine_ref, received_ref, gu_ref, down_ref):
+        core = core_ref[0]
+        for which, rows in ((core, mine_ref), (1 - core, received_ref)):
+            gu_ref[which] = rows[:gu_shard, :].astype(F32)
+            down_ref[which] = rows[gu_shard:, :].astype(F32)
+
+    vmem = pl.BlockSpec(memory_space=pltpu.VMEM)
+    return pl.pallas_call(
+        kernel,
+        in_specs=[pl.BlockSpec(memory_space=pltpu.SMEM), vmem, vmem],
+        out_specs=[vmem, vmem],
+        out_shape=[
+            jax.ShapeDtypeStruct((CORES, gu_shard, width), F32),
+            jax.ShapeDtypeStruct((CORES, down_shard, width), F32),
+        ],
+        compiler_params=pltpu.CompilerParams(vmem_limit_bytes=48 * 1024 * 1024),
+        cost_estimate=SMALL,
+        name="expert_shards",
+    )(core.astype(jnp.int32).reshape(1), mine, received)
+
+
+def projection_shards(core, summed, received, columns):
+    own_query, whole = columns
+    rows = summed.shape[1]
+    own_width = own_query + 2 * HEAD_SIZE
+    key_at = KEY_VALUE_HEADS * own_query
+    value_at = key_at + KEY_VALUE_HEADS * HEAD_SIZE
+
+    def kernel(core_ref, summed_ref, received_ref, out_ref, extra_ref):
+        core = core_ref[0]
+        mine, other = summed_ref[core], received_ref[...].astype(F32)
+        for which, part in ((core, mine), (1 - core, other)):
+            for start, size, at in (
+                (0, own_query, 0),
+                (key_at, HEAD_SIZE, own_query),
+                (value_at, HEAD_SIZE, own_query + HEAD_SIZE),
+            ):
+                target = pl.ds(pl.multiple_of(start + which * size, LANES), size)
+                out_ref[:, target] = part[:, at : at + size]
+        extra_ref[...] = mine[:, own_width:] + other[:, own_width:]
+
+    vmem = pl.BlockSpec(memory_space=pltpu.VMEM)
+    return pl.pallas_call(
+        kernel,
+        in_specs=[pl.BlockSpec(memory_space=pltpu.SMEM), vmem, vmem],
+        out_specs=[vmem, vmem],
+        out_shape=[
+            jax.ShapeDtypeStruct((rows, whole), F32),
+            jax.ShapeDtypeStruct((rows, LANES), F32),
+        ],
+        cost_estimate=SMALL,
+        name="projection_shards",
+    )(core.astype(jnp.int32).reshape(1), summed, received)
 
 
 def on_device(
@@ -1285,7 +1378,6 @@
         expert_received = plane_joined(
             plane_moved_part(expert_grads, False), plane_moved_part(expert_grads, True)
         )
-    gu_block = CORES * gu_shard
 
     if phased:
         results_handed = xor_shift(outs[0][rows:], 1)
@@ -1376,30 +1468,17 @@
     out_sum = in_core_order(of_core(out_sum, core), out_other)
     grad_out_proj = out_sum.swapaxes(0, 1).reshape(shard, query_width).T
 
-    first_sum, second_sum = plane_sum(expert_grads, expert_received, expert_handed)
-    gu_sum = jnp.concatenate([first_sum[:gu_block], second_sum[:gu_block]], axis=1)
-    down_sum = jnp.concatenate([first_sum[gu_block:], second_sum[gu_block:]], axis=1)
-    gu_sum = gu_sum.reshape(CORES, gu_shard, 2 * hidden_units)
-    down_sum = down_sum.reshape(CORES, down_shard, width)
-    to_other = jnp.concatenate([of_core(gu_sum, other_core), of_core(down_sum, other_core)], 0)
-    to_other = to_other.astype(BF16)
-    qkv_sum = after(qkv_sum, to_other)
-    received = core_swap(to_other).astype(F32)
-    grad_gate_up = in_core_order(of_core(gu_sum, core), received[:gu_shard])
-    grad_down = in_core_order(of_core(down_sum, core), received[gu_shard:])
-
-    qkv_other = core_swap(of_core(qkv_sum, other_core).astype(BF16)).astype(F32)
-    qkv_mine = of_core(qkv_sum, core)
-    extra_sum = qkv_mine[:, own_width:] + qkv_other[:, own_width:]
-    pair = in_core_order(qkv_mine[:, :own_width], qkv_other[:, :own_width])
-    key_at, value_at = own_query, own_query + HEAD_SIZE
-    grad_qkv = jnp.concatenate(
-        [
-            pair[:, :, :key_at].swapaxes(0, 1).reshape(shard, -1),
-            pair[:, :, key_at:value_at].swapaxes(0, 1).reshape(shard, -1),
-            pair[:, :, value_at:].swapaxes(0, 1).reshape(shard, -1),
-        ],
-        axis=1,
+    blocks = [
+        [half[0][0], *(came[0] for came in received), *handed]
+        for half, received, handed in zip(expert_grads, expert_received, expert_handed)
+    ]
+    mine, to_other = expert_sums(core, blocks, gu_shard, down_shard)
+    grad_gate_up, grad_down = expert_shards(
+        core, mine, core_swap(to_other), gu_shard, down_shard
+    )
+    qkv_other = core_swap(of_core(qkv_sum, other_core).astype(BF16))
+    grad_qkv, extra_sum = projection_shards(
+        core, qkv_sum, qkv_other, (own_query, qkv_weight.shape[1])
     )
     return (
         output[None],

time: 506 us -> 500 us (0.988)
  Pallas kernels: 151 us -> 158 us
  waiting for transfers between devices: 137 us -> 131 us
    pallas_call x0 -> x3, Pallas kernels: none -> 8.06 us  [the longest x1 4.27 us: expert_sums(): pl.pallas_call(kernel, in_specs=[pl.BlockSpec(memory_space=pltpu.SMEM)] +...]
    ppermute x34, waiting for transfers between devices: 67.5 us -> 62.1 us  [shifted(): lax.ppermute(value, name, [(i, (i + step * stride) % n) for i in range(n)])]
    unnamed x221 -> x213, local copies, waits for them, and re-layouts: 40.9 us -> 36.2 us
  transfers between devices with their start and end apart: 72 -> 72, of which waited for: 29 -> 29; matrix products, arithmetic and copies ran while one was open for 15% -> 17% of each run, Pallas kernels for 30% -> 31%
where the time goes in v4:
time: 500 us; the launch traced here: 494 us
  Pallas kernels  158 us (32%)
  waiting for transfers between devices  131 us (26%)
  other arithmetic  64.5 us (13%)
  starting transfers between devices  62.5 us (12%)
  local copies, waits for them, and re-layouts  56.2 us (11%)
  between operations  15.6 us (3%)
  matrix products  6.75 us (1%)
    ppermute x34, waiting for transfers between devices, shifted(): lax.ppermute(value, name, [(i, (i + step * stride) % n) for i in range(n)])  62.1 us
    ppermute x18, waiting for transfers between devices, xor_shift(): return lax.ppermute(value, 'exp', [(i, i ^ step) for i in range(n)])  61.5 us
    pallas_call x4, Pallas kernels, expert_step(): pl.pallas_call(kernel, in_specs=[pl.BlockSpec(memory_space=pltpu.SMEM), p...  49.6 us
    ppermute x34, starting transfers between devices, shifted(): lax.ppermute(value, name, [(i, (i + step * stride) % n) for i in range(n)])  37.4 us
    unnamed x213, local copies, waits for them, and re-layouts  36.2 us
    ppermute x18, starting transfers between devices, xor_shift(): return lax.ppermute(value, 'exp', [(i, i ^ step) for i in range(n)])  22.6 us
    pallas_call x1, Pallas kernels, gate_up_grads(): pl.pallas_call(kernel, grid=(width // tile,), in_specs=[pl.BlockSpec((n_r...  15 us
    pallas_call x1, Pallas kernels, attention_backward(): pl.pallas_call(kernel, grid=(heads,), in_specs=[by_head, by_head, fixed(l...  14.5 us
  transfers between devices with their start and end apart: 72, of which 29 were waited for; matrix products, arithmetic and copies ran while one was open for 17% of the time, Pallas kernels for 31%

profile of v4, /device:TPU:0, one launch (start us, length us, event | category | flops | bytes accessed | tf_op | source)
XLA Modules:
  0.0 494.5 jit_solution(16590473188044570202)
XLA Ops:
  27.3 12.9 %collective-permute-done.2 = bf16[96,1920]{1,0:T(8,128)(2,1)S(1)} collective-permute-done((bf16[96,1920]{1,0:T(8,128)(2,1)S(1)}, bf16[96,1920]{1,0:T(8,128)(2,1)S(1)}, u32[]{:S(2)}, u32[]{:S(2)}) %collective-permute-start.2) | collective-permute-done | bytes 368672 | tf_op jit(solution)/shard_map/ppermute | solution.py:205
  40.8 8.3 %collective-permute-done.3 = bf16[96,1920]{1,0:T(8,128)(2,1)S(1)} collective-permute-done((bf16[96,1920]{1,0:T(8,128)(2,1)S(1)}, bf16[96,1920]{1,0:T(8,128)(2,1)S(1)}, u32[]{:S(2)}, u32[]{:S(2)}) %collective-permute-start.3) | collective-permute-done | bytes 368672 | tf_op jit(solution)/shard_map/ppermute | solution.py:205
  62.2 14.7 %collective-permute-done.10.refs_3_ = bf16[384,512]{1,0:T(8,128)(2,1)S(1)} collective-permute-done((bf16[384,512]{1,0:T(8,128)(2,1)}, bf16[384,512]{1,0:T(8,128)(2,1)S(1)}, u32[]{:S(2)}, u32[]{:S(2)}) %collective-permute-start.10) | collective-permute-done | bytes 393248 | tf_op jit(solution)/shard_map/ppermute | solution.py:102
  83.3 7.8 %collective-permute-done.13.refs_7_ = bf16[384,512]{1,0:T(8,128)(2,1)S(1)} collective-permute-done((bf16[384,512]{1,0:T(8,128)(2,1)}, bf16[384,512]{1,0:T(8,128)(2,1)S(1)}, u32[]{:S(2)}, u32[]{:S(2)}) %collective-permute-start.13) | collective-permute-done | bytes 393248 | tf_op jit(solution)/shard_map/ppermute | solution.py:102
  94.8 4.2 place_blocks.3
  110.8 8.7 %collective-permute-done.16.refs_7_.refs_1_ = bf16[512,256]{1,0:T(8,128)(2,1)S(1)} collective-permute-done((bf16[512,256]{1,0:T(8,128)(2,1)S(1)}, bf16[512,256]{1,0:T(8,128)(2,1)S(1)}, u32[]{:S(2)}, u32[]{:S(2)}) %collective-permute-start.16) | collective-permute-done | bytes 262176 | tf_op jit(solution)/shard_map/ppermute | solution.py:102
  126.9 12.8 %attention_forward.1 = (bf16[512,768]{1,0:T(8,128)(2,1)}, bf16[512,768]{1,0:T(8,128)(2,1)}, f32[8,512]{1,0:T(8,128)}) custom-call(f32[512,1024]{1,0:T(8,128)} %get-tuple-element.197.projected_ref, f32[512,128]{1,0:T(8,128)} %get-tuple-element.430.cos_ref, f32[512,128]{1,0:T(8,128)} %get-tuple-element.404.sin_ref, s32[1024,1]{1,0:T(8,128)} %copy.187.place_ref, ...), custom_call_target="tpu_custom_call" | custom-call | flops 1 | bytes 1 | tf_op jit(solution)/shard_map/attention_forward/pallas_call | solution.py:442
  142.1 3.4 fusion.56
  162.9 9.4 %collective-permute-done.28.refs_3_ = bf16[576,768]{1,0:T(8,128)(2,1)} collective-permute-done((bf16[576,768]{1,0:T(8,128)(2,1)}, bf16[576,768]{1,0:T(8,128)(2,1)}, u32[]{:S(2)}, u32[]{:S(2)}) %collective-permute-start.28) | collective-permute-done | bytes 884768 | tf_op jit(solution)/shard_map/ppermute | solution.py:102
  176.1 6.1 %place_blocks.5 = (bf16[1536,1536]{1,0:T(8,128)(2,1)}, bf16[768,1536]{1,0:T(8,128)(2,1)}) custom-call(s32[2]{0:T(128)S(1)} %pad_add_fusion.3.place_ref, bf16[576,768]{1,0:T(8,128)(2,1)S(1)} %copy-done.14, bf16[576,768]{1,0:T(8,128)(2,1)} %collective-permute-done.26.refs_2_.refs_1_, bf16[576,768]{1,0:T(8,128)(2,1)S(1)} %copy-done.9, ...), custom_call_target="tpu_custom_call" | custom-call | flops 1 | bytes 1 | tf_op jit(solution)/shard_map/place_blocks/pallas_call | solution.py:182
  182.2 12.2 %expert_step.4 = (bf16[256,1664]{1,0:T(8,128)(2,1)}, bf16[256,1664]{1,0:T(8,128)(2,1)}, bf16[2048,1536]{1,0:T(8,128)(2,1)}, bf16[2048,1536]{1,0:T(8,128)(2,1)}, ...) custom-call(s32[2]{0:T(128)} %pad_add_fusion.5.scalar_ref, ...), custom_call_target="tpu_custom_call" | custom-call | flops 1 | bytes 1 | tf_op jit(solution)/shard_map/expert_step/pallas_call | solution.py:639
  201.2 12.7 %expert_step.5 = (bf16[256,1664]{1,0:T(8,128)(2,1)}, bf16[256,1664]{1,0:T(8,128)(2,1)}, bf16[2048,1536]{1,0:T(8,128)(2,1)}, bf16[2048,1536]{1,0:T(8,128)(2,1)}, ...) custom-call(s32[2]{0:T(128)} %pad_add_fusion.6.scalar_ref, ...), custom_call_target="tpu_custom_call", output_to_operand_aliasing={{2}: (8, {}), {3}: (9, {}), {4}: (10, {}), {5}: (11, {}), {... | custom-call | flops 1 | bytes 1 | tf_op jit(solution)/shard_map/expert_step/pallas_call | solution.py:639
  214.0 3.7 collective-permute-done.33.refs_1_
  223.6 12.3 %expert_step.6 = (bf16[256,1664]{1,0:T(8,128)(2,1)}, bf16[256,1664]{1,0:T(8,128)(2,1)}, bf16[2048,1536]{1,0:T(8,128)(2,1)}, bf16[2048,1536]{1,0:T(8,128)(2,1)}, ...) custom-call(s32[2]{0:T(128)} %pad_add_fusion.7.scalar_ref, ...), custom_call_target="tpu_custom_call", output_to_operand_aliasing={{2}: (8, {}), {3}: (9, {}), {4}: (10, {}), {5}: (11, {}), {... | custom-call | flops 1 | bytes 1 | tf_op jit(solution)/shard_map/expert_step/pallas_call | solution.py:639
  236.6 12.4 %expert_step.7 = (bf16[256,1664]{1,0:T(8,128)(2,1)}, bf16[256,1664]{1,0:T(8,128)(2,1)}, bf16[2048,1536]{1,0:T(8,128)(2,1)}, bf16[2048,1536]{1,0:T(8,128)(2,1)}, ...) custom-call(s32[2]{0:T(128)} %pad_add_fusion.4.scalar_ref, ...), custom_call_target="tpu_custom_call", output_to_operand_aliasing={{2}: (8, {}), {3}: (9, {}), {4}: (10, {}), {5}: (11, {}), {... | custom-call | flops 1 | bytes 1 | tf_op jit(solution)/shard_map/expert_step/pallas_call | solution.py:639
  258.4 15.0 %gate_up_grads.1 = (bf16[1536,768]{1,0:T(8,128)(2,1)}, bf16[1536,768]{1,0:T(8,128)(2,1)}) custom-call(bf16[2048,1536]{1,0:T(8,128)(2,1)} %get-tuple-element.251.rows_ref, bf16[2048,768]{1,0:T(8,128)(2,1)} %get-tuple-element.252.gate_ref, bf16[2048,768]{1,0:T(8,128)(2,1)} %get-tuple-element.253.up_ref), custom_call_target="tpu_custom_call" | custom-call | flops 1 | bytes 1 | tf_op jit(solution)/shard_map/gate_up_grads/pallas_call | solution.py:679
  283.7 13.6 %expert_weight_grads.1 = (bf16[576,768]{1,0:T(8,128)(2,1)}, bf16[576,768]{1,0:T(8,128)(2,1)}, bf16[576,768]{1,0:T(8,128)(2,1)}, bf16[576,768]{1,0:T(8,128)(2,1)}...) custom-call(s32[2]{0:T(128)} %copy-done.48, ...), custom_call_target="tpu_custom_call" | custom-call | flops 1 | bytes 1 | tf_op jit(solution)/shard_map/expert_weight_grads/pallas_call | solution.py:734
  297.4 5.1 %collective-permute-done.40.refs_9_ = bf16[128,1664]{1,0:T(8,128)(2,1)S(1)} collective-permute-done((bf16[128,1664]{1,0:T(8,128)(2,1)S(1)}, bf16[128,1664]{1,0:T(8,128)(2,1)S(1)}, u32[]{:S(2)}, u32[]{:S(2)}) %collective-permute-start.40) | collective-permute-done | bytes 426016 | tf_op jit(solution)/shard_map/ppermute | solution.py:205
  308.2 8.4 %expert_results.1 = (bf16[1024,1536]{1,0:T(8,128)(2,1)}, bf16[1024,1536]{1,0:T(8,128)(2,1)}) custom-call(bf16[2048,768]{1,0:T(8,128)(2,1)} %get-tuple-element.275.gated_ref, bf16[768,1536]{1,0:T(8,128)(2,1)} %get-tuple-element.210.refs_5_.down_ref), custom_call_target="tpu_custom_call" | custom-call | flops 1 | bytes 1 | tf_op jit(solution)/shard_map/expert_results/pallas_call | solution.py:765
  316.7 8.8 %collective-permute-done.41.refs_2_ = bf16[128,1664]{1,0:T(8,128)(2,1)S(1)} collective-permute-done((bf16[128,1664]{1,0:T(8,128)(2,1)}, bf16[128,1664]{1,0:T(8,128)(2,1)S(1)}, u32[]{:S(2)}, u32[]{:S(2)}) %collective-permute-start.41) | collective-permute-done | bytes 426016 | tf_op jit(solution)/shard_map/ppermute | solution.py:205
  331.2 4.5 middle_backward.1
  337.4 3.9 add_convert_fusion.1
  345.9 7.7 %branch_backward.1 = (bf16[512,768]{1,0:T(8,128)(2,1)}, bf16[2,384,384]{2,1,0:T(8,128)(2,1)}, bf16[2,384,384]{2,1,0:T(8,128)(2,1)}, bf16[2,384,384]{2,1,0:T(8,128)(2,1)}, bf16[2,384,384]{2,1,0:T(8,128)(2,1)}) custom-call(s32[2]{0:T(128)} %copy-done.48, bf16[256,1536]{1,0:T(8,128)(2,1)} %copy-done.47, bf16[256,1536]{1,0:T(8,128)(2,1)} %copy-done.89, ...), custom_call_target="tpu_custom_call" | custom-call | flops 1 | bytes 1 | tf_op jit(solution)/shard_map/branch_backward/pallas_call | solution.py:825
  353.6 14.5 %attention_backward.1 = (bf16[512,768]{1,0:T(8,128)(2,1)}, f32[512,256]{1,0:T(8,128)}, bf16[512,256]{1,0:T(8,128)(2,1)}) custom-call(bf16[512,768]{1,0:T(8,128)(2,1)} %get-tuple-element.290.query_ref, bf16[512,768]{1,0:T(8,128)(2,1)} %after.56.grad_ref, f32[8,512]{1,0:T(8,128)} %get-tuple-element.295.lse_ref, f32[512,128]{1,0:T(8,128)} %get-tuple-element.430.cos_ref, ...), custom_call_target="tpu_custom_call" | custom-call | flops 1 | bytes 1 | tf_op jit(solution)/shard_map/attention_backward/pallas_call | solution.py:518
  381.9 11.1 %projection_backward.1 = (f32[256,1536]{1,0:T(8,128)}, bf16[256,1536]{1,0:T(8,128)(2,1)}, bf16[2,384,640]{2,1,0:T(8,128)(2,1)}, bf16[2,384,640]{2,1,0:T(8,128)(2...) custom-call(s32[2]{0:T(128)} %copy-done.48, bf16[512,1536]{1,0:T(8,128)(2,1)} %copy-done.65, ...), custom_call_target="tpu_custom_call" | custom-call | flops 1 | bytes 1 | tf_op jit(solution)/shard_map/projection_backward/pallas_call | solution.py:903
  404.8 8.1 %collective-permute-done.54 = bf16[2,384,512]{2,1,0:T(8,128)(2,1)} collective-permute-done((bf16[2,384,512]{2,1,0:T(8,128)(2,1)}, bf16[2,384,512]{2,1,0:T(8,128)(2,1)}, u32[]{:S(2)}, u32[]{:S(2)}) %collective-permute-start.54) | collective-permute-done | bytes 786464 | tf_op jit(solution)/shard_map/ppermute | solution.py:102
  415.1 5.0 %collective-permute-done.53 = bf16[2,384,640]{2,1,0:T(8,128)(2,1)} collective-permute-done((bf16[2,384,640]{2,1,0:T(8,128)(2,1)}, bf16[2,384,640]{2,1,0:T(8,128)(2,1)}, u32[]{:S(2)}, u32[]{:S(2)}) %collective-permute-start.53) | collective-permute-done | bytes 983072 | tf_op jit(solution)/shard_map/ppermute | solution.py:102
  428.3 3.6 add_bitcast_fusion.1
  433.2 3.4 collective-permute-done.61.refs_0_.refs_2_
  445.5 7.9 %collective-permute-done.63 = bf16[2,2,48,768]{3,2,1,0:T(8,128)(2,1)S(1)} collective-permute-done((bf16[2,2,48,768]{3,2,1,0:T(8,128)(2,1)S(1)}, bf16[2,2,48,768]{3,2,1,0:T(8,128)(2,1)S(1)}, u32[]{:S(2)}, u32[]{:S(2)}) %collective-permute-start.63) | collective-permute-done | bytes 294944 | tf_op jit(solution)/shard_map/ppermute | solution.py:205
  464.8 4.3 expert_sums.1
  469.3 6.7 %collective-permute-done.59 = bf16[2,48,1152]{2,1,0:T(8,128)(2,1)} collective-permute-done((bf16[2,48,1152]{2,1,0:T(8,128)(2,1)}, bf16[2,48,1152]{2,1,0:T(8,128)(2,1)}, u32[]{:S(2)}, u32[]{:S(2)}) %collective-permute-start.59) | collective-permute-done | bytes 221216 | tf_op jit(solution)/shard_map/ppermute | solution.py:205
  (493 shorter events, 205.9 us)
Async XLA Ops:
  7.2 113.0 %all-gather.3.cloned.1.call-start = ((), (), s32[]{:S(2)}) async-start(), calls=%async_computation | async-start | bytes 4259840 | tf_op jit(solution)/shard_map/all_gather | solution.py:1184
  18.1 22.6 %collective-permute-start.1 = (bf16[96,1920]{1,0:T(8,128)(2,1)S(1)}, bf16[96,1920]{1,0:T(8,128)(2,1)S(1)}, u32[]{:S(2)}, u32[]{:S(2)}) collective-permute-start(bf16[96,1920]{1,0:T(8,128)(2,1)S(1)} %bitcast.183), channel_id=1, source_target_pairs={{0,1},{1,0},{2,3},{3,2},{4,5},{5,4},{6,7},{7,6},{8,9},{9,8},{10,11... | collective-permute-start | bytes 1105928 | tf_op jit(solution)/shard_map/ppermute | solution.py:205
  23.9 25.2 %collective-permute-start.6 = (bf16[576,768]{1,0:T(8,128)(2,1)S(1)}, bf16[576,768]{1,0:T(8,128)(2,1)S(1)}, u32[]{:S(2)}, u32[]{:S(2)}) collective-permute-start(bf16[576,768]{1,0:T(8,128)(2,1)S(1)} %pad_maximum_fusion.2.refs_3_), channel_id=1, source_target_pairs={{0,8},{4,12},{8,0},{12,4},{1,9},{5,13},{9,1},{13,5},{2,10},{6,14},... | collective-permute-start | bytes 2654216 | tf_op jit(solution)/shard_map/ppermute | solution.py:102
  25.6 23.5 %collective-permute-start.5 = (bf16[576,768]{1,0:T(8,128)(2,1)S(1)}, bf16[576,768]{1,0:T(8,128)(2,1)S(1)}, u32[]{:S(2)}, u32[]{:S(2)}) collective-permute-start(bf16[576,768]{1,0:T(8,128)(2,1)S(1)} %pad_maximum_fusion.1.refs_2_), channel_id=1, source_target_pairs={{0,16},{16,0},{1,17},{17,1},{2,18},{18,2},{3,19},{19,3},{4,20},{20... | collective-permute-start | bytes 2654216 | tf_op jit(solution)/shard_map/ppermute | solution.py:102
  53.7 24.3 %collective-permute-start.11 = (bf16[256,1536]{1,0:T(8,128)(2,1)}, bf16[256,1536]{1,0:T(8,128)(2,1)}, u32[]{:S(2)}, u32[]{:S(2)}) collective-permute-start(bf16[256,1536]{1,0:T(8,128)(2,1)} %unit_rows.1.unit_ref), channel_id=1, source_target_pairs={{0,4},{4,0},{8,12},{12,8},{1,5},{5,1},{9,13},{13,9},{2,6},{6,2},{1... | collective-permute-start | bytes 2359304 | tf_op jit(solution)/shard_map/ppermute | solution.py:107
  54.5 23.5 %collective-permute-start.7 = (bf16[384,640]{1,0:T(8,128)(2,1)}, bf16[384,640]{1,0:T(8,128)(2,1)S(1)}, u32[]{:S(2)}, u32[]{:S(2)}) collective-permute-start(bf16[384,640]{1,0:T(8,128)(2,1)} %slice.254.refs_0_), channel_id=1, source_target_pairs={{0,16},{16,0},{1,17},{17,1},{2,18},{18,2},{3,19},{19,3},{4,20},{20... | collective-permute-start | bytes 1474568 | tf_op jit(solution)/shard_map/ppermute | solution.py:102
  56.0 22.0 %collective-permute-start.9 = (bf16[384,640]{1,0:T(8,128)(2,1)}, bf16[384,640]{1,0:T(8,128)(2,1)}, u32[]{:S(2)}, u32[]{:S(2)}) collective-permute-start(bf16[384,640]{1,0:T(8,128)(2,1)} %slice.254.refs_0_), channel_id=1, source_target_pairs={{0,8},{4,12},{8,0},{12,4},{1,9},{5,13},{9,1},{13,5},{2,10},{6,14},... | collective-permute-start | bytes 1474568 | tf_op jit(solution)/shard_map/ppermute | solution.py:102
  99.0 20.4 %collective-permute-start.14 = (bf16[384,384]{1,0:T(8,128)(2,1)}, bf16[384,384]{1,0:T(8,128)(2,1)S(1)}, u32[]{:S(2)}, u32[]{:S(2)}) collective-permute-start(bf16[384,384]{1,0:T(8,128)(2,1)} %get-tuple-element.192.refs_0_), channel_id=1, source_target_pairs={{0,16},{16,0},{1,17},{17,1},{2,18},{18,2},{3,19},{19,3},{4,20},{20... | collective-permute-start | bytes 884744 | tf_op jit(solution)/shard_map/ppermute | solution.py:102
  121.0 21.2 %collective-permute-start.21 = (bf16[4,256,1664]{2,1,0:T(8,128)(2,1)}, bf16[4,256,1664]{2,1,0:T(8,128)(2,1)}, u32[]{:S(2)}, u32[]{:S(2)}) collective-permute-start(bf16[4,256,1664]{2,1,0:T(8,128)(2,1)} %get-tuple-element.201.refs_2_), channel_id=1, source_target_pairs={{0,4},{4,0},{8,12},{12,8},{1,5},{5,1},{9,13},{13,9},{2,6},{6,2},{1... | collective-permute-start | bytes 10223624 | tf_op jit(solution)/shard_map/ppermute | solution.py:107
  125.4 24.4 %collective-permute-start.26 = (bf16[576,768]{1,0:T(8,128)(2,1)}, bf16[576,768]{1,0:T(8,128)(2,1)}, u32[]{:S(2)}, u32[]{:S(2)}) collective-permute-start(bf16[576,768]{1,0:T(8,128)(2,1)} %get-tuple-element.203.refs_0_), channel_id=1, source_target_pairs={{0,8},{4,12},{8,0},{12,4},{1,9},{5,13},{9,1},{13,5},{2,10},{6,14},... | collective-permute-start | bytes 2654216 | tf_op jit(solution)/shard_map/ppermute | solution.py:102
  125.9 25.1 %collective-permute-start.27 = (bf16[576,768]{1,0:T(8,128)(2,1)}, bf16[576,768]{1,0:T(8,128)(2,1)}, u32[]{:S(2)}, u32[]{:S(2)}) collective-permute-start(bf16[576,768]{1,0:T(8,128)(2,1)} %get-tuple-element.206.refs_4_), channel_id=1, source_target_pairs={{0,16},{16,0},{1,17},{17,1},{2,18},{18,2},{3,19},{19,3},{4,20},{20... | collective-permute-start | bytes 2654216 | tf_op jit(solution)/shard_map/ppermute | solution.py:102
  151.0 21.3 %collective-permute-start.28 = (bf16[576,768]{1,0:T(8,128)(2,1)}, bf16[576,768]{1,0:T(8,128)(2,1)}, u32[]{:S(2)}, u32[]{:S(2)}) collective-permute-start(bf16[576,768]{1,0:T(8,128)(2,1)} %get-tuple-element.207), channel_id=1, source_target_pairs={{0,8},{4,12},{8,0},{12,4},{1,9},{5,13},{9,1},{13,5},{2,10},{6,14},... | collective-permute-start | bytes 2654216 | tf_op jit(solution)/shard_map/ppermute | solution.py:102
  151.5 21.1 %collective-permute-start.29 = (bf16[576,768]{1,0:T(8,128)(2,1)}, bf16[576,768]{1,0:T(8,128)(2,1)}, u32[]{:S(2)}, u32[]{:S(2)}) collective-permute-start(bf16[576,768]{1,0:T(8,128)(2,1)} %get-tuple-element.208), channel_id=1, source_target_pairs={{0,16},{16,0},{1,17},{17,1},{2,18},{18,2},{3,19},{19,3},{4,20},{20... | collective-permute-start | bytes 2654216 | tf_op jit(solution)/shard_map/ppermute | solution.py:102
  158.2 24.0 %collective-permute-start.25 = (bf16[256,1536]{1,0:T(8,128)(2,1)}, bf16[256,1536]{1,0:T(8,128)(2,1)}, u32[]{:S(2)}, u32[]{:S(2)}) collective-permute-start(bf16[256,1536]{1,0:T(8,128)(2,1)} %multiply_convert_fusion.1.refs_0_.refs_1_), channel_id=1, source_target_pairs={{0,4},{4,0},{8,12},{12,8},{1,5},{5,1},{9,13},{13,9},{2,6},{6,2},{1... | collective-permute-start | bytes 2359304 | tf_op jit(solution)/shard_map/ppermute | solution.py:107
  158.2 36.9 %collective-permute-start.23 = (bf16[256,1536]{1,0:T(8,128)(2,1)}, bf16[256,1536]{1,0:T(8,128)(2,1)}, u32[]{:S(2)}, u32[]{:S(2)}) collective-permute-start(bf16[256,1536]{1,0:T(8,128)(2,1)} %multiply_convert_fusion.1.refs_0_.refs_1_), channel_id=1, source_target_pairs={{0,1},{1,0},{2,3},{3,2},{4,5},{5,4},{6,7},{7,6},{8,9},{9,8},{10,11... | collective-permute-start | bytes 2359304 | tf_op jit(solution)/shard_map/ppermute | solution.py:205
  159.7 37.8 %collective-permute-start.24 = (bf16[256,1536]{1,0:T(8,128)(2,1)}, bf16[256,1536]{1,0:T(8,128)(2,1)}, u32[]{:S(2)}, u32[]{:S(2)}) collective-permute-start(bf16[256,1536]{1,0:T(8,128)(2,1)} %multiply_convert_fusion.1.refs_0_.refs_1_), channel_id=1, source_target_pairs={{0,2},{1,3},{2,0},{3,1},{4,6},{5,7},{6,4},{7,5},{8,10},{9,11},{10,... | collective-permute-start | bytes 2359304 | tf_op jit(solution)/shard_map/ppermute | solution.py:205
  194.5 23.2 %collective-permute-start.32 = (bf16[256,1664]{1,0:T(8,128)(2,1)}, bf16[256,1664]{1,0:T(8,128)(2,1)}, u32[]{:S(2)}, u32[]{:S(2)}) collective-permute-start(bf16[256,1664]{1,0:T(8,128)(2,1)} %get-tuple-element.211.refs_2_), channel_id=1, source_target_pairs={{0,4},{4,0},{8,12},{12,8},{1,5},{5,1},{9,13},{13,9},{2,6},{6,2},{1... | collective-permute-start | bytes 2555912 | tf_op jit(solution)/shard_map/ppermute | solution.py:107
  223.3 25.8 %collective-permute-start.37 = (bf16[256,1664]{1,0:T(8,128)(2,1)}, bf16[256,1664]{1,0:T(8,128)(2,1)S(1)}, u32[]{:S(2)}, u32[]{:S(2)}) collective-permute-start(bf16[256,1664]{1,0:T(8,128)(2,1)} %add_convert_fusion.8.refs_2_), channel_id=1, source_target_pairs={{0,1},{1,0},{2,3},{3,2},{4,5},{5,4},{6,7},{7,6},{8,9},{9,8},{10,11... | collective-permute-start | bytes 2555912 | tf_op jit(solution)/shard_map/ppermute | solution.py:205
  254.0 21.4 %collective-permute-start.39 = (bf16[256,1664]{1,0:T(8,128)(2,1)S(1)}, bf16[256,1664]{1,0:T(8,128)(2,1)}, u32[]{:S(2)}, u32[]{:S(2)}) collective-permute-start(bf16[256,1664]{1,0:T(8,128)(2,1)S(1)} %add_convert_fusion.7.refs_5_.refs_2_), channel_id=1, source_target_pairs={{0,1},{1,0},{2,3},{3,2},{4,5},{5,4},{6,7},{7,6},{8,9},{9,8},{10,11... | collective-permute-start | bytes 2555912 | tf_op jit(solution)/shard_map/ppermute | solution.py:205
  281.1 21.3 %collective-permute-start.40 = (bf16[128,1664]{1,0:T(8,128)(2,1)S(1)}, bf16[128,1664]{1,0:T(8,128)(2,1)S(1)}, u32[]{:S(2)}, u32[]{:S(2)}) collective-permute-start(bf16[128,1664]{1,0:T(8,128)(2,1)S(1)} %get-tuple-element.421.refs_10_), channel_id=1, source_target_pairs={{0,2},{1,3},{2,0},{3,1},{4,6},{5,7},{6,4},{7,5},{8,10},{9,11},{10,... | collective-permute-start | bytes 1277960 | tf_op jit(solution)/shard_map/ppermute | solution.py:205
  303.2 22.3 %collective-permute-start.42 = (bf16[576,768]{1,0:T(8,128)(2,1)}, bf16[576,768]{1,0:T(8,128)(2,1)S(1)}, u32[]{:S(2)}, u32[]{:S(2)}) collective-permute-start(bf16[576,768]{1,0:T(8,128)(2,1)} %get-tuple-element.279.refs_8_), channel_id=1, source_target_pairs={{0,16},{16,0},{1,17},{17,1},{2,18},{18,2},{3,19},{19,3},{4,20},{20... | collective-permute-start | bytes 2654216 | tf_op jit(solution)/shard_map/ppermute | solution.py:102
  304.2 21.3 %collective-permute-start.43 = (bf16[576,768]{1,0:T(8,128)(2,1)}, bf16[576,768]{1,0:T(8,128)(2,1)S(1)}, u32[]{:S(2)}, u32[]{:S(2)}) collective-permute-start(bf16[576,768]{1,0:T(8,128)(2,1)} %get-tuple-element.280.refs_12_), channel_id=1, source_target_pairs={{0,8},{4,12},{8,0},{12,4},{1,9},{5,13},{9,1},{13,5},{2,10},{6,14},... | collective-permute-start | bytes 2654216 | tf_op jit(solution)/shard_map/ppermute | solution.py:102
  305.7 19.8 %collective-permute-start.41 = (bf16[128,1664]{1,0:T(8,128)(2,1)}, bf16[128,1664]{1,0:T(8,128)(2,1)S(1)}, u32[]{:S(2)}, u32[]{:S(2)}) collective-permute-start(bf16[128,1664]{1,0:T(8,128)(2,1)} %get-tuple-element.278), channel_id=1, source_target_pairs={{0,2},{1,3},{2,0},{3,1},{4,6},{5,7},{6,4},{7,5},{8,10},{9,11},{10,... | collective-permute-start | bytes 1277960 | tf_op jit(solution)/shard_map/ppermute | solution.py:205
  342.7 25.3 %collective-permute-start.46 = (bf16[256,1536]{1,0:T(8,128)(2,1)}, bf16[256,1536]{1,0:T(8,128)(2,1)}, u32[]{:S(2)}, u32[]{:S(2)}) collective-permute-start(bf16[256,1536]{1,0:T(8,128)(2,1)} %get-tuple-element.411), channel_id=1, source_target_pairs={{0,1},{1,0},{2,3},{3,2},{4,5},{5,4},{6,7},{7,6},{8,9},{9,8},{10,11... | collective-permute-start | bytes 2359304 | tf_op jit(solution)/shard_map/ppermute | solution.py:205
  342.7 57.1 %collective-permute-start.66 = (bf16[576,768]{1,0:T(8,128)(2,1)}, bf16[576,768]{1,0:T(8,128)(2,1)S(1)}, u32[]{:S(2)}, u32[]{:S(2)}) collective-permute-start(bf16[576,768]{1,0:T(8,128)(2,1)} %get-tuple-element.342), channel_id=1, source_target_pairs={{0,16},{16,0},{1,17},{17,1},{2,18},{18,2},{3,19},{19,3},{4,20},{20... | collective-permute-start | bytes 2654216 | tf_op jit(solution)/shard_map/ppermute | solution.py:102
  343.8 56.6 %collective-permute-start.67 = (bf16[576,768]{1,0:T(8,128)(2,1)}, bf16[576,768]{1,0:T(8,128)(2,1)}, u32[]{:S(2)}, u32[]{:S(2)}) collective-permute-start(bf16[576,768]{1,0:T(8,128)(2,1)} %get-tuple-element.344), channel_id=1, source_target_pairs={{0,8},{4,12},{8,0},{12,4},{1,9},{5,13},{9,1},{13,5},{2,10},{6,14},... | collective-permute-start | bytes 2654216 | tf_op jit(solution)/shard_map/ppermute | solution.py:102
  395.1 25.0 %collective-permute-start.53 = (bf16[2,384,640]{2,1,0:T(8,128)(2,1)}, bf16[2,384,640]{2,1,0:T(8,128)(2,1)}, u32[]{:S(2)}, u32[]{:S(2)}) collective-permute-start(bf16[2,384,640]{2,1,0:T(8,128)(2,1)} %get-tuple-element.322.refs_5_), channel_id=1, source_target_pairs={{0,16},{16,0},{1,17},{17,1},{2,18},{18,2},{3,19},{19,3},{4,20},{20... | collective-permute-start | bytes 2949128 | tf_op jit(solution)/shard_map/ppermute | solution.py:102
  396.2 31.4 %collective-permute-start.50 = (bf16[256,1536]{1,0:T(8,128)(2,1)}, bf16[256,1536]{1,0:T(8,128)(2,1)}, u32[]{:S(2)}, u32[]{:S(2)}) collective-permute-start(bf16[256,1536]{1,0:T(8,128)(2,1)} %after.60), channel_id=1, source_target_pairs={{0,1},{1,0},{2,3},{3,2},{4,5},{5,4},{6,7},{7,6},{8,9},{9,8},{10,11... | collective-permute-start | bytes 2359304 | tf_op jit(solution)/shard_map/ppermute | solution.py:205
  399.8 28.4 %collective-permute-start.49 = (bf16[192,1536]{1,0:T(8,128)(2,1)}, bf16[192,1536]{1,0:T(8,128)(2,1)}, u32[]{:S(2)}, u32[]{:S(2)}) collective-permute-start(bf16[192,1536]{1,0:T(8,128)(2,1)} %slice.222), channel_id=1, source_target_pairs={{0,2},{1,3},{2,0},{3,1},{4,6},{5,7},{6,4},{7,5},{8,10},{9,11},{10,... | collective-permute-start | bytes 1769480 | tf_op jit(solution)/shard_map/ppermute | solution.py:205
  428.3 25.3 %collective-permute-start.55 = (bf16[256,1536]{1,0:T(8,128)(2,1)}, bf16[256,1536]{1,0:T(8,128)(2,1)}, u32[]{:S(2)}, u32[]{:S(2)}) collective-permute-start(bf16[256,1536]{1,0:T(8,128)(2,1)} %after.64), channel_id=1, source_target_pairs={{0,4},{4,0},{8,12},{12,8},{1,5},{5,1},{9,13},{13,9},{2,6},{6,2},{1... | collective-permute-start | bytes 2359304 | tf_op jit(solution)/shard_map/ppermute | solution.py:107
  436.6 28.1 %collective-permute-start.68 = (bf16[576,768]{1,0:T(8,128)(2,1)}, bf16[576,768]{1,0:T(8,128)(2,1)}, u32[]{:S(2)}, u32[]{:S(2)}) collective-permute-start(bf16[576,768]{1,0:T(8,128)(2,1)} %get-tuple-element.351), channel_id=1, source_target_pairs={{0,8},{4,12},{8,0},{12,4},{1,9},{5,13},{9,1},{13,5},{2,10},{6,14},... | collective-permute-start | bytes 2654216 | tf_op jit(solution)/shard_map/ppermute | solution.py:102
  438.1 26.6 %collective-permute-start.69 = (bf16[576,768]{1,0:T(8,128)(2,1)}, bf16[576,768]{1,0:T(8,128)(2,1)}, u32[]{:S(2)}, u32[]{:S(2)}) collective-permute-start(bf16[576,768]{1,0:T(8,128)(2,1)} %get-tuple-element.352), channel_id=1, source_target_pairs={{0,16},{16,0},{1,17},{17,1},{2,18},{18,2},{3,19},{19,3},{4,20},{20... | collective-permute-start | bytes 2654216 | tf_op jit(solution)/shard_map/ppermute | solution.py:102
  (142 other events, 1060.0 us)
Sparse Core Ops, SparseCore 0:
  50.9 68.9 all-gather.2

commit v5 on v4

--- a/solution.py
+++ b/solution.py
@@ -994,6 +994,31 @@
     )(*arrays, gates, middle, gain, router, grad_out)
 
 
+def middle_forward(hidden, own, other, gain):
+    rows, width = hidden.shape
+
+    def kernel(hidden_ref, own_ref, other_ref, gain_ref, middle_ref, inner_ref):
+        middle = hidden_ref[...] + own_ref[...] + other_ref[...].astype(F32)
+        middle_ref[...] = middle
+        root = lax.rsqrt(jnp.mean(middle * middle, axis=-1, keepdims=True) + EPS)
+        inner_ref[...] = (middle * root * gain_ref[...]).astype(BF16)
+
+    block = pl.BlockSpec((rows, width), lambda j: (0, 0))
+    return pl.pallas_call(
+        kernel,
+        grid=(1,),
+        in_specs=[block, block, block, pl.BlockSpec((1, width), lambda j: (0, 0))],
+        out_specs=[block, block],
+        out_shape=[
+            jax.ShapeDtypeStruct((rows, width), F32),
+            jax.ShapeDtypeStruct((rows, width), BF16),
+        ],
+        compiler_params=kernel_params(),
+        cost_estimate=SMALL,
+        name="middle_forward",
+    )(hidden, own, other, gain)
+
+
 def expert_sums(core, halves, gu_shard, down_shard):
     block_rows, half = halves[0][0].shape
     counts = [len(blocks) for blocks in halves]
@@ -1245,8 +1270,9 @@
     (out_turned,) = place_blocks(
         out_halves, (out_first, out_second, out_third), ((0, block_rows, 0, own_query),)
     )
-    middle = hidden + core_sum(dot_turned(mixed, out_turned))
-    inner = norm_rows(middle, gain_two).astype(BF16)
+    branch = dot_turned(mixed, out_turned)
+    branch_other = core_swap(branch[rows:].astype(BF16))
+    middle, inner = middle_forward(hidden, branch, branch_other, gain_two[None, :])
     gate_up_all, down_all = place_blocks(
         expert_halves,
         (expert_first, expert_second, expert_third),

time: 500 us -> 496 us (level)
    unnamed x213 -> x251, local copies, waits for them, and re-layouts: 36.2 us -> 36.6 us
  transfers between devices with their start and end apart: 72 -> 72, of which waited for: 29 -> 30; matrix products, arithmetic and copies ran while one was open for 17% -> 16% of each run, Pallas kernels for 31% -> 32%
where the time goes in v5:
time: 496 us; the launch traced here: 490 us
  Pallas kernels  160 us (32%)
  waiting for transfers between devices  129 us (26%)
  other arithmetic  63.9 us (13%)
  starting transfers between devices  62.1 us (13%)
  local copies, waits for them, and re-layouts  55.5 us (11%)
  between operations  15.6 us (3%)
    ppermute x18, waiting for transfers between devices, xor_shift(): return lax.ppermute(value, 'exp', [(i, i ^ step) for i in range(n)])  61.8 us
    ppermute x34, waiting for transfers between devices, shifted(): lax.ppermute(value, name, [(i, (i + step * stride) % n) for i in range(n)])  57.3 us
    pallas_call x4, Pallas kernels, expert_step(): pl.pallas_call(kernel, in_specs=[pl.BlockSpec(memory_space=pltpu.SMEM), p...  49.6 us
    ppermute x34, starting transfers between devices, shifted(): lax.ppermute(value, name, [(i, (i + step * stride) % n) for i in range(n)])  37.2 us
    unnamed x251, local copies, waits for them, and re-layouts  36.6 us
    ppermute x18, starting transfers between devices, xor_shift(): return lax.ppermute(value, 'exp', [(i, i ^ step) for i in range(n)])  22.1 us
    pallas_call x1, Pallas kernels, gate_up_grads(): pl.pallas_call(kernel, grid=(width // tile,), in_specs=[pl.BlockSpec((n_r...  15 us
    pallas_call x1, Pallas kernels, attention_backward(): pl.pallas_call(kernel, grid=(heads,), in_specs=[by_head, by_head, fixed(l...  14.5 us
  transfers between devices with their start and end apart: 72, of which 30 were waited for; matrix products, arithmetic and copies ran while one was open for 16% of the time, Pallas kernels for 32%

profile of v5, /device:TPU:0, one launch (start us, length us, event | category | flops | bytes accessed | tf_op | source)
XLA Modules:
  0.0 490.4 jit_solution(6692017950508116150)
XLA Ops:
  29.0 13.0 %collective-permute-done.2 = bf16[96,1920]{1,0:T(8,128)(2,1)S(1)} collective-permute-done((bf16[96,1920]{1,0:T(8,128)(2,1)S(1)}, bf16[96,1920]{1,0:T(8,128)(2,1)S(1)}, u32[]{:S(2)}, u32[]{:S(2)}) %collective-permute-start.2) | collective-permute-done | bytes 368672 | tf_op jit(solution)/shard_map/ppermute | solution.py:205
  42.5 8.3 %collective-permute-done.3 = bf16[96,1920]{1,0:T(8,128)(2,1)S(1)} collective-permute-done((bf16[96,1920]{1,0:T(8,128)(2,1)S(1)}, bf16[96,1920]{1,0:T(8,128)(2,1)S(1)}, u32[]{:S(2)}, u32[]{:S(2)}) %collective-permute-start.3) | collective-permute-done | bytes 368672 | tf_op jit(solution)/shard_map/ppermute | solution.py:205
  62.7 16.2 %collective-permute-done.8.refs_1_ = bf16[384,512]{1,0:T(8,128)(2,1)S(1)} collective-permute-done((bf16[384,512]{1,0:T(8,128)(2,1)S(1)}, bf16[384,512]{1,0:T(8,128)(2,1)S(1)}, u32[]{:S(2)}, u32[]{:S(2)}) %collective-permute-start.8) | collective-permute-done | bytes 393248 | tf_op jit(solution)/shard_map/ppermute | solution.py:102
  85.6 6.6 %collective-permute-done.13.refs_7_ = bf16[384,512]{1,0:T(8,128)(2,1)S(1)} collective-permute-done((bf16[384,512]{1,0:T(8,128)(2,1)}, bf16[384,512]{1,0:T(8,128)(2,1)S(1)}, u32[]{:S(2)}, u32[]{:S(2)}) %collective-permute-start.13) | collective-permute-done | bytes 393248 | tf_op jit(solution)/shard_map/ppermute | solution.py:102
  97.0 2.8 place_blocks.3
  112.1 7.8 %collective-permute-done.16.refs_7_.refs_1_ = bf16[512,256]{1,0:T(8,128)(2,1)S(1)} collective-permute-done((bf16[512,256]{1,0:T(8,128)(2,1)S(1)}, bf16[512,256]{1,0:T(8,128)(2,1)S(1)}, u32[]{:S(2)}, u32[]{:S(2)}) %collective-permute-start.16) | collective-permute-done | bytes 262176 | tf_op jit(solution)/shard_map/ppermute | solution.py:102
  127.8 12.8 %attention_forward.1 = (bf16[512,768]{1,0:T(8,128)(2,1)}, bf16[512,768]{1,0:T(8,128)(2,1)}, f32[8,512]{1,0:T(8,128)}) custom-call(f32[512,1024]{1,0:T(8,128)} %get-tuple-element.199.projected_ref, f32[512,128]{1,0:T(8,128)} %get-tuple-element.431.cos_ref, f32[512,128]{1,0:T(8,128)} %get-tuple-element.406.sin_ref, s32[1024,1]{1,0:T(8,128)} %copy.187.place_ref, ...), custom_call_target="tpu_custom_call" | custom-call | flops 1 | bytes 1 | tf_op jit(solution)/shard_map/attention_forward/pallas_call | solution.py:442
  155.5 3.9 middle_forward.1
  163.3 10.1 %collective-permute-done.28.refs_3_ = bf16[576,768]{1,0:T(8,128)(2,1)} collective-permute-done((bf16[576,768]{1,0:T(8,128)(2,1)}, bf16[576,768]{1,0:T(8,128)(2,1)}, u32[]{:S(2)}, u32[]{:S(2)}) %collective-permute-start.28) | collective-permute-done | bytes 884768 | tf_op jit(solution)/shard_map/ppermute | solution.py:102
  175.8 5.7 %place_blocks.5 = (bf16[1536,1536]{1,0:T(8,128)(2,1)}, bf16[768,1536]{1,0:T(8,128)(2,1)}) custom-call(s32[2]{0:T(128)S(1)} %pad_add_fusion.3.place_ref, bf16[576,768]{1,0:T(8,128)(2,1)S(1)} %copy-done.12, bf16[576,768]{1,0:T(8,128)(2,1)S(1)} %copy-done.21, bf16[576,768]{1,0:T(8,128)(2,1)S(1)} %copy-done.7, bf16[576,768]{1,0:T(8,128)(2,1)} %collective-permute-done.28.refs_3_, ...), custom_call_target="tpu_custom_call" | custom-call | flops 1 | bytes 1 | tf_op jit(solution)/shard_map/place_blocks/pallas_call | solution.py:182
  181.5 12.2 %expert_step.4 = (bf16[256,1664]{1,0:T(8,128)(2,1)}, bf16[256,1664]{1,0:T(8,128)(2,1)}, bf16[2048,1536]{1,0:T(8,128)(2,1)}, bf16[2048,1536]{1,0:T(8,128)(2,1)}, ...) custom-call(s32[2]{0:T(128)} %pad_add_fusion.5.scalar_ref, ...), custom_call_target="tpu_custom_call" | custom-call | flops 1 | bytes 1 | tf_op jit(solution)/shard_map/expert_step/pallas_call | solution.py:639
  202.5 12.7 %expert_step.5 = (bf16[256,1664]{1,0:T(8,128)(2,1)}, bf16[256,1664]{1,0:T(8,128)(2,1)}, bf16[2048,1536]{1,0:T(8,128)(2,1)}, bf16[2048,1536]{1,0:T(8,128)(2,1)}, ...) custom-call(s32[2]{0:T(128)} %pad_add_fusion.6.scalar_ref, ...), custom_call_target="tpu_custom_call", output_to_operand_aliasing={{2}: (8, {}), {3}: (9, {}), {4}: (10, {}), {5}: (11, {}), {... | custom-call | flops 1 | bytes 1 | tf_op jit(solution)/shard_map/expert_step/pallas_call | solution.py:639
  215.2 2.9 collective-permute-done.33.refs_1_
  225.4 12.3 %expert_step.6 = (bf16[256,1664]{1,0:T(8,128)(2,1)}, bf16[256,1664]{1,0:T(8,128)(2,1)}, bf16[2048,1536]{1,0:T(8,128)(2,1)}, bf16[2048,1536]{1,0:T(8,128)(2,1)}, ...) custom-call(s32[2]{0:T(128)} %pad_add_fusion.7.scalar_ref, ...), custom_call_target="tpu_custom_call", output_to_operand_aliasing={{2}: (8, {}), {3}: (9, {}), {4}: (10, {}), {5}: (11, {}), {... | custom-call | flops 1 | bytes 1 | tf_op jit(solution)/shard_map/expert_step/pallas_call | solution.py:639
  239.2 12.4 %expert_step.7 = (bf16[256,1664]{1,0:T(8,128)(2,1)}, bf16[256,1664]{1,0:T(8,128)(2,1)}, bf16[2048,1536]{1,0:T(8,128)(2,1)}, bf16[2048,1536]{1,0:T(8,128)(2,1)}, ...) custom-call(s32[2]{0:T(128)} %pad_add_fusion.4.scalar_ref, ...), custom_call_target="tpu_custom_call", output_to_operand_aliasing={{2}: (8, {}), {3}: (9, {}), {4}: (10, {}), {5}: (11, {}), {... | custom-call | flops 1 | bytes 1 | tf_op jit(solution)/shard_map/expert_step/pallas_call | solution.py:639
  260.3 15.0 %gate_up_grads.1 = (bf16[1536,768]{1,0:T(8,128)(2,1)}, bf16[1536,768]{1,0:T(8,128)(2,1)}) custom-call(bf16[2048,1536]{1,0:T(8,128)(2,1)} %get-tuple-element.255.rows_ref, bf16[2048,768]{1,0:T(8,128)(2,1)} %get-tuple-element.256.gate_ref, bf16[2048,768]{1,0:T(8,128)(2,1)} %get-tuple-element.257.up_ref), custom_call_target="tpu_custom_call" | custom-call | flops 1 | bytes 1 | tf_op jit(solution)/shard_map/gate_up_grads/pallas_call | solution.py:679
  275.2 3.0 collective-permute-done.39.refs_2_
  287.5 13.7 %expert_weight_grads.1 = (bf16[576,768]{1,0:T(8,128)(2,1)}, bf16[576,768]{1,0:T(8,128)(2,1)}, bf16[576,768]{1,0:T(8,128)(2,1)}, bf16[576,768]{1,0:T(8,128)(2,1)}...) custom-call(s32[2]{0:T(128)} %copy-done.56, ...), custom_call_target="tpu_custom_call" | custom-call | flops 1 | bytes 1 | tf_op jit(solution)/shard_map/expert_weight_grads/pallas_call | solution.py:734
  301.1 5.1 %collective-permute-done.40.refs_9_ = bf16[128,1664]{1,0:T(8,128)(2,1)S(1)} collective-permute-done((bf16[128,1664]{1,0:T(8,128)(2,1)S(1)}, bf16[128,1664]{1,0:T(8,128)(2,1)S(1)}, u32[]{:S(2)}, u32[]{:S(2)}) %collective-permute-start.40) | collective-permute-done | bytes 426016 | tf_op jit(solution)/shard_map/ppermute | solution.py:205
  310.8 8.5 %expert_results.1 = (bf16[1024,1536]{1,0:T(8,128)(2,1)}, bf16[1024,1536]{1,0:T(8,128)(2,1)}) custom-call(bf16[2048,768]{1,0:T(8,128)(2,1)} %get-tuple-element.279.gated_ref, bf16[768,1536]{1,0:T(8,128)(2,1)} %get-tuple-element.214.refs_5_.down_ref), custom_call_target="tpu_custom_call" | custom-call | flops 1 | bytes 1 | tf_op jit(solution)/shard_map/expert_results/pallas_call | solution.py:765
  319.3 8.6 %collective-permute-done.41.refs_2_ = bf16[128,1664]{1,0:T(8,128)(2,1)S(1)} collective-permute-done((bf16[128,1664]{1,0:T(8,128)(2,1)}, bf16[128,1664]{1,0:T(8,128)(2,1)S(1)}, u32[]{:S(2)}, u32[]{:S(2)}) %collective-permute-start.41) | collective-permute-done | bytes 426016 | tf_op jit(solution)/shard_map/ppermute | solution.py:205
  331.8 4.5 middle_backward.1
  345.7 7.7 %branch_backward.1 = (bf16[512,768]{1,0:T(8,128)(2,1)}, bf16[2,384,384]{2,1,0:T(8,128)(2,1)}, bf16[2,384,384]{2,1,0:T(8,128)(2,1)}, bf16[2,384,384]{2,1,0:T(8,128)(2,1)}, bf16[2,384,384]{2,1,0:T(8,128)(2,1)}) custom-call(s32[2]{0:T(128)} %copy-done.56, bf16[256,1536]{1,0:T(8,128)(2,1)} %copy-done.54, bf16[256,1536]{1,0:T(8,128)(2,1)} %copy-done.103, ...), custom_call_target="tpu_custom_call" | custom-call | flops 1 | bytes 1 | tf_op jit(solution)/shard_map/branch_backward/pallas_call | solution.py:825
  353.4 14.5 %attention_backward.1 = (bf16[512,768]{1,0:T(8,128)(2,1)}, f32[512,256]{1,0:T(8,128)}, bf16[512,256]{1,0:T(8,128)(2,1)}) custom-call(bf16[512,768]{1,0:T(8,128)(2,1)} %get-tuple-element.294.query_ref, bf16[512,768]{1,0:T(8,128)(2,1)} %after.56.grad_ref, f32[8,512]{1,0:T(8,128)} %get-tuple-element.299.lse_ref, f32[512,128]{1,0:T(8,128)} %get-tuple-element.431.cos_ref, ...), custom_call_target="tpu_custom_call" | custom-call | flops 1 | bytes 1 | tf_op jit(solution)/shard_map/attention_backward/pallas_call | solution.py:518
  379.7 11.1 %projection_backward.1 = (f32[256,1536]{1,0:T(8,128)}, bf16[256,1536]{1,0:T(8,128)(2,1)}, bf16[2,384,640]{2,1,0:T(8,128)(2,1)}, bf16[2,384,640]{2,1,0:T(8,128)(2...) custom-call(s32[2]{0:T(128)} %copy-done.56, bf16[512,1536]{1,0:T(8,128)(2,1)} %copy-done.72, ...), custom_call_target="tpu_custom_call" | custom-call | flops 1 | bytes 1 | tf_op jit(solution)/shard_map/projection_backward/pallas_call | solution.py:903
  403.5 7.5 %collective-permute-done.54 = bf16[2,384,512]{2,1,0:T(8,128)(2,1)} collective-permute-done((bf16[2,384,512]{2,1,0:T(8,128)(2,1)}, bf16[2,384,512]{2,1,0:T(8,128)(2,1)}, u32[]{:S(2)}, u32[]{:S(2)}) %collective-permute-start.54) | collective-permute-done | bytes 786464 | tf_op jit(solution)/shard_map/ppermute | solution.py:102
  422.1 2.9 collective-permute-done.50.refs_2_
  426.0 3.6 add_bitcast_fusion.1
  445.1 10.2 %collective-permute-done.63 = bf16[2,2,48,768]{3,2,1,0:T(8,128)(2,1)S(1)} collective-permute-done((bf16[2,2,48,768]{3,2,1,0:T(8,128)(2,1)S(1)}, bf16[2,2,48,768]{3,2,1,0:T(8,128)(2,1)S(1)}, u32[]{:S(2)}, u32[]{:S(2)}) %collective-permute-start.63) | collective-permute-done | bytes 294944 | tf_op jit(solution)/shard_map/ppermute | solution.py:205
  456.2 2.8 add_bitcast_fusion
  462.9 3.6 collective-permute-done.64
  468.6 4.3 expert_sums.1
  (530 shorter events, 208.6 us)
Async XLA Ops:
  7.2 114.5 %all-gather.3.cloned.1.call-start = ((), (), s32[]{:S(2)}) async-start(), calls=%async_computation | async-start | bytes 4259840 | tf_op jit(solution)/shard_map/all_gather | solution.py:1209
  19.8 22.6 %collective-permute-start.1 = (bf16[96,1920]{1,0:T(8,128)(2,1)S(1)}, bf16[96,1920]{1,0:T(8,128)(2,1)S(1)}, u32[]{:S(2)}, u32[]{:S(2)}) collective-permute-start(bf16[96,1920]{1,0:T(8,128)(2,1)S(1)} %bitcast.182), channel_id=1, source_target_pairs={{0,1},{1,0},{2,3},{3,2},{4,5},{5,4},{6,7},{7,6},{8,9},{9,8},{10,11... | collective-permute-start | bytes 1105928 | tf_op jit(solution)/shard_map/ppermute | solution.py:205
  25.6 25.3 %collective-permute-start.5 = (bf16[576,768]{1,0:T(8,128)(2,1)S(1)}, bf16[576,768]{1,0:T(8,128)(2,1)S(1)}, u32[]{:S(2)}, u32[]{:S(2)}) collective-permute-start(bf16[576,768]{1,0:T(8,128)(2,1)S(1)} %pad_maximum_fusion.1.refs_2_), channel_id=1, source_target_pairs={{0,16},{16,0},{1,17},{17,1},{2,18},{18,2},{3,19},{19,3},{4,20},{20... | collective-permute-start | bytes 2654216 | tf_op jit(solution)/shard_map/ppermute | solution.py:102
  27.2 23.7 %collective-permute-start.6 = (bf16[576,768]{1,0:T(8,128)(2,1)S(1)}, bf16[576,768]{1,0:T(8,128)(2,1)S(1)}, u32[]{:S(2)}, u32[]{:S(2)}) collective-permute-start(bf16[576,768]{1,0:T(8,128)(2,1)S(1)} %pad_maximum_fusion.2.refs_3_), channel_id=1, source_target_pairs={{0,8},{4,12},{8,0},{12,4},{1,9},{5,13},{9,1},{13,5},{2,10},{6,14},... | collective-permute-start | bytes 2654216 | tf_op jit(solution)/shard_map/ppermute | solution.py:102
  55.5 23.4 %collective-permute-start.11 = (bf16[256,1536]{1,0:T(8,128)(2,1)}, bf16[256,1536]{1,0:T(8,128)(2,1)}, u32[]{:S(2)}, u32[]{:S(2)}) collective-permute-start(bf16[256,1536]{1,0:T(8,128)(2,1)} %unit_rows.1.unit_ref), channel_id=1, source_target_pairs={{0,4},{4,0},{8,12},{12,8},{1,5},{5,1},{9,13},{13,9},{2,6},{6,2},{1... | collective-permute-start | bytes 2359304 | tf_op jit(solution)/shard_map/ppermute | solution.py:107
  55.6 23.3 %collective-permute-start.7 = (bf16[384,640]{1,0:T(8,128)(2,1)S(1)}, bf16[384,640]{1,0:T(8,128)(2,1)S(1)}, u32[]{:S(2)}, u32[]{:S(2)}) collective-permute-start(bf16[384,640]{1,0:T(8,128)(2,1)S(1)} %slice.250.refs_0_), channel_id=1, source_target_pairs={{0,16},{16,0},{1,17},{17,1},{2,18},{18,2},{3,19},{19,3},{4,20},{20... | collective-permute-start | bytes 1474568 | tf_op jit(solution)/shard_map/ppermute | solution.py:102
  57.2 21.8 %collective-permute-start.9 = (bf16[384,640]{1,0:T(8,128)(2,1)S(1)}, bf16[384,640]{1,0:T(8,128)(2,1)S(1)}, u32[]{:S(2)}, u32[]{:S(2)}) collective-permute-start(bf16[384,640]{1,0:T(8,128)(2,1)S(1)} %slice.250.refs_0_), channel_id=1, source_target_pairs={{0,8},{4,12},{8,0},{12,4},{1,9},{5,13},{9,1},{13,5},{2,10},{6,14},... | collective-permute-start | bytes 1474568 | tf_op jit(solution)/shard_map/ppermute | solution.py:102
  58.7 20.2 %collective-permute-start.8 = (bf16[384,512]{1,0:T(8,128)(2,1)S(1)}, bf16[384,512]{1,0:T(8,128)(2,1)S(1)}, u32[]{:S(2)}, u32[]{:S(2)}) collective-permute-start(bf16[384,512]{1,0:T(8,128)(2,1)S(1)} %slice.251.refs_4_), channel_id=1, source_target_pairs={{0,8},{4,12},{8,0},{12,4},{1,9},{5,13},{9,1},{13,5},{2,10},{6,14},... | collective-permute-start | bytes 1179656 | tf_op jit(solution)/shard_map/ppermute | solution.py:102
  121.8 21.5 %collective-permute-start.21 = (bf16[4,256,1664]{2,1,0:T(8,128)(2,1)}, bf16[4,256,1664]{2,1,0:T(8,128)(2,1)}, u32[]{:S(2)}, u32[]{:S(2)}) collective-permute-start(bf16[4,256,1664]{2,1,0:T(8,128)(2,1)} %get-tuple-element.203.refs_2_), channel_id=1, source_target_pairs={{0,4},{4,0},{8,12},{12,8},{1,5},{5,1},{9,13},{13,9},{2,6},{6,2},{1... | collective-permute-start | bytes 10223624 | tf_op jit(solution)/shard_map/ppermute | solution.py:107
  126.7 24.3 %collective-permute-start.26 = (bf16[576,768]{1,0:T(8,128)(2,1)}, bf16[576,768]{1,0:T(8,128)(2,1)S(1)}, u32[]{:S(2)}, u32[]{:S(2)}) collective-permute-start(bf16[576,768]{1,0:T(8,128)(2,1)} %get-tuple-element.207.refs_0_), channel_id=1, source_target_pairs={{0,8},{4,12},{8,0},{12,4},{1,9},{5,13},{9,1},{13,5},{2,10},{6,14},... | collective-permute-start | bytes 2654216 | tf_op jit(solution)/shard_map/ppermute | solution.py:102
  127.2 24.6 %collective-permute-start.27 = (bf16[576,768]{1,0:T(8,128)(2,1)}, bf16[576,768]{1,0:T(8,128)(2,1)}, u32[]{:S(2)}, u32[]{:S(2)}) collective-permute-start(bf16[576,768]{1,0:T(8,128)(2,1)} %get-tuple-element.210.refs_4_), channel_id=1, source_target_pairs={{0,16},{16,0},{1,17},{17,1},{2,18},{18,2},{3,19},{19,3},{4,20},{20... | collective-permute-start | bytes 2654216 | tf_op jit(solution)/shard_map/ppermute | solution.py:102
  151.9 21.5 %collective-permute-start.28 = (bf16[576,768]{1,0:T(8,128)(2,1)}, bf16[576,768]{1,0:T(8,128)(2,1)}, u32[]{:S(2)}, u32[]{:S(2)}) collective-permute-start(bf16[576,768]{1,0:T(8,128)(2,1)} %get-tuple-element.211), channel_id=1, source_target_pairs={{0,8},{4,12},{8,0},{12,4},{1,9},{5,13},{9,1},{13,5},{2,10},{6,14},... | collective-permute-start | bytes 2654216 | tf_op jit(solution)/shard_map/ppermute | solution.py:102
  153.4 21.2 %collective-permute-start.29 = (bf16[576,768]{1,0:T(8,128)(2,1)}, bf16[576,768]{1,0:T(8,128)(2,1)}, u32[]{:S(2)}, u32[]{:S(2)}) collective-permute-start(bf16[576,768]{1,0:T(8,128)(2,1)} %get-tuple-element.212), channel_id=1, source_target_pairs={{0,16},{16,0},{1,17},{17,1},{2,18},{18,2},{3,19},{19,3},{4,20},{20... | collective-permute-start | bytes 2654216 | tf_op jit(solution)/shard_map/ppermute | solution.py:102
  159.4 22.1 %collective-permute-start.25 = (bf16[256,1536]{1,0:T(8,128)(2,1)}, bf16[256,1536]{1,0:T(8,128)(2,1)}, u32[]{:S(2)}, u32[]{:S(2)}) collective-permute-start(bf16[256,1536]{1,0:T(8,128)(2,1)} %get-tuple-element.206.refs_0_.refs_1_), channel_id=1, source_target_pairs={{0,4},{4,0},{8,12},{12,8},{1,5},{5,1},{9,13},{13,9},{2,6},{6,2},{1... | collective-permute-start | bytes 2359304 | tf_op jit(solution)/shard_map/ppermute | solution.py:107
  159.4 36.8 %collective-permute-start.23 = (bf16[256,1536]{1,0:T(8,128)(2,1)}, bf16[256,1536]{1,0:T(8,128)(2,1)}, u32[]{:S(2)}, u32[]{:S(2)}) collective-permute-start(bf16[256,1536]{1,0:T(8,128)(2,1)} %get-tuple-element.206.refs_0_.refs_1_), channel_id=1, source_target_pairs={{0,1},{1,0},{2,3},{3,2},{4,5},{5,4},{6,7},{7,6},{8,9},{9,8},{10,11... | collective-permute-start | bytes 2359304 | tf_op jit(solution)/shard_map/ppermute | solution.py:205
  160.2 37.8 %collective-permute-start.24 = (bf16[256,1536]{1,0:T(8,128)(2,1)}, bf16[256,1536]{1,0:T(8,128)(2,1)}, u32[]{:S(2)}, u32[]{:S(2)}) collective-permute-start(bf16[256,1536]{1,0:T(8,128)(2,1)} %get-tuple-element.206.refs_0_.refs_1_), channel_id=1, source_target_pairs={{0,2},{1,3},{2,0},{3,1},{4,6},{5,7},{6,4},{7,5},{8,10},{9,11},{10,... | collective-permute-start | bytes 2359304 | tf_op jit(solution)/shard_map/ppermute | solution.py:205
  193.7 24.4 %collective-permute-start.32 = (bf16[256,1664]{1,0:T(8,128)(2,1)}, bf16[256,1664]{1,0:T(8,128)(2,1)S(1)}, u32[]{:S(2)}, u32[]{:S(2)}) collective-permute-start(bf16[256,1664]{1,0:T(8,128)(2,1)} %get-tuple-element.215.refs_2_), channel_id=1, source_target_pairs={{0,4},{4,0},{8,12},{12,8},{1,5},{5,1},{9,13},{13,9},{2,6},{6,2},{1... | collective-permute-start | bytes 2555912 | tf_op jit(solution)/shard_map/ppermute | solution.py:107
  225.2 26.5 %collective-permute-start.37 = (bf16[256,1664]{1,0:T(8,128)(2,1)S(1)}, bf16[256,1664]{1,0:T(8,128)(2,1)S(1)}, u32[]{:S(2)}, u32[]{:S(2)}) collective-permute-start(bf16[256,1664]{1,0:T(8,128)(2,1)S(1)} %copy-done.81), channel_id=1, source_target_pairs={{0,1},{1,0},{2,3},{3,2},{4,5},{5,4},{6,7},{7,6},{8,9},{9,8},{10,11... | collective-permute-start | bytes 2555912 | tf_op jit(solution)/shard_map/ppermute | solution.py:205
  257.0 21.3 %collective-permute-start.39 = (bf16[256,1664]{1,0:T(8,128)(2,1)S(1)}, bf16[256,1664]{1,0:T(8,128)(2,1)S(1)}, u32[]{:S(2)}, u32[]{:S(2)}) collective-permute-start(bf16[256,1664]{1,0:T(8,128)(2,1)S(1)} %add_convert_fusion.7.refs_5_.refs_2_), channel_id=1, source_target_pairs={{0,1},{1,0},{2,3},{3,2},{4,5},{5,4},{6,7},{7,6},{8,9},{9,8},{10,11... | collective-permute-start | bytes 2555912 | tf_op jit(solution)/shard_map/ppermute | solution.py:205
  284.9 21.3 %collective-permute-start.40 = (bf16[128,1664]{1,0:T(8,128)(2,1)S(1)}, bf16[128,1664]{1,0:T(8,128)(2,1)S(1)}, u32[]{:S(2)}, u32[]{:S(2)}) collective-permute-start(bf16[128,1664]{1,0:T(8,128)(2,1)S(1)} %get-tuple-element.422.refs_10_), channel_id=1, source_target_pairs={{0,2},{1,3},{2,0},{3,1},{4,6},{5,7},{6,4},{7,5},{8,10},{9,11},{10,... | collective-permute-start | bytes 1277960 | tf_op jit(solution)/shard_map/ppermute | solution.py:205
  307.0 20.9 %collective-permute-start.42 = (bf16[576,768]{1,0:T(8,128)(2,1)}, bf16[576,768]{1,0:T(8,128)(2,1)S(1)}, u32[]{:S(2)}, u32[]{:S(2)}) collective-permute-start(bf16[576,768]{1,0:T(8,128)(2,1)} %get-tuple-element.283.refs_8_), channel_id=1, source_target_pairs={{0,16},{16,0},{1,17},{17,1},{2,18},{18,2},{3,19},{19,3},{4,20},{20... | collective-permute-start | bytes 2654216 | tf_op jit(solution)/shard_map/ppermute | solution.py:102
  307.7 20.3 %collective-permute-start.43 = (bf16[576,768]{1,0:T(8,128)(2,1)}, bf16[576,768]{1,0:T(8,128)(2,1)S(1)}, u32[]{:S(2)}, u32[]{:S(2)}) collective-permute-start(bf16[576,768]{1,0:T(8,128)(2,1)} %get-tuple-element.284.refs_12_), channel_id=1, source_target_pairs={{0,8},{4,12},{8,0},{12,4},{1,9},{5,13},{9,1},{13,5},{2,10},{6,14},... | collective-permute-start | bytes 2654216 | tf_op jit(solution)/shard_map/ppermute | solution.py:102
  339.6 28.2 %collective-permute-start.46 = (bf16[256,1536]{1,0:T(8,128)(2,1)}, bf16[256,1536]{1,0:T(8,128)(2,1)}, u32[]{:S(2)}, u32[]{:S(2)}) collective-permute-start(bf16[256,1536]{1,0:T(8,128)(2,1)} %get-tuple-element.412), channel_id=1, source_target_pairs={{0,1},{1,0},{2,3},{3,2},{4,5},{5,4},{6,7},{7,6},{8,9},{9,8},{10,11... | collective-permute-start | bytes 2359304 | tf_op jit(solution)/shard_map/ppermute | solution.py:205
  341.1 56.0 %collective-permute-start.66 = (bf16[576,768]{1,0:T(8,128)(2,1)}, bf16[576,768]{1,0:T(8,128)(2,1)S(1)}, u32[]{:S(2)}, u32[]{:S(2)}) collective-permute-start(bf16[576,768]{1,0:T(8,128)(2,1)} %get-tuple-element.346), channel_id=1, source_target_pairs={{0,16},{16,0},{1,17},{17,1},{2,18},{18,2},{3,19},{19,3},{4,20},{20... | collective-permute-start | bytes 2654216 | tf_op jit(solution)/shard_map/ppermute | solution.py:102
  342.6 56.1 %collective-permute-start.67 = (bf16[576,768]{1,0:T(8,128)(2,1)}, bf16[576,768]{1,0:T(8,128)(2,1)S(1)}, u32[]{:S(2)}, u32[]{:S(2)}) collective-permute-start(bf16[576,768]{1,0:T(8,128)(2,1)} %get-tuple-element.348), channel_id=1, source_target_pairs={{0,8},{4,12},{8,0},{12,4},{1,9},{5,13},{9,1},{13,5},{2,10},{6,14},... | collective-permute-start | bytes 2654216 | tf_op jit(solution)/shard_map/ppermute | solution.py:102
  391.5 23.4 %collective-permute-start.53 = (bf16[2,384,640]{2,1,0:T(8,128)(2,1)}, bf16[2,384,640]{2,1,0:T(8,128)(2,1)}, u32[]{:S(2)}, u32[]{:S(2)}) collective-permute-start(bf16[2,384,640]{2,1,0:T(8,128)(2,1)} %get-tuple-element.326.refs_5_), channel_id=1, source_target_pairs={{0,16},{16,0},{1,17},{17,1},{2,18},{18,2},{3,19},{19,3},{4,20},{20... | collective-permute-start | bytes 2949128 | tf_op jit(solution)/shard_map/ppermute | solution.py:102
  394.6 30.4 %collective-permute-start.50 = (bf16[256,1536]{1,0:T(8,128)(2,1)}, bf16[256,1536]{1,0:T(8,128)(2,1)}, u32[]{:S(2)}, u32[]{:S(2)}) collective-permute-start(bf16[256,1536]{1,0:T(8,128)(2,1)} %after.60), channel_id=1, source_target_pairs={{0,1},{1,0},{2,3},{3,2},{4,5},{5,4},{6,7},{7,6},{8,9},{9,8},{10,11... | collective-permute-start | bytes 2359304 | tf_op jit(solution)/shard_map/ppermute | solution.py:205
  397.0 28.4 %collective-permute-start.49 = (bf16[192,1536]{1,0:T(8,128)(2,1)}, bf16[192,1536]{1,0:T(8,128)(2,1)}, u32[]{:S(2)}, u32[]{:S(2)}) collective-permute-start(bf16[192,1536]{1,0:T(8,128)(2,1)} %slice.218), channel_id=1, source_target_pairs={{0,2},{1,3},{2,0},{3,1},{4,6},{5,7},{6,4},{7,5},{8,10},{9,11},{10,... | collective-permute-start | bytes 1769480 | tf_op jit(solution)/shard_map/ppermute | solution.py:205
  418.4 25.0 %collective-permute-start.55 = (bf16[256,1536]{1,0:T(8,128)(2,1)}, bf16[256,1536]{1,0:T(8,128)(2,1)}, u32[]{:S(2)}, u32[]{:S(2)}) collective-permute-start(bf16[256,1536]{1,0:T(8,128)(2,1)} %after.64), channel_id=1, source_target_pairs={{0,4},{4,0},{8,12},{12,8},{1,5},{5,1},{9,13},{13,9},{2,6},{6,2},{1... | collective-permute-start | bytes 2359304 | tf_op jit(solution)/shard_map/ppermute | solution.py:107
  433.4 35.2 %collective-permute-start.68 = (bf16[576,768]{1,0:T(8,128)(2,1)}, bf16[576,768]{1,0:T(8,128)(2,1)}, u32[]{:S(2)}, u32[]{:S(2)}) collective-permute-start(bf16[576,768]{1,0:T(8,128)(2,1)} %get-tuple-element.355), channel_id=1, source_target_pairs={{0,8},{4,12},{8,0},{12,4},{1,9},{5,13},{9,1},{13,5},{2,10},{6,14},... | collective-permute-start | bytes 2654216 | tf_op jit(solution)/shard_map/ppermute | solution.py:102
  434.9 33.7 %collective-permute-start.69 = (bf16[576,768]{1,0:T(8,128)(2,1)}, bf16[576,768]{1,0:T(8,128)(2,1)}, u32[]{:S(2)}, u32[]{:S(2)}) collective-permute-start(bf16[576,768]{1,0:T(8,128)(2,1)} %get-tuple-element.356), channel_id=1, source_target_pairs={{0,16},{16,0},{1,17},{17,1},{2,18},{18,2},{3,19},{19,3},{4,20},{20... | collective-permute-start | bytes 2654216 | tf_op jit(solution)/shard_map/ppermute | solution.py:102
  438.6 20.4 %collective-permute-start.58 = (bf16[2,2,48,1152]{3,2,1,0:T(8,128)(2,1)}, bf16[2,2,48,1152]{3,2,1,0:T(8,128)(2,1)}, u32[]{:S(2)}, u32[]{:S(2)}) collective-permute-start(bf16[2,2,48,1152]{3,2,1,0:T(8,128)(2,1)} %pad_maximum_fusion.4), channel_id=1, source_target_pairs={{0,1},{1,0},{2,3},{3,2},{4,5},{5,4},{6,7},{7,6},{8,9},{9,8},{10,11... | collective-permute-start | bytes 1327112 | tf_op jit(solution)/shard_map/ppermute | solution.py:205
  (161 other events, 1101.2 us)
Sparse Core Ops, SparseCore 0:
  52.7 68.9 all-gather.2
